TPU v7x, 32 devices: a whole 2x2x4 slice. The times are simulated.
32 devices in a mesh: ctx: 8 (over z, x), head: 4 (over y, core).
Axes of the slice: x: 2, y: 2, z: 4, core: 2. Of those that a mesh axis runs over, the one named last changes fastest.
Arguments:
- input_x_channels: bfloat16 [8192, 8192], P('ctx', 'head'), may hold values from -4 to 4
- input_b_channels: bfloat16 [8192, 1024], P('ctx', 'head'), may hold values from -3 to 3
- input_c_channels: bfloat16 [8192, 1024], P('ctx', 'head'), may hold values from -3 to 3
- input_gate_channels: bfloat16 [8192, 8192], P('ctx', 'head'), may hold values from -75 to 75
- raw_step_sizes: float32 [128, 8192], P('head', 'ctx'), may hold values from -7 to 800
- log_decay_rate: float32 [128], P('head'), may hold values from -8 to -2.3
- head_skip_coeff: float32 [128], P('head'), may hold values from 0.5 to 2
- x_conv_taps: bfloat16 [4, 8192], P(None, 'head'), may hold values from -3 to 3
- b_conv_taps: bfloat16 [4, 1024], P(None, 'head'), may hold values from -3 to 3
- c_conv_taps: bfloat16 [4, 1024], P(None, 'head'), may hold values from -3 to 3
- gated_norm_gain: bfloat16 [8192], P('head'), may hold values from 0.099609375 to 1.8984375
- output_weight: bfloat16 [8192, 4096], P('head'), may hold values from -0.0625 to 0.0625
- adapter_down_panels: bfloat16 [48, 8192, 64], P('ctx', 'head'), may hold values from -0.0625 to 0.0625
- adapter_up_panels: bfloat16 [48, 64, 4096], P('ctx', None, 'head'), may hold values from -0.75 to 0.75
- turn_first_token: int32 [16], replicated, may hold values from 0 to 8064, as said below
- tenant_of_turn: int32 [16], replicated, may hold values from 0 to 47
- tenant_panel_index: int32 [48], replicated, may hold values from 0 to 47, each once
Outputs:
- out: bfloat16 [8192, 4096], P('ctx', 'head')
Inputs may be any that keep to these rules, and one draw needn't show every extreme that they name: `turn_first_token`: strictly increasing multiples of 128; the first is 0; every aligned block of 1024 tokens holds exactly 2 starts, and in every block but the first the earlier of them lies past the block's first token.
All inputs are finite; a program needn't handle non-finite values.
Results may differ from a plain program's by a relative error of at most 0.014.
Values may be sent and summed in bfloat16 or wider, within the bound.
No kernel may reach another device: no remote copies, remote signals or barrier semaphores. Data moves between devices by JAX's collectives and lax.ppermute only.
A program may use at most 192 MiB of HBM per device.

v0:
```python
import jax
import jax.numpy as jnp
from jax import lax
from jax.sharding import PartitionSpec as P

P_SIZE = 64
N = 128
K = 4
Q = 128
TURN_DEV = 2


highest = lax.Precision.HIGHEST
epsilon = 1e-05


def shifted(block, axis, distance):
    devices = range(lax.axis_size(axis))
    route = [(i - distance, i) for i in devices if i - distance in devices]
    return lax.ppermute(block, axis, route)


def conv_rows(sequence, tail_rows, weight):
    token_rows = sequence.shape[0]
    joined = jnp.concatenate([tail_rows, sequence], axis=0).astype(jnp.float32)
    total = jnp.zeros((token_rows, sequence.shape[1]), jnp.float32)
    for tap in range(weight.shape[0]):
        total = total + weight[tap].astype(jnp.float32) * joined[tap : tap + token_rows]
    return jax.nn.silu(total).astype(jnp.bfloat16)


def local(
    input_x_channels,
    input_b_channels,
    input_c_channels,
    input_gate_channels,
    raw_step_sizes,
    log_decay_rate,
    head_skip_coeff,
    x_conv_taps,
    b_conv_taps,
    c_conv_taps,
    gated_norm_gain,
    output_weight,
    adapter_down_panels,
    adapter_up_panels,
    turn_first_token,
    tenant_of_turn,
    tenant_panel_index,
):
    token_rows = input_x_channels.shape[0]
    head_count = log_decay_rate.shape[0]
    group_count = input_b_channels.shape[1] // N
    per_group = head_count // group_count
    conv_edge = K - 1
    conv_tails = shifted(
        (
            input_x_channels[token_rows - conv_edge :],
            input_b_channels[token_rows - conv_edge :],
            input_c_channels[token_rows - conv_edge :],
        ),
        "ctx",
        1,
    )
    x_conv = conv_rows(input_x_channels, conv_tails[0], x_conv_taps)
    b_conv = conv_rows(input_b_channels, conv_tails[1], b_conv_taps)
    c_conv = conv_rows(input_c_channels, conv_tails[2], c_conv_taps)
    block_count = token_rows // Q
    step_sizes = jax.nn.softplus(raw_step_sizes)
    decay_rate = jnp.exp(log_decay_rate)
    step_heads = step_sizes.reshape(head_count, block_count, Q)
    running = jnp.cumsum(-step_heads * decay_rate[:, None, None], axis=2)
    run_blocks = running.transpose(1, 0, 2).reshape(block_count, group_count, per_group, Q)
    step_blocks = step_heads.transpose(1, 0, 2).reshape(block_count, group_count, per_group, Q)
    x_blocks = x_conv.astype(jnp.float32).reshape(block_count, Q, group_count, per_group, P_SIZE)
    b_blocks = b_conv.astype(jnp.float32).reshape(block_count, Q, group_count, N)
    c_blocks = c_conv.astype(jnp.float32).reshape(block_count, Q, group_count, N)
    scores = jnp.einsum("cqgn,ckgn->cgqk", c_blocks, b_blocks, precision=highest)
    causal = jnp.arange(Q)[:, None] >= jnp.arange(Q)[None, :]
    log_gap = run_blocks[..., :, None] - run_blocks[..., None, :]
    decay_mat = jnp.where(causal, jnp.exp(jnp.where(causal, log_gap, 0.0)), 0.0)
    mixing = scores[:, :, None] * decay_mat * step_blocks[..., None, :]
    y_local = jnp.einsum("cghqk,ckghp->cqghp", mixing, x_blocks, precision=highest)
    tail_weight = jnp.exp(run_blocks[..., -1:] - run_blocks) * step_blocks
    block_states = jnp.einsum(
        "cghk,ckghp,ckgn->cghpn", tail_weight, x_blocks, b_blocks, precision=highest
    )
    block_log = run_blocks[..., -1]

    def carry_step(carried, inputs):
        fresh_state, step_log = inputs
        return (jnp.exp(step_log)[..., None, None] * carried + fresh_state, carried)

    empty_state = jnp.zeros((group_count, per_group, P_SIZE, N), jnp.float32)
    device_state, before = lax.scan(carry_step, empty_state, (block_states, block_log))
    device_log = jnp.sum(block_log, axis=0)
    run_tokens = run_blocks.transpose(0, 3, 1, 2)
    y_local = y_local + jnp.exp(run_tokens)[..., None] * jnp.einsum(
        "cqgn,cghpn->cqghp", c_blocks, before, precision=highest
    )
    all_logs, states = (
        lax.all_gather(device_log[None], "ctx", axis=0, tiled=True),
        lax.all_gather(device_state[None], "ctx", axis=0, tiled=True),
    )
    device_count = all_logs.shape[0]
    own_index = lax.axis_index("ctx")
    order_index = jnp.arange(device_count)
    between = (order_index[:, None] < order_index[None, :]) & (order_index[None, :] < own_index)
    span_log = jnp.einsum("jk,kgh->jgh", between.astype(jnp.float32), all_logs, precision=highest)
    weights = jnp.where((order_index < own_index)[:, None, None], jnp.exp(span_log), 0.0)
    incoming = jnp.einsum("jgh,jghpn->ghpn", weights, states, precision=highest)
    start_log = jnp.cumsum(block_log, axis=0) - block_log
    device_running = start_log[:, None] + run_tokens
    y_value = y_local + jnp.exp(device_running)[..., None] * jnp.einsum(
        "cqgn,ghpn->cqghp", c_blocks, incoming, precision=highest
    )
    y_value = y_value + head_skip_coeff.reshape(group_count, per_group)[:, :, None] * x_blocks
    group_width = per_group * P_SIZE
    gated = y_value.reshape(token_rows, group_count, group_width) * jax.nn.silu(
        input_gate_channels.astype(jnp.float32)
    ).reshape(token_rows, group_count, group_width)
    norm_scale = lax.rsqrt(jnp.mean(gated * gated, axis=2, keepdims=True) + epsilon)
    y_normed = (
        (gated * norm_scale).reshape(token_rows, -1) * gated_norm_gain.astype(jnp.float32)
    ).astype(jnp.bfloat16)
    own_index = lax.axis_index("ctx")
    slot_count = TURN_DEV + 1
    slot_turns = TURN_DEV * own_index - 1 + jnp.arange(slot_count)
    clipped = jnp.maximum(slot_turns, 0)
    tenants = jnp.take(tenant_of_turn, clipped)
    slot_homes = jnp.take(tenant_panel_index, tenants)
    all_down, all_up = (
        lax.all_gather(adapter_down_panels, "ctx", axis=0, tiled=True),
        lax.all_gather(adapter_up_panels, "ctx", axis=0, tiled=True),
    )
    down_slots = jnp.take(all_down, slot_homes, axis=0)
    up_slots = jnp.take(all_up, slot_homes, axis=0)
    base_out = lax.psum_scatter(
        jnp.dot(y_normed, output_weight, preferred_element_type=jnp.float32).astype(jnp.bfloat16),
        "head",
        scatter_dimension=1,
        tiled=True,
    ).astype(jnp.float32)
    own_starts = lax.dynamic_slice_in_dim(turn_first_token, TURN_DEV * own_index, TURN_DEV, 0)
    token_place = own_index * token_rows + jnp.arange(token_rows)
    token_slot = jnp.sum((token_place[:, None] >= own_starts[None, :]).astype(jnp.int32), axis=1)
    slot_mask = (token_slot[:, None] == jnp.arange(slot_count)[None, :]).astype(jnp.float32)
    low_slots = jnp.einsum("tc,scr->tsr", y_normed, down_slots, preferred_element_type=jnp.float32)
    rank_reduced = jnp.sum(low_slots * slot_mask[:, :, None], axis=1)
    rank_reduced = lax.psum(rank_reduced, "head").astype(jnp.bfloat16)
    adapter_out = jnp.einsum(
        "tr,srd->tsd", rank_reduced, up_slots, preferred_element_type=jnp.float32
    )
    adapter_out = jnp.sum(adapter_out * slot_mask[:, :, None], axis=1)
    return (base_out + adapter_out).astype(jnp.bfloat16)


def solution(mesh):
    in_specs = (
        P("ctx", "head"),
        P("ctx", "head"),
        P("ctx", "head"),
        P("ctx", "head"),
        P("head", "ctx"),
        P("head"),
        P("head"),
        P(None, "head"),
        P(None, "head"),
        P(None, "head"),
        P("head"),
        P("head", None),
        P("ctx", "head", None),
        P("ctx", None, "head"),
        P(),
        P(),
        P(),
    )
    out_specs = P("ctx", "head")
    return jax.shard_map(local, mesh=mesh, in_specs=in_specs, out_specs=out_specs, check_vma=False)
```

profile of v0, /device:TPU:0, one launch (start us, length us, event | category | flops | bytes accessed | tf_op | source)
XLA Modules:
  0.0 569.8 jit_solution(5970229263737441092)
XLA Ops:
  7.7 4.9 collective-permute-start
  13.3 3.4 collective-permute-start.2
  18.5 9.0 %reduce_window_sum.22 = f32[32,8,128]{2,1,0:T(8,128)S(1)} reduce-window(f32[32,8,128]{2,1,0:T(8,128)S(1)} %negate_multiply_fusion, f32[]{:T(128)} %constant.95.clone.1), window={size=1x1x128 pad=0_0x0_0x127_0}, to_apply=%region_0.1 | reduce-window | flops 4161536 | bytes 262148 | tf_op jit(solution)/shard_map/jit(cumsum)/reduce_window_sum | solution.py:72
  28.1 1.5 slice_convert_fusion.3
  30.4 1.4 slice_convert_fusion.7
  31.8 6.4 %copy.74 = bf16[1024,2048]{0,1:T(8,128)(2,1)} copy(bf16[1024,2048]{1,0:T(8,128)(2,1)} %param.19) | data formatting | bytes 8388608 | tf_op args[0]
  38.3 1.3 multiply_convert_fusion.1
  39.8 4.5 maximum_convert_fusion
  44.4 8.7 %fusion.31 = bf16[256,8,8,128]{3,1,2,0:T(8,128)(2,1)S(1)} fusion(f32[1027,2048]{0,1:T(8,128)S(1)} %maximum_convert_fusion, f32[2048]{0:T(1024)S(1)} %bitcast.149, f32[2048]{0:T(1024)S(1)} %bitcast.150, f32[2048]{0:T(1024)S(1)} %bitcast.148, f32[2048]{0:T(1024)S(1)} %bitcast.147), kind=kLoop, calls=%fused_computation.55 | loop fusion | flops 25165824 | bytes 37781504
  53.1 1.1 copy.110
  54.2 2.0 copy-done.4
  56.2 6.5 %fusion.7 = f32[8,2,16,64,128]{4,3,2,1,0:T(8,128)} fusion(f32[8,128,2,16]{1,3,2,0:T(8,128)S(1)} %get-tuple-element.66, bf16[8,128,2,16,64]{1,0,4,3,2:T(8,128)(2,1)S(1)} %bitcast.132, bf16[8,128,2,128,1]{3,2,1,0,4:T(2,128)(2,1)S(1)} %bitcast.138), kind=kOutput, calls=%fused_computation.19 | convolution fusion | flops 3225419776 | bytes 13238272 | tf_op jit(solution)/shard_map/cghk,ckghp,ckgn->cghpn/dot_general | solution.py:85
  62.7 20.0 %while.13 = (s32[]{:T(128)}, f32[2,16,64,128]{3,2,1,0:T(8,128)S(1)}, f32[8,2,16,64,128]{4,3,2,1,0:T(8,128)}, f32[8,2,16]{2,1,0:T(2,128)S(1)}, f32[8,2,16,64,128]{4,3,2,1,0:T(8,128)}, /*index=5*/s32[]{:T(128)}, s32[]{:T(128)}) while((s32[]{:T(128)}, f32[2,16,64,128]{3,2,1,0:T(8,128)S(1)}, f32[8,2,16,64,128]{4,3,2,1,0:T(8,128)}, ...), condition=%wide.region_2.3_spmd.clone, body=%wide.region_1.2_spmd.clone.sunk | while | flops 1048579 | bytes 5243872 | solution.py:95
  62.7 1.1 bitcast_dynamic-update-slice_fusion.2
  63.8 1.4 bitcast_add_fusion.2
  66.2 1.4 bitcast_add_fusion.2
  67.7 1.1 bitcast_dynamic-update-slice_fusion.2
  68.8 1.4 bitcast_add_fusion.2
  71.3 1.4 bitcast_add_fusion.2
  73.8 1.4 bitcast_add_fusion.2
  75.2 1.1 bitcast_dynamic-update-slice_fusion.2
  76.3 1.4 bitcast_add_fusion.2
  78.8 1.4 bitcast_add_fusion.2
  80.2 1.1 bitcast_dynamic-update-slice_fusion.2
  81.3 1.4 bitcast_add_fusion.2
  85.3 3.4 collective-permute-start.1
  88.7 6.6 %copy.92 = bf16[1024,2048]{0,1:T(8,128)(2,1)} copy(bf16[1024,2048]{1,0:T(8,128)(2,1)} %param.22) | data formatting | bytes 8388608 | tf_op args[3]
  95.2 18.4 %all-gather.2 = f32[8,2,16]{2,1,0:T(2,128)S(1)} all-gather(f32[1,2,16]{2,1,0:T(2,128)S(1)} %bitcast.151), channel_id=2, replica_groups=mesh['ctx'=8,'head'=4] {'ctx'}, dimensions={0}, use_global_device_ids=true | all-gather | bytes 1152 | tf_op jit(solution)/shard_map/all_gather | solution.py:102
  113.8 5.9 %fusion.36 = f32[256,8,8,128]{3,1,2,0:T(8,128)} fusion(bf16[1024,2048]{0,1:T(8,128)(2,1)} %copy.92), kind=kLoop, calls=%fused_computation.58 | loop fusion | flops 10485760 | bytes 12582912
  119.9 8.9 %copy.113 = f32[256,8,8,128]{3,2,1,0:T(8,128)} copy(f32[256,8,8,128]{3,1,2,0:T(8,128)} %fusion.36) | data formatting | bytes 16777216
  130.2 8.2 %fusion.51 = f32[8,2,16,64,128]{4,3,2,1,0:T(8,128)} fusion(f32[8,2,16,64,128]{4,3,2,1,0:T(8,128)} %get-tuple-element.33, bf16[8,128,2,128,1]{3,2,1,0,4:T(2,128)(2,1)S(1)} %bitcast.134), kind=kOutput, calls=%fused_computation.89 | convolution fusion | flops 3221225472 | bytes 17301504 | tf_op jit(solution)/shard_map/cqgn,cghpn->cqghp/dot_general | solution.py:98
  138.4 70.7 %all-gather.11.cloned.1.call-done = f32[16,16,64,128]{3,2,1,0:T(8,128)} async-done(((f32[2,16,64,128]{3,2,1,0:T(8,128)}), f32[16,16,64,128]{3,2,1,0:T(8,128)}) %all-gather.11.cloned.1.call-update) | async-done | bytes 8388624 | tf_op jit(solution)/shard_map/all_gather | solution.py:103
  209.1 15.6 %fusion.20 = f32[2,16,1,64,128]{4,2,3,1,0:T(1,128)S(1)} fusion(f32[8,2,16,1,1]{0,3,4,2,1:T(1,128)S(1)} %copy.97, f32[8,2,16,64,128]{4,3,2,1,0:T(8,128)} %bitcast.136), kind=kOutput, calls=%fused_computation.39 | convolution fusion | flops 25165824 | bytes 9438208 | tf_op jit(solution)/shard_map/jgh,jghpn->ghpn/dot_general | solution.py:111
  224.8 3.5 fusion.49
  228.3 21.4 %fusion.23 = (f32[8,128,2]{1,2,0:T(2,128)S(1)}, f32[8,128,2,16,64]{1,4,3,2,0:T(8,128)S(1)}) fusion(f32[8,128,2,16,64]{1,0,4,3,2:T(8,128)} %bitcast.137, bf16[8,128,2,16,64]{1,0,4,3,2:T(8,128)(2,1)S(1)} %bitcast.133, f32[2,16]{1,0:T(2,128)S(1)} %mul.352, f32[2,16,64,8,128]{4,2,1,0,3:T(8,128)S(1)} %fusion.49, f32[8,128,2,16]{1,3,2,0:T(8,128)S(1)} %get-tuple-element.64, ...), kind=kOutput, calls=%fused_computation.43 | convolution fusion | flops 3263166464 | bytes 39346304 | tf_op jit(solution)/shard_map/cghqk,ckghp->cqghp/dot_general | solution.py:83
  249.8 7.7 %copy.91 = f32[8,128,2,16,64]{1,0,4,3,2:T(8,128)S(1)} copy(f32[8,128,2,16,64]{1,4,3,2,0:T(8,128)S(1)} %get-tuple-element.83) | data formatting | bytes 16777216 | tf_op jit(solution)/shard_map/add | solution.py:117
  257.6 3.1 fusion.14
  260.7 2.0 copy-done.6
  262.7 22.8 %convolution_convert_fusion = bf16[1024,4096]{1,0:T(8,128)(2,1)} fusion(bf16[1024,2048]{0,1:T(8,128)(2,1)S(1)} %fusion.14, bf16[2048,4096]{1,0:T(8,128)(2,1)} %param.30), kind=kOutput, calls=%fused_computation.51 | convolution fusion | flops 17184063488 | bytes 29360128 | tf_op jit(solution)/shard_map/dot_general | solution.py:139
  287.1 21.5 %all-gather.9.cloned.1.call-done = bf16[48,64,1024]{2,1,0:T(8,128)(2,1)} async-done(((bf16[6,64,1024]{2,1,0:T(8,128)(2,1)}), bf16[48,64,1024]{2,1,0:T(8,128)(2,1)}) %all-gather.9.cloned.1.call-update) | async-done | bytes 6291472 | tf_op jit(solution)/shard_map/all_gather | solution.py:134
  308.5 3.4 gather_fusion.3
  311.9 173.5 %all-gather.7.cloned.1.call-done = bf16[48,2048,64]{1,2,0:T(8,128)(2,1)} async-done(((bf16[6,2048,64]{1,2,0:T(8,128)(2,1)}), bf16[48,2048,64]{1,2,0:T(8,128)(2,1)}) %all-gather.7.cloned.1.call-update) | async-done | bytes 12582928 | tf_op jit(solution)/shard_map/all_gather | solution.py:133
  485.4 5.2 gather_fusion.2
  490.7 3.6 fusion.74
  494.4 14.1 %all-reduce.1 = bf16[1024,64]{0,1:T(8,128)(2,1)S(1)} all-reduce(f32[1024,64]{0,1:T(8,128)S(1)} %multiply_reduce_fusion.1), channel_id=1, replica_groups=mesh['ctx'=8,'head'=4] {'head'}, use_global_device_ids=true, to_apply=%region_9.10 | all-reduce | flops 65536 | bytes 393216 | tf_op jit(solution)/shard_map/psum | solution.py:150
  508.5 4.5 multiply_reduce_fusion
  512.9 44.9 %reduce-scatter.2.cloned.1.call-done = bf16[1024,1024]{1,0:T(8,128)(2,1)} async-done(((bf16[1024,4096]{1,0:T(8,128)(2,1)}), bf16[1024,1024]{1,0:T(8,128)(2,1)}) %reduce-scatter.2.cloned.1.call-update) | async-done | bytes 2097168 | tf_op jit(solution)/shard_map/reduce_scatter | solution.py:138
  557.8 5.0 add_convert_fusion
  (107 shorter events, 15.4 us)
Async XLA Ops:
  6.5 279.0 %copy-start = (s32[16]{0:T(128)S(1)}, s32[16]{0:T(128)}, u32[]{:S(2)}) copy-start(s32[16]{0:T(128)} %param.34) | copy-start | bytes 196
  6.5 31.7 %copy-start.7 = (bf16[1024,256]{1,0:T(8,128)(2,1)S(1)}, bf16[1024,256]{1,0:T(8,128)(2,1)}, u32[]{:S(2)}) copy-start(bf16[1024,256]{1,0:T(8,128)(2,1)} %param.20) | copy-start | bytes 1572868
  6.5 202.6 %all-gather.11.cloned.1.call-start = ((), (), s32[]{:S(2)}) async-start(), calls=%async_computation.4 | async-start | bytes 9437184 | tf_op jit(solution)/shard_map/all_gather | solution.py:103
  7.7 32.1 %collective-permute-start = (bf16[3,2048]{0,1:T(8,128)(2,1)S(1)}, bf16[3,2048]{0,1:T(8,128)(2,1)S(1)}, u32[]{:S(2)}, u32[]{:S(2)}) collective-permute-start(bf16[3,2048]{0,1:T(8,128)(2,1)S(1)} %copy.73), channel_id=1, source_target_pairs={{0,4},{4,8},{8,12},{12,16},{16,20},{20,24},{24,28},{1,5},{5,9},{9,... | collective-permute-start | bytes 36872 | tf_op jit(solution)/shard_map/ppermute | solution.py:20
  13.3 24.9 %collective-permute-start.2 = (bf16[3,256]{1,0:T(4,128)(2,1)S(1)}, bf16[3,256]{1,0:T(4,128)(2,1)S(1)}, u32[]{:S(2)}, u32[]{:S(2)}) collective-permute-start(bf16[3,256]{1,0:T(4,128)(2,1)S(1)} %slice.104), channel_id=1, source_target_pairs={{0,4},{4,8},{8,12},{12,16},{16,20},{20,24},{24,28},{1,5},{5,9},{9,... | collective-permute-start | bytes 4616 | tf_op jit(solution)/shard_map/ppermute | solution.py:20
  39.8 4.5 copy-start.11
  39.8 4.5 copy-start.12
  39.8 4.5 copy-start.13
  39.8 4.5 copy-start.14
  54.2 2.0 copy-start.4
  62.7 22.6 %copy-start.8 = (bf16[1024,256]{1,0:T(8,128)(2,1)S(1)}, bf16[1024,256]{1,0:T(8,128)(2,1)}, u32[]{:S(2)}) copy-start(bf16[1024,256]{1,0:T(8,128)(2,1)} %param.21) | copy-start | bytes 1572868
  82.7 1.0 copy-start.2
  82.7 31.1 %copy-start.15 = (bf16[4,256]{1,0:T(4,128)(2,1)S(1)}, bf16[4,256]{1,0:T(4,128)(2,1)}, u32[]{:S(2)}) copy-start(bf16[4,256]{1,0:T(4,128)(2,1)} %param.28) | copy-start | bytes 6148
  83.7 224.8 %all-gather.9.cloned.1.call-start = ((), (), s32[]{:S(2)}) async-start(), calls=%async_computation.3 | async-start | bytes 7077888 | tf_op jit(solution)/shard_map/all_gather | solution.py:134
  84.5 400.9 %all-gather.7.cloned.1.call-start = ((), (), s32[]{:S(2)}) async-start(), calls=%async_computation.2 | async-start | bytes 14155776 | tf_op jit(solution)/shard_map/all_gather | solution.py:133
  85.2 472.6 %reduce-scatter.2.cloned.1.call-start = ((), (), s32[]{:S(2)}) async-start(), calls=%async_computation.1 | async-start | bytes 10485760 | tf_op jit(solution)/shard_map/reduce_scatter | solution.py:138
  85.3 43.6 %collective-permute-start.1 = (bf16[3,256]{1,0:T(4,128)(2,1)S(1)}, bf16[3,256]{1,0:T(4,128)(2,1)S(1)}, u32[]{:S(2)}, u32[]{:S(2)}) collective-permute-start(bf16[3,256]{1,0:T(4,128)(2,1)S(1)} %slice.95), channel_id=1, source_target_pairs={{0,4},{4,8},{8,12},{12,16},{16,20},{20,24},{24,28},{1,5},{5,9},{9,... | collective-permute-start | bytes 4616 | tf_op jit(solution)/shard_map/ppermute | solution.py:20
  119.9 8.9 %copy-start.17 = (f32[32]{0:T(128)S(1)}, f32[32]{0:T(128)}, u32[]{:S(2)}) copy-start(f32[32]{0:T(128)} %param.25) | copy-start | bytes 388
  119.9 9.0 %copy-start.16 = (bf16[2048]{0:T(1024)(128)(2,1)S(1)}, bf16[2048]{0:T(1024)(128)(2,1)}, u32[]{:S(2)}) copy-start(bf16[2048]{0:T(1024)(128)(2,1)} %param.29) | copy-start | bytes 12292
  209.1 19.2 %slice-start = ((s8[8388608]{0:T(1024)(128)(4,1)}), s8[4194304]{0:T(1024)(128)(4,1)S(1)}, s32[]{:S(2)}) async-start(s8[8388608]{0:T(1024)(128)(4,1)} %bitcast.130), calls=%async_computation.5 | async-start | bytes 8388608
  224.7 3.6 copy-start.5
  224.7 3.6 copy-start.9
  224.7 3.6 copy-start.10
  224.7 3.6 slice-start.1
  249.8 7.8 %copy-start.3 = (bf16[1024,2048]{0,1:T(8,128)(2,1)S(1)}, bf16[1024,2048]{0,1:T(8,128)(2,1)}, u32[]{:S(2)}) copy-start(bf16[1024,2048]{0,1:T(8,128)(2,1)} %copy.92) | copy-start | bytes 12582916
  260.7 2.0 copy-start.6
  285.4 0.7 copy-start.1
  285.4 1.4 copy-start.18
Sparse Core Ops, SparseCore 0:
  83.8 125.2 all-gather.10
  211.3 97.1 all-gather.8
  310.7 174.6 all-gather.6
  487.8 69.9 reduce-scatter.1
where the time goes:
time: 578 us; the launch traced here: 570 us
  waiting for transfers between devices  312 us (54%)
  matrix products  86.7 us (15%)
  other arithmetic  63.9 us (11%)
  local copies, waits for them, and re-layouts  48.6 us (8%)
  blocking collectives  32.5 us (6%)
  between operations  14.1 us (2%)
  starting transfers between devices  11.8 us (2%)
    all_gather x1, waiting for transfers between devices, local(): lax.all_gather(adapter_down_panels, 'ctx', axis=0, tiled=True)  173 us
    all_gather x1, waiting for transfers between devices, local(): lax.all_gather(device_state[None], 'ctx', axis=0, tiled=True)  70.7 us
    reduce_scatter x1, waiting for transfers between devices, local(): lax.psum_scatter(jnp.dot(y_normed, output_weight, preferred_element_type=...  44.9 us
    unnamed x48, local copies, waits for them, and re-layouts  28.1 us
    dot_general x1, matrix products, local(): jnp.dot(y_normed, output_weight, preferred_element_type=jnp.float32)  22.8 us
    all_gather x1, waiting for transfers between devices, local(): lax.all_gather(adapter_up_panels, 'ctx', axis=0, tiled=True)  21.5 us
    dot_general x1, matrix products, local(): jnp.einsum('cghqk,ckghp->cqghp', mixing, x_blocks, precision=highest)  21.4 us
    all_gather x1, blocking collectives, local(): lax.all_gather(device_log[None], 'ctx', axis=0, tiled=True)  18.4 us
  transfers between devices with their start and end apart: 7, of which 4 were waited for; matrix products, arithmetic and copies ran while one was open for 26% of the time, Pallas kernels for 0%

commit v1 on v0

v1 whole, which is shorter than its diff:
```python
import functools

import jax
import jax.numpy as jnp
from jax import lax
from jax.experimental import pallas as pl
from jax.experimental.pallas import tpu as pltpu
from jax.sharding import PartitionSpec as P

P_SIZE = 64
N = 128
K = 4
Q = 128
TURN_DEV = 2
HALO = 16
LANES = 128
PIECES = 4
Y_PARTS = 4

F32 = jnp.float32
BF16 = jnp.bfloat16
epsilon = 1e-05
VMEM_LIMIT = 48 * 1024 * 1024


def params():
    return pltpu.CompilerParams(vmem_limit_bytes=VMEM_LIMIT)


def cost(flops, moved):
    return pl.CostEstimate(flops=int(flops), bytes_accessed=int(moved), transcendentals=0)


def silu(v):
    half = 0.5 * v
    return half + half * jnp.tanh(half)


def conv_rows(current, previous, taps):
    rows = current.shape[0]
    joined = jnp.concatenate([previous, current], axis=0)
    total = taps[K - 1 : K] * current
    for back in range(1, K):
        total = total + taps[K - 1 - back : K - back] * pltpu.roll(joined, back, 0)[8 : 8 + rows]
    return silu(total).astype(BF16)


def two_terms(v):
    high = v.astype(BF16).astype(F32)
    return high, v - high


def pad_rows(stack):
    rows = stack.shape[0]
    if rows % LANES:
        fill = jnp.zeros((LANES - rows % LANES, stack.shape[1]), F32)
        stack = jnp.concatenate([stack, fill], axis=0)
    return stack


def panel_kernel(local_ref, owned_ref, down_ref, up_ref, out_ref):
    turn = pl.program_id(0)
    half = down_ref.shape[1] // 2
    rank = down_ref.shape[2]

    @pl.when(owned_ref[turn] == 1)
    def _():
        out_ref[0, :half, :] = jnp.concatenate(
            [down_ref[0, :half, :], down_ref[0, half:, :]], axis=1
        )
        for part in range(up_ref.shape[2] // LANES):
            out_ref[0, half + part * rank : half + (part + 1) * rank, :] = up_ref[
                0, :, part * LANES : (part + 1) * LANES
            ]

    @pl.when(owned_ref[turn] == 0)
    def _():
        out_ref[...] = jnp.zeros_like(out_ref)


def pack_panels(down, up, local_index, owned):
    turns = local_index.shape[0]
    _, channels, rank = down.shape
    features = up.shape[2]
    rows = channels // 2 + rank * (features // LANES)
    return pl.pallas_call(
        panel_kernel,
        grid_spec=pltpu.PrefetchScalarGridSpec(
            num_scalar_prefetch=2,
            grid=(turns,),
            in_specs=[
                pl.BlockSpec((1, channels, rank), lambda j, loc, own: (loc[j], 0, 0)),
                pl.BlockSpec((1, rank, features), lambda j, loc, own: (loc[j], 0, 0)),
            ],
            out_specs=pl.BlockSpec((1, rows, LANES), lambda j, loc, own: (j, 0, 0)),
        ),
        out_shape=jax.ShapeDtypeStruct((turns, rows, LANES), BF16),
        compiler_params=params(),
        cost_estimate=cost(0, turns * rows * LANES * 4),
        name="pack_panels",
    )(local_index, owned, down, up)


def state_kernel(
    parity_ref, x_ref, b_ref, halo_ref, raw_ref, rate_ref, xt_ref, bt_ref, spread_ref,
    xc_ref, bc_ref, run_ref, shifted_ref, before_ref, start_ref, keep_ref, send_ref,
    x_prev, b_prev, weight, x_weighted, state, decay_product,
):
    block = pl.program_id(0)
    inner = x_ref.shape[1]
    bc_width = b_ref.shape[1]
    groups = bc_width // N
    width = inner // groups

    @pl.when(block == 0)
    def _():
        x_prev[...] = halo_ref[:, :inner].astype(F32)[8:]
        b_prev[...] = halo_ref[:, inner : inner + bc_width].astype(F32)[8:]
        state[...] = jnp.zeros_like(state)
        decay_product[...] = jnp.ones_like(decay_product)

    raw = raw_ref[...]
    step = jnp.maximum(raw, 0.0) + jnp.log1p(jnp.exp(-jnp.abs(raw)))
    change = -step * jnp.exp(rate_ref[...])
    heads = raw.shape[0]
    first = change.astype(BF16)
    rest = change - first.astype(F32)
    second = rest.astype(BF16)
    third = (rest - second.astype(F32)).astype(BF16)
    upper = (
        lax.broadcasted_iota(jnp.int32, (Q, Q), 0) <= lax.broadcasted_iota(jnp.int32, (Q, Q), 1)
    ).astype(F32).astype(BF16)
    sums = jnp.dot(jnp.concatenate([first, second, third], axis=0), upper, preferred_element_type=F32)
    run = sums[:heads] + sums[heads : 2 * heads] + sums[2 * heads :]
    run_ref[...] = run
    shifted_ref[...] = jnp.log(step) - run
    last = run[:, Q - 1 : Q]
    tail = jnp.exp(last - run) * step
    whole = jnp.broadcast_to(jnp.exp(last), (heads, Q))
    columns = pad_rows(jnp.concatenate([*two_terms(tail), *two_terms(whole)], axis=0)).T
    spread = spread_ref[...]
    weight[...] = jnp.dot(columns[:, : 2 * heads].astype(BF16), spread, preferred_element_type=F32)
    decay_row = jnp.dot(
        columns[:16, 2 * heads : 4 * heads].astype(BF16), spread, preferred_element_type=F32
    )[:8]

    bc = conv_rows(b_ref[...].astype(F32), b_prev[...], bt_ref[...].astype(F32))
    b_prev[...] = b_ref[Q - HALO :, :].astype(F32)[8:]
    bc_ref[...] = bc

    def conv_lanes(part, carried):
        lanes = pl.ds(pl.multiple_of(part * LANES, LANES), LANES)
        current = x_ref[:, lanes].astype(F32)
        xc = conv_rows(current, x_prev[:, lanes], xt_ref[:, lanes].astype(F32))
        x_prev[:, lanes] = current[Q - 8 :]
        xc_ref[:, lanes] = xc
        x_weighted[:, lanes] = (xc.astype(F32) * weight[:, lanes]).astype(BF16)
        return carried

    lax.fori_loop(0, inner // LANES, conv_lanes, 0, unroll=2)

    start_ref[...] = decay_product[...]
    decay_product[...] = decay_product[...] * decay_row
    for group in range(groups):
        lanes = slice(group * width, (group + 1) * width)
        fresh = lax.dot_general(
            bc[:, group * N : (group + 1) * N],
            x_weighted[:, lanes],
            (((0,), (0,)), ((), ())),
            preferred_element_type=F32,
        )
        held = state[:, lanes]
        before_ref[:, lanes] = held.astype(BF16)
        state[:, lanes] = held * decay_row[:1, lanes] + fresh

    @pl.when(block == pl.num_programs(0) - 1)
    def _():
        half = inner // 2
        row = lax.broadcasted_iota(jnp.int32, (HALO, half), 0)
        for out_ref, place in ((keep_ref, parity_ref[0]), (send_ref, 1 - parity_ref[0])):
            lanes = pl.ds(pl.multiple_of(place * half, LANES), half)
            out_ref[:N] = state[:, lanes].astype(BF16)
            high, low = two_terms(decay_product[:1, lanes])
            out_ref[N:] = jnp.where(row == 0, high, jnp.where(row == 1, low, 0.0)).astype(BF16)


def local_states(parity, x, b, halo, raw, rate, x_taps, b_taps, spread):
    tokens, inner = x.shape
    bc_width = b.shape[1]
    heads = raw.shape[0]
    blocks = tokens // Q
    half = inner // 2
    whole = lambda c, p: (0, 0)
    rows = lambda c, p: (c, 0)
    columns = lambda c, p: (0, c)
    return pl.pallas_call(
        state_kernel,
        grid_spec=pltpu.PrefetchScalarGridSpec(
            num_scalar_prefetch=1,
            grid=(blocks,),
            in_specs=[
                pl.BlockSpec((Q, inner), rows),
                pl.BlockSpec((Q, bc_width), rows),
                pl.BlockSpec(halo.shape, whole),
                pl.BlockSpec((heads, Q), columns),
                pl.BlockSpec((heads, 1), whole),
                pl.BlockSpec((K, inner), whole),
                pl.BlockSpec((K, bc_width), whole),
                pl.BlockSpec(spread.shape, whole),
            ],
            out_specs=[
                pl.BlockSpec((Q, inner), rows),
                pl.BlockSpec((Q, bc_width), rows),
                pl.BlockSpec((heads, Q), columns),
                pl.BlockSpec((heads, Q), columns),
                pl.BlockSpec((N, inner), rows),
                pl.BlockSpec((8, inner), rows),
                pl.BlockSpec((N + HALO, half), whole),
                pl.BlockSpec((N + HALO, half), whole),
            ],
            scratch_shapes=[
                pltpu.VMEM((8, inner), F32),
                pltpu.VMEM((8, bc_width), F32),
                pltpu.VMEM((Q, inner), F32),
                pltpu.VMEM((Q, inner), BF16),
                pltpu.VMEM((N, inner), F32),
                pltpu.VMEM((8, inner), F32),
            ],
        ),
        out_shape=[
            jax.ShapeDtypeStruct((tokens, inner), BF16),
            jax.ShapeDtypeStruct((tokens, bc_width), BF16),
            jax.ShapeDtypeStruct((heads, tokens), F32),
            jax.ShapeDtypeStruct((heads, tokens), F32),
            jax.ShapeDtypeStruct((blocks * N, inner), BF16),
            jax.ShapeDtypeStruct((blocks * 8, inner), F32),
            jax.ShapeDtypeStruct((N + HALO, half), BF16),
            jax.ShapeDtypeStruct((N + HALO, half), BF16),
        ],
        compiler_params=params(),
        cost_estimate=cost(10e9, 20e6),
        name="local_states",
    )(parity, x, b, halo, raw, rate, x_taps, b_taps, spread)


def mix_kernel(
    first, has_alias, *refs
):
    (
        xc_ref, bc_ref, c_ref, c_prev_ref, halo_ref, run_ref, shifted_ref, before_ref, start_ref,
        gate_ref, skip_ref, ct_ref, spread_ref,
    ) = refs[:13]
    refs = refs[13 + (3 if has_alias else 0) :]
    part_ref, scale_ref, cc_ref, rise = refs
    block = pl.program_id(0) + first
    inner = xc_ref.shape[1]
    bc_width = c_ref.shape[1]
    groups = bc_width // N
    width = inner // groups
    heads = run_ref.shape[0]

    c_halo = halo_ref[:, inner + bc_width :].astype(F32)[8:]
    c_before = jnp.where(block == 0, c_halo, c_prev_ref[...].astype(F32)[8:])
    cc = conv_rows(c_ref[...].astype(F32), c_before, ct_ref[...].astype(F32))
    cc_ref[...] = cc
    run = run_ref[...]
    columns = pad_rows(jnp.concatenate([*two_terms(jnp.exp(run)), run], axis=0)).T
    rise[...] = jnp.dot(
        columns[:, : 2 * heads].astype(BF16), spread_ref[...], preferred_element_type=F32
    )
    causal = lax.broadcasted_iota(jnp.int32, (Q, Q), 0) >= lax.broadcasted_iota(jnp.int32, (Q, Q), 1)
    left = lax.broadcasted_iota(jnp.int32, (Q, LANES), 1) < P_SIZE
    for group in range(groups):
        state_lanes = slice(group * N, (group + 1) * N)
        scores = lax.dot_general(
            cc[:, state_lanes],
            bc_ref[:, state_lanes],
            (((1,), (1,)), ((), ())),
            preferred_element_type=F32,
        )
        scores = jnp.where(causal, scores, 0.0)
        for pair in range(width // LANES):
            lanes = slice(group * width + pair * LANES, group * width + (pair + 1) * LANES)
            mixing = []
            for head in (lanes.start // P_SIZE, lanes.start // P_SIZE + 1):
                gap = columns[:, 2 * heads + head : 2 * heads + head + 1] + shifted_ref[head : head + 1, :]
                mixing.append((scores * jnp.exp(jnp.where(causal, gap, 0.0))).astype(BF16))
            x = xc_ref[:, lanes].astype(F32)
            x_pair = jnp.concatenate(
                [jnp.where(left, x, 0.0).astype(BF16), jnp.where(left, 0.0, x).astype(BF16)], axis=0
            )
            y = jnp.dot(jnp.concatenate(mixing, axis=1), x_pair, preferred_element_type=F32)
            carried = jnp.dot(cc[:, state_lanes], before_ref[:, lanes], preferred_element_type=F32)
            rise_part = rise[:, lanes]
            y = y + rise_part * carried + skip_ref[:, lanes] * x
            gate = silu(gate_ref[:, lanes].astype(F32))
            part_ref[:, lanes] = (y * gate).astype(BF16)
            scale_ref[:, lanes] = (gate * rise_part * start_ref[:1, lanes]).astype(BF16)


def mix(first, count, xc, bc, c, halo, run, shifted, before, start, gate, skip, c_taps, spread, held):
    tokens, inner = xc.shape
    bc_width = c.shape[1]
    heads = run.shape[0]
    whole = lambda i: (0, 0)
    rows = lambda i: (first + i, 0)
    columns = lambda i: (0, first + i)
    per_block = Q // HALO
    any_spec = pl.BlockSpec(memory_space=pl.ANY)
    aliased = list(held) if held is not None else []
    return pl.pallas_call(
        functools.partial(mix_kernel, first, bool(aliased)),
        grid=(count,),
        in_specs=[
            pl.BlockSpec((Q, inner), rows),
            pl.BlockSpec((Q, bc_width), rows),
            pl.BlockSpec((Q, bc_width), rows),
            pl.BlockSpec((HALO, bc_width), lambda i: (jnp.maximum((first + i) * per_block - 1, 0), 0)),
            pl.BlockSpec(halo.shape, whole),
            pl.BlockSpec((heads, Q), columns),
            pl.BlockSpec((heads, Q), columns),
            pl.BlockSpec((N, inner), rows),
            pl.BlockSpec((8, inner), rows),
            pl.BlockSpec((Q, inner), rows),
            pl.BlockSpec((1, inner), whole),
            pl.BlockSpec((K, bc_width), whole),
            pl.BlockSpec(spread.shape, whole),
        ]
        + [any_spec] * len(aliased),
        out_specs=[
            pl.BlockSpec((Q, inner), rows),
            pl.BlockSpec((Q, inner), rows),
            pl.BlockSpec((Q, bc_width), rows),
        ],
        out_shape=[
            jax.ShapeDtypeStruct((tokens, inner), BF16),
            jax.ShapeDtypeStruct((tokens, inner), BF16),
            jax.ShapeDtypeStruct((tokens, bc_width), BF16),
        ],
        input_output_aliases={13 + i: i for i in range(len(aliased))},
        scratch_shapes=[pltpu.VMEM((Q, inner), F32)],
        compiler_params=params(),
        cost_estimate=cost(count * 2e9, count * 3e6),
        name="mix",
    )(xc, bc, c, c, halo, run, shifted, before, start, gate, skip, c_taps, spread, *aliased)


def norm_kernel(parity_ref, part_ref, scale_ref, cc_ref, keep_ref, got_ref, gain_ref, out_ref, state):
    inner = part_ref.shape[1]
    groups = cc_ref.shape[1] // N
    width = inner // groups
    half = inner // 2

    @pl.when(pl.program_id(0) == 0)
    def _():
        for ref, place in ((keep_ref, parity_ref[0]), (got_ref, 1 - parity_ref[0])):
            state[:, pl.ds(pl.multiple_of(place * half, LANES), half)] = ref[...]

    for group in range(groups):
        lanes = slice(group * width, (group + 1) * width)
        carried = jnp.dot(
            cc_ref[:, group * N : (group + 1) * N], state[:, lanes], preferred_element_type=F32
        )
        gated = part_ref[:, lanes].astype(F32) + scale_ref[:, lanes].astype(F32) * carried
        mean = jnp.sum(gated * gated, axis=1, keepdims=True) * (1.0 / width)
        out_ref[:, lanes] = (gated * lax.rsqrt(mean + epsilon) * gain_ref[:, lanes]).astype(BF16)


def finish_norm(parity, part, scale, cc, keep, got, gain):
    tokens, inner = part.shape
    tile = 2 * Q
    whole = lambda i, p: (0, 0)
    rows = lambda i, p: (i, 0)
    return pl.pallas_call(
        norm_kernel,
        grid_spec=pltpu.PrefetchScalarGridSpec(
            num_scalar_prefetch=1,
            grid=(tokens // tile,),
            in_specs=[
                pl.BlockSpec((tile, inner), rows),
                pl.BlockSpec((tile, inner), rows),
                pl.BlockSpec((tile, cc.shape[1]), rows),
                pl.BlockSpec(keep.shape, whole),
                pl.BlockSpec(got.shape, whole),
                pl.BlockSpec((1, inner), whole),
            ],
            out_specs=pl.BlockSpec((tile, inner), rows),
            scratch_shapes=[pltpu.VMEM((N, inner), BF16)],
        ),
        out_shape=jax.ShapeDtypeStruct((tokens, inner), BF16),
        compiler_params=params(),
        cost_estimate=cost(2e9, 13e6),
        name="finish_norm",
    )(parity, part, scale, cc, keep, got, gain)


def project_kernel(places_ref, y_ref, w_ref, send_ref, keep_ref):
    rows = 256
    for which, out_ref in enumerate((send_ref, keep_ref)):

        @pl.when(pl.program_id(0) == which)
        def _(out_ref=out_ref):
            def tile(i, carried):
                at = pl.ds(pl.multiple_of(i * rows, rows), rows)
                out_ref[at, :] = jnp.dot(
                    y_ref[at, :], w_ref[...], preferred_element_type=F32
                ).astype(BF16)
                return carried

            lax.fori_loop(0, y_ref.shape[0] // rows, tile, 0)


def project(places, y, weight, width):
    tokens, inner = y.shape
    whole = lambda i, p: (0, 0)
    return pl.pallas_call(
        project_kernel,
        grid_spec=pltpu.PrefetchScalarGridSpec(
            num_scalar_prefetch=1,
            grid=(2,),
            in_specs=[
                pl.BlockSpec((tokens, inner), whole),
                pl.BlockSpec((inner, width), lambda i, p: (0, p[i])),
            ],
            out_specs=[pl.BlockSpec((tokens, width), whole)] * 2,
        ),
        out_shape=[jax.ShapeDtypeStruct((tokens, width), BF16)] * 2,
        compiler_params=params(),
        cost_estimate=cost(4 * tokens * inner * width, 2 * inner * (tokens + 2 * width)),
        name="project",
    )(places, y, weight)


def low_kernel(slot_ref, y_ref, panel_ref, out_ref):
    half = y_ref.shape[1] // 2
    rank = LANES // 2
    panel = panel_ref[0, :half, :]
    low = (
        jnp.dot(y_ref[:, :half], panel, preferred_element_type=F32)[:, :rank]
        + jnp.dot(y_ref[:, half:], panel, preferred_element_type=F32)[:, rank:]
    )
    fold = low.shape[0] // 2
    out_ref[...] = jnp.concatenate([low[:fold], low[fold:]], axis=1)


def low_part(slots, y, panels):
    tokens, inner = y.shape
    return pl.pallas_call(
        low_kernel,
        grid_spec=pltpu.PrefetchScalarGridSpec(
            num_scalar_prefetch=1,
            grid=(tokens // Q,),
            in_specs=[
                pl.BlockSpec((Q, inner), lambda i, s: (i, 0)),
                pl.BlockSpec((1,) + panels.shape[1:], lambda i, s: (s[i], 0, 0)),
            ],
            out_specs=pl.BlockSpec((Q // 2, LANES), lambda i, s: (i, 0)),
        ),
        out_shape=jax.ShapeDtypeStruct((tokens // 2, LANES), F32),
        compiler_params=params(),
        cost_estimate=cost(1e9, 6e6),
        name="low_part",
    )(slots, y, panels)


def final_kernel(count, slot_ref, own_ref, pair_ref, low_ref, panel_ref, *refs):
    parts, out_ref = refs[:-1], refs[-1]
    features = own_ref.shape[1]
    rank = LANES // 2
    base_row = panel_ref.shape[1] - rank * (features // LANES)
    low = low_ref[...].astype(BF16)
    low = jnp.concatenate([low[:, :rank], low[:, rank:]], axis=0)
    part_width = features // count
    for block in range(features // LANES):
        lanes = slice(block * LANES, (block + 1) * LANES)
        total = jnp.dot(
            low,
            panel_ref[0, base_row + block * rank : base_row + (block + 1) * rank, :],
            preferred_element_type=F32,
        )
        total = total + own_ref[:, lanes].astype(F32) + pair_ref[:, lanes].astype(F32)
        place = lanes.start // part_width
        inside = lanes.start - place * part_width
        for ref in parts[place::count]:
            total = total + ref[:, inside : inside + LANES].astype(F32)
        out_ref[:, lanes] = total.astype(BF16)


def final_sum(slots, own, pair, low, panels, parts, count):
    tokens, features = own.shape
    rows = lambda i, s: (i, 0)
    return pl.pallas_call(
        functools.partial(final_kernel, count),
        grid_spec=pltpu.PrefetchScalarGridSpec(
            num_scalar_prefetch=1,
            grid=(tokens // Q,),
            in_specs=[
                pl.BlockSpec((Q, features), rows),
                pl.BlockSpec((Q, features), rows),
                pl.BlockSpec((Q // 2, LANES), rows),
                pl.BlockSpec((1,) + panels.shape[1:], lambda i, s: (s[i], 0, 0)),
            ]
            + [pl.BlockSpec((Q, features // count), rows)] * len(parts),
            out_specs=pl.BlockSpec((Q, features), rows),
        ),
        out_shape=jax.ShapeDtypeStruct((tokens, features), BF16),
        compiler_params=params(),
        cost_estimate=cost(1e8, 10e6),
        name="final_sum",
    )(slots, own, pair, low, panels, *parts)


def shift_up(block, axis, distance):
    devices = range(lax.axis_size(axis))
    route = [(i, i + distance) for i in devices if i + distance in devices]
    return lax.ppermute(block, axis, route)


def swap(block, axis, bits):
    return lax.ppermute(block, axis, [(i, i ^ bits) for i in range(lax.axis_size(axis))])


def unpacked(packed):
    decay = packed[N : N + 1].astype(F32) + packed[N + 1 : N + 2].astype(F32)
    return packed[:N].astype(F32), decay


def packed(state, decay):
    high = decay.astype(BF16)
    low = (decay - high.astype(F32)).astype(BF16)
    fill = jnp.zeros((HALO - 2, state.shape[1]), BF16)
    return jnp.concatenate([state.astype(BF16), high, low, fill], axis=0)


def local(
    input_x_channels,
    input_b_channels,
    input_c_channels,
    input_gate_channels,
    raw_step_sizes,
    log_decay_rate,
    head_skip_coeff,
    x_conv_taps,
    b_conv_taps,
    c_conv_taps,
    gated_norm_gain,
    output_weight,
    adapter_down_panels,
    adapter_up_panels,
    turn_first_token,
    tenant_of_turn,
    tenant_panel_index,
):
    tokens, inner = input_x_channels.shape
    heads = log_decay_rate.shape[0]
    blocks = tokens // Q
    features = adapter_up_panels.shape[2]
    panel_count = adapter_down_panels.shape[0]
    ctx = lax.axis_index("ctx")
    head = lax.axis_index("head")
    parity = (ctx % 2).astype(jnp.int32)
    parity_arg = parity[None]

    edge = jnp.concatenate(
        [array[tokens - HALO :] for array in (input_x_channels, input_b_channels, input_c_channels)],
        axis=1,
    )
    halo = shift_up(edge, "ctx", 1)

    turn_panels = jnp.take(tenant_panel_index, tenant_of_turn)
    owned = (turn_panels // panel_count == ctx).astype(jnp.int32)
    local_index = jnp.where(owned == 1, turn_panels % panel_count, 0)
    packs = pack_panels(adapter_down_panels, adapter_up_panels, local_index, owned)
    own_packs = lax.psum_scatter(packs, "ctx", scatter_dimension=0, tiled=True)
    earlier_pack = shift_up(own_packs[TURN_DEV - 1 :], "ctx", 1)
    own_starts = lax.dynamic_slice_in_dim(turn_first_token, TURN_DEV * ctx, TURN_DEV, 0)
    block_starts = ctx * tokens + Q * jnp.arange(blocks)
    slots = jnp.sum((block_starts[:, None] >= own_starts[None, :]).astype(jnp.int32), axis=1)
    slots = slots.astype(jnp.int32)

    lane_head = jnp.arange(inner) // P_SIZE
    spread = (jnp.arange(2 * heads)[:, None] % heads == lane_head[None, :]).astype(BF16)
    xc, bc, run, shifted, before, start, keep, send = local_states(
        parity_arg,
        input_x_channels,
        input_b_channels,
        halo,
        raw_step_sizes,
        log_decay_rate[:, None],
        x_conv_taps,
        b_conv_taps,
        spread,
    )
    skip = jnp.repeat(head_skip_coeff, P_SIZE)[None]
    count = blocks // PIECES

    def mix_piece(piece, held):
        return mix(
            piece * count, count, xc, bc, input_c_channels, halo, run, shifted, before, start,
            input_gate_channels, skip, c_conv_taps, spread, held,
        )

    got = swap(send, "ctx", 1)
    held = mix_piece(0, None)
    own_state, own_decay = unpacked(keep)
    got_state, got_decay = unpacked(got)
    first = parity == 0
    first_state = jnp.where(first, own_state, got_state)
    first_decay = jnp.where(first, own_decay, got_decay)
    second_state = jnp.where(first, got_state, own_state)
    second_decay = jnp.where(first, got_decay, own_decay)
    window = second_state + second_decay * first_state
    window_decay = second_decay * first_decay
    pairs = lax.axis_size("ctx") // 2
    distance = 1
    incoming = None
    piece = 1
    while distance < pairs:
        arrived = shift_up(packed(window, window_decay), "ctx", 2 * distance)
        if piece < PIECES:
            held = mix_piece(piece, held)
            piece += 1
        state, decay = unpacked(arrived)
        if incoming is None:
            incoming, incoming_decay = state, decay
        else:
            incoming = incoming + incoming_decay * state
            incoming_decay = incoming_decay * decay
        window = window + window_decay * state
        window_decay = window_decay * decay
        distance *= 2
    incoming_second = first_state + first_decay * incoming
    back = swap(jnp.where(first, incoming_second, incoming).astype(BF16), "ctx", 1)
    kept = jnp.where(first, incoming, incoming_second).astype(BF16)
    while piece < PIECES:
        held = mix_piece(piece, held)
        piece += 1
    part, scale, cc = held
    y_normed = finish_norm(
        parity_arg, part, scale, cc, kept, back, gated_norm_gain.astype(F32)[None]
    )

    y_chips = lax.axis_size("head") // 2
    width = features // Y_PARTS
    parts = []
    for chip in range(1, y_chips):
        other = head ^ (2 * chip)
        for part_index in range(Y_PARTS):
            places = jnp.stack([(other ^ 1) * Y_PARTS + part_index, other * Y_PARTS + part_index])
            to_pair, mine = project(places.astype(jnp.int32), y_normed, output_weight, width)
            from_pair = swap(to_pair, "head", 1)
            both = (mine.astype(F32) + from_pair.astype(F32)).astype(BF16)
            parts.append(swap(both, "head", 2 * chip))
    places = jnp.stack([head ^ 1, head]).astype(jnp.int32)
    to_pair, own = project(places, y_normed, output_weight, features)
    pair = swap(to_pair, "head", 1)

    panels = jnp.concatenate([earlier_pack, own_packs], axis=0)
    low = low_part(slots, y_normed, panels)
    low = low + swap(low, "head", 1)
    low_sent = low.astype(BF16)
    for chip in range(1, y_chips):
        low = low + swap(low_sent, "head", 2 * chip).astype(F32)
    return final_sum(slots, own, pair, low, panels, parts, Y_PARTS)


def solution(mesh):
    in_specs = (
        P("ctx", "head"),
        P("ctx", "head"),
        P("ctx", "head"),
        P("ctx", "head"),
        P("head", "ctx"),
        P("head"),
        P("head"),
        P(None, "head"),
        P(None, "head"),
        P(None, "head"),
        P("head"),
        P("head", None),
        P("ctx", "head", None),
        P("ctx", None, "head"),
        P(),
        P(),
        P(),
    )
    out_specs = P("ctx", "head")
    return jax.shard_map(local, mesh=mesh, in_specs=in_specs, out_specs=out_specs, check_vma=False)
```

time: 578 us -> 233 us (0.40)
  the two profiles are of different devices: /device:TPU:0 before, /device:TPU:18 now
where the time goes in v1:
time: 233 us
  Pallas kernels  105 us (45%)
  waiting for transfers between devices  65.9 us (28%)
  starting transfers between devices  32.2 us (14%)
  between operations  13.8 us (6%)
  local copies, waits for them, and re-layouts  9.38 us (4%)
  other arithmetic  7.24 us (3%)
    pallas_call x5, Pallas kernels, project(): pl.pallas_call(project_kernel, grid_spec=pltpu.PrefetchScalarGridSpec(num...  41.4 us
    ppermute x13, waiting for transfers between devices, swap(): lax.ppermute(block, axis, [(i, i ^ bits) for i in range(lax.axis_size(axi...  40.1 us
    ppermute x4, waiting for transfers between devices, shift_up(): return lax.ppermute(block, axis, route)  24.6 us
    pallas_call x4, Pallas kernels, mix(): pl.pallas_call(functools.partial(mix_kernel, first, bool(aliased)), grid=...  20.5 us
    pallas_call x1, Pallas kernels, local_states(): pl.pallas_call(state_kernel, grid_spec=pltpu.PrefetchScalarGridSpec(num_s...  18.6 us
    ppermute x4, starting transfers between devices, shift_up(): return lax.ppermute(block, axis, route)  17.9 us
    ppermute x13, starting transfers between devices, swap(): lax.ppermute(block, axis, [(i, i ^ bits) for i in range(lax.axis_size(axi...  14.3 us
    pallas_call x1, Pallas kernels, pack_panels(): pl.pallas_call(panel_kernel, grid_spec=pltpu.PrefetchScalarGridSpec(num_s...  7.45 us
  transfers between devices with their start and end apart: 18, of which 10 were waited for; matrix products, arithmetic and copies ran while one was open for 4% of the time, Pallas kernels for 39%

profile of v1, /device:TPU:18, one launch (start us, length us, event | category | flops | bytes accessed | tf_op | source)
XLA Modules:
  0.0 233.4 jit_solution(14854600616899008570)
XLA Ops:
  6.5 0.7 compare_select_fusion
  7.3 3.1 %copy.32.down_ref = bf16[6,2048,64]{2,1,0:T(8,128)(2,1)S(1)} copy(bf16[6,2048,64]{1,2,0:T(8,128)(2,1)} %param.29) | data formatting | bytes 3145728 | tf_op args[12]
  10.4 0.7 gather_fusion
  11.1 1.1 copy-done.5
  12.3 7.5 %pack_panels.1 = bf16[16,1536,128]{2,1,0:T(8,128)(2,1)} custom-call(s32[16]{0:T(128)S(1)} %get-tuple-element.67.local_ref, s32[16]{0:T(128)S(1)} %get-tuple-element.68.owned_ref, bf16[6,2048,64]{2,1,0:T(8,128)(2,1)S(1)} %copy.32.down_ref, bf16[6,64,1024]{2,1,0:T(8,128)(2,1)S(1)} %copy-done.5), custom_call_target="tpu_custom_call" | custom-call | bytes 12582912 | tf_op jit(solution)/shard_map/pack_panels/pallas_call | solution.py:86
  19.8 0.6 slice-done
  20.6 3.2 %collective-permute-start = (bf16[16,2560]{1,0:T(8,128)(2,1)S(1)}, bf16[16,2560]{1,0:T(8,128)(2,1)S(1)}, u32[]{:S(2)}, u32[]{:S(2)}) collective-permute-start(bf16[16,2560]{1,0:T(8,128)(2,1)S(1)} %pad_maximum_fusion), channel_id=1, source_target_pairs={{0,4},{4,8},{8,12},{12,16},{16,20},{20,24},{24,28},{1,5},{5,9},{9,... | collective-permute-start | bytes 245768 | tf_op jit(solution)/shard_map/ppermute | solution.py:516
  24.8 2.1 collective-permute-done.halo_ref.refs_4_
  26.9 18.6 %local_states.1 = (bf16[1024,2048]{1,0:T(8,128)(2,1)}, bf16[1024,256]{1,0:T(8,128)(2,1)S(1)}, f32[32,1024]{1,0:T(8,128)S(1)}, f32[32,1024]{1,0:T(8,128)S(1)}, bf...) custom-call(s32[1]{0:T(128)} %bitcast.2.parity_ref, ...), custom_call_target="tpu_custom_call" | custom-call | flops 10000000000 | bytes 20000000 | tf_op jit(solution)/shard_map/local_states/pallas_call | solution.py:196
  45.6 1.6 collective-permute-start.1
  47.2 5.1 %mix.4 = (bf16[1024,2048]{1,0:T(8,128)(2,1)}, bf16[1024,2048]{1,0:T(8,128)(2,1)}, bf16[1024,256]{1,0:T(8,128)(2,1)S(1)}) custom-call(bf16[1024,2048]{1,0:T(8,128)(2,1)} %get-tuple-element.35.refs_0_, bf16[1024,256]{1,0:T(8,128)(2,1)S(1)} %get-tuple-element.36.refs_1_, bf16[1024,256]{1,0:T(8,128)(2,1)S(1)} %copy-done.4, bf16[1024,256]{1,0:T(8,128)(2,1)S(1)} %copy-done.4, ...), custom_call_target="tpu_custom_call" | custom-call | flops 4000000000 | bytes 6000000 | tf_op jit(solution)/shard_map/mix/pallas_call | solution.py:311
  52.3 4.7 %collective-permute-done.1 = bf16[144,1024]{1,0:T(8,128)(2,1)S(1)} collective-permute-done((bf16[144,1024]{1,0:T(8,128)(2,1)S(1)}, bf16[144,1024]{1,0:T(8,128)(2,1)S(1)}, u32[]{:S(2)}, u32[]{:S(2)}) %collective-permute-start.1) | collective-permute-done | bytes 294944 | tf_op jit(solution)/shard_map/ppermute | solution.py:520
  57.3 4.7 %collective-permute-start.2 = (bf16[144,1024]{1,0:T(8,128)(2,1)S(1)}, bf16[144,1024]{1,0:T(8,128)(2,1)S(1)}, u32[]{:S(2)}, u32[]{:S(2)}) collective-permute-start(bf16[144,1024]{1,0:T(8,128)(2,1)S(1)} %maximum_maximum_fusion), channel_id=1, source_target_pairs={{0,8},{4,12},{8,16},{12,20},{16,24},{20,28},{1,9},{5,13},{9,17},{1... | collective-permute-start | bytes 884744 | tf_op jit(solution)/shard_map/ppermute | solution.py:516
  61.9 5.1 %mix.5 = (bf16[1024,2048]{1,0:T(8,128)(2,1)}, bf16[1024,2048]{1,0:T(8,128)(2,1)}, bf16[1024,256]{1,0:T(8,128)(2,1)S(1)}) custom-call(bf16[1024,2048]{1,0:T(8,128)(2,1)} %get-tuple-element.35.refs_0_, bf16[1024,256]{1,0:T(8,128)(2,1)S(1)} %get-tuple-element.36.refs_1_, ...), custom_call_target="tpu_custom_call", output_to_operand_aliasing={{0}: (13, {}), {1}: (14, {}), {2}: (15, {})} | custom-call | flops 4000000000 | bytes 6000000 | tf_op jit(solution)/shard_map/mix/pallas_call | solution.py:311
  67.1 15.4 %collective-permute-done.2 = bf16[144,1024]{1,0:T(8,128)(2,1)S(1)} collective-permute-done((bf16[144,1024]{1,0:T(8,128)(2,1)S(1)}, bf16[144,1024]{1,0:T(8,128)(2,1)S(1)}, u32[]{:S(2)}, u32[]{:S(2)}) %collective-permute-start.2) | collective-permute-done | bytes 294944 | tf_op jit(solution)/shard_map/ppermute | solution.py:516
  82.8 1.5 collective-permute-start.3
  84.3 5.1 %mix.6 = (bf16[1024,2048]{1,0:T(8,128)(2,1)}, bf16[1024,2048]{1,0:T(8,128)(2,1)}, bf16[1024,256]{1,0:T(8,128)(2,1)S(1)}) custom-call(bf16[1024,2048]{1,0:T(8,128)(2,1)} %get-tuple-element.35.refs_0_, bf16[1024,256]{1,0:T(8,128)(2,1)S(1)} %get-tuple-element.36.refs_1_, ...), custom_call_target="tpu_custom_call", output_to_operand_aliasing={{0}: (13, {}), {1}: (14, {}), {2}: (15, {})} | custom-call | flops 4000000000 | bytes 6000000 | tf_op jit(solution)/shard_map/mix/pallas_call | solution.py:311
  89.4 3.0 %collective-permute-done.3 = bf16[144,1024]{1,0:T(8,128)(2,1)S(1)} collective-permute-done((bf16[144,1024]{1,0:T(8,128)(2,1)S(1)}, bf16[144,1024]{1,0:T(8,128)(2,1)S(1)}, u32[]{:S(2)}, u32[]{:S(2)}) %collective-permute-start.3) | collective-permute-done | bytes 294944 | tf_op jit(solution)/shard_map/ppermute | solution.py:516
  92.7 3.3 %collective-permute-start.4 = (bf16[128,1024]{1,0:T(8,128)(2,1)S(1)}, bf16[128,1024]{1,0:T(8,128)(2,1)S(1)}, u32[]{:S(2)}, u32[]{:S(2)}) collective-permute-start(bf16[128,1024]{1,0:T(8,128)(2,1)S(1)} %get-tuple-element.75), channel_id=1, source_target_pairs={{0,4},{4,0},{8,12},{12,8},{16,20},{20,16},{24,28},{28,24},{1,5},{5... | collective-permute-start | bytes 786440 | tf_op jit(solution)/shard_map/ppermute | solution.py:520
  96.0 5.1 %mix.7 = (bf16[1024,2048]{1,0:T(8,128)(2,1)}, bf16[1024,2048]{1,0:T(8,128)(2,1)}, bf16[1024,256]{1,0:T(8,128)(2,1)S(1)}) custom-call(bf16[1024,2048]{1,0:T(8,128)(2,1)} %get-tuple-element.35.refs_0_, bf16[1024,256]{1,0:T(8,128)(2,1)S(1)} %get-tuple-element.36.refs_1_, ...), custom_call_target="tpu_custom_call", output_to_operand_aliasing={{0}: (13, {}), {1}: (14, {}), {2}: (15, {})} | custom-call | flops 4000000000 | bytes 6000000 | tf_op jit(solution)/shard_map/mix/pallas_call | solution.py:311
  101.1 3.6 %collective-permute-done.4.got_ref = bf16[128,1024]{1,0:T(8,128)(2,1)S(1)} collective-permute-done((bf16[128,1024]{1,0:T(8,128)(2,1)S(1)}, bf16[128,1024]{1,0:T(8,128)(2,1)S(1)}, u32[]{:S(2)}, u32[]{:S(2)}) %collective-permute-start.4) | collective-permute-done | bytes 262176 | tf_op jit(solution)/shard_map/ppermute | solution.py:520
  104.8 5.7 %finish_norm.1.y_ref = bf16[1024,2048]{1,0:T(8,128)(2,1)S(1)} custom-call(s32[1]{0:T(128)} %bitcast.2.parity_ref, bf16[1024,2048]{1,0:T(8,128)(2,1)} %get-tuple-element.50.part_ref, bf16[1024,2048]{1,0:T(8,128)(2,1)} %get-tuple-element.51.scale_ref, bf16[1024,256]{1,0:T(8,128)(2,1)S(1)} %get-tuple-element.52.cc_ref, ...), custom_call_target="tpu_custom_call" | custom-call | flops 2000000000 | bytes 13000000 | tf_op jit(solution)/shard_map/finish_norm/pallas_call | solution.py:374
  110.5 7.1 %project.9 = (bf16[1024,256]{1,0:T(8,128)(2,1)}, bf16[1024,256]{1,0:T(8,128)(2,1)S(1)}) custom-call(s32[2]{0:T(128)S(1)} %pad_add_fusion.4.places_ref, bf16[1024,2048]{1,0:T(8,128)(2,1)S(1)} %finish_norm.1.y_ref, bf16[2048,4096]{1,0:T(8,128)(2,1)} %w_ref.9), custom_call_target="tpu_custom_call" | custom-call | flops 2147483648 | bytes 6291456 | tf_op jit(solution)/shard_map/project/pallas_call | solution.py:416
  117.5 0.8 copy-done.7
  118.3 6.2 %project.8 = (bf16[1024,256]{1,0:T(8,128)(2,1)}, bf16[1024,256]{1,0:T(8,128)(2,1)S(1)}) custom-call(s32[2]{0:T(128)S(1)} %pad_add_fusion.3.places_ref, bf16[1024,2048]{1,0:T(8,128)(2,1)S(1)} %finish_norm.1.y_ref, bf16[2048,4096]{1,0:T(8,128)(2,1)} %w_ref.9), custom_call_target="tpu_custom_call" | custom-call | flops 2147483648 | bytes 6291456 | tf_op jit(solution)/shard_map/project/pallas_call | solution.py:416
  124.5 0.5 collective-permute-start.13
  125.1 6.4 %project.7 = (bf16[1024,256]{1,0:T(8,128)(2,1)}, bf16[1024,256]{1,0:T(8,128)(2,1)S(1)}) custom-call(s32[2]{0:T(128)S(1)} %pad_add_fusion.2.places_ref, bf16[1024,2048]{1,0:T(8,128)(2,1)S(1)} %finish_norm.1.y_ref, bf16[2048,4096]{1,0:T(8,128)(2,1)} %w_ref.9), custom_call_target="tpu_custom_call" | custom-call | flops 2147483648 | bytes 6291456 | tf_op jit(solution)/shard_map/project/pallas_call | solution.py:416
  131.5 6.2 %project.6 = (bf16[1024,256]{1,0:T(8,128)(2,1)}, bf16[1024,256]{1,0:T(8,128)(2,1)S(1)}) custom-call(s32[2]{0:T(128)S(1)} %pad_add_fusion.1.places_ref, bf16[1024,2048]{1,0:T(8,128)(2,1)S(1)} %finish_norm.1.y_ref, bf16[2048,4096]{1,0:T(8,128)(2,1)} %w_ref.9), custom_call_target="tpu_custom_call" | custom-call | flops 2147483648 | bytes 6291456 | tf_op jit(solution)/shard_map/project/pallas_call | solution.py:416
  137.7 0.5 collective-permute-start.9
  138.2 15.5 %project.5 = (bf16[1024,1024]{1,0:T(8,128)(2,1)}, bf16[1024,1024]{1,0:T(8,128)(2,1)S(1)}) custom-call(s32[2]{0:T(128)S(1)} %pad_add_fusion.places_ref, bf16[1024,2048]{1,0:T(8,128)(2,1)} %copy-done.2, bf16[2048,4096]{1,0:T(8,128)(2,1)} %w_ref.9), custom_call_target="tpu_custom_call" | custom-call | flops 8589934592 | bytes 12582912 | tf_op jit(solution)/shard_map/project/pallas_call | solution.py:416
  153.7 1.1 reduce-scatter.2.cloned.1.call-done
  154.8 1.2 slice.65
  156.0 8.6 %collective-permute-start.6 = (bf16[1,1536,128]{2,1,0:T(8,128)(2,1)S(1)}, bf16[1,1536,128]{2,1,0:T(8,128)(2,1)S(1)}, u32[]{:S(2)}, u32[]{:S(2)}) collective-permute-start(bf16[1,1536,128]{2,1,0:T(8,128)(2,1)S(1)} %slice.65), channel_id=1, source_target_pairs={{0,4},{4,8},{8,12},{12,16},{16,20},{20,24},{24,28},{1,5},{5,9},{9,... | collective-permute-start | bytes 1179656 | tf_op jit(solution)/shard_map/ppermute | solution.py:516
  164.6 1.3 add_convert_fusion
  165.9 2.2 collective-permute-start.16
  168.2 1.3 add_convert_fusion.1
  169.5 4.1 %collective-permute-done.6 = bf16[1,1536,128]{2,1,0:T(8,128)(2,1)S(1)} collective-permute-done((bf16[1,1536,128]{2,1,0:T(8,128)(2,1)S(1)}, bf16[1,1536,128]{2,1,0:T(8,128)(2,1)S(1)}, u32[]{:S(2)}, u32[]{:S(2)}) %collective-permute-start.6) | collective-permute-done | bytes 393248 | tf_op jit(solution)/shard_map/ppermute | solution.py:516
  173.6 2.2 collective-permute-start.14
  175.8 1.2 constant_dynamic-update-slice_fusion.panel_ref
  177.0 4.0 %low_part.1 = f32[512,128]{1,0:T(8,128)S(1)} custom-call(s32[8]{0:T(128)S(1)} %fusion.9.slot_ref, bf16[1024,2048]{1,0:T(8,128)(2,1)S(1)} %copy-done.3, bf16[3,1536,128]{2,1,0:T(8,128)(2,1)S(1)} %constant_dynamic-update-slice_fusion.panel_ref), custom_call_target="tpu_custom_call" | custom-call | flops 1000000000 | bytes 6000000 | tf_op jit(solution)/shard_map/low_part/pallas_call | solution.py:448
  181.2 1.2 add_convert_fusion.2
  182.4 0.3 collective-permute-done.7
  182.8 2.1 collective-permute-start.8
  184.9 1.2 add_convert_fusion.3
  186.0 19.7 %collective-permute-done.8 = bf16[512,128]{1,0:T(8,128)(2,1)S(1)} collective-permute-done((bf16[512,128]{1,0:T(8,128)(2,1)S(1)}, bf16[512,128]{1,0:T(8,128)(2,1)S(1)}, u32[]{:S(2)}, u32[]{:S(2)}) %collective-permute-start.8) | collective-permute-done | bytes 131104 | tf_op jit(solution)/shard_map/ppermute | solution.py:520
  205.7 1.7 collective-permute-start.10
  207.5 11.8 %collective-permute-done.10.refs_0_ = bf16[1024,256]{1,0:T(8,128)(2,1)S(1)} collective-permute-done((bf16[1024,256]{1,0:T(8,128)(2,1)S(1)}, bf16[1024,256]{1,0:T(8,128)(2,1)S(1)}, u32[]{:S(2)}, u32[]{:S(2)}) %collective-permute-start.10) | collective-permute-done | bytes 524320 | tf_op jit(solution)/shard_map/ppermute | solution.py:520
  219.3 7.3 %final_sum.1 = bf16[1024,1024]{1,0:T(8,128)(2,1)} custom-call(s32[8]{0:T(128)S(1)} %fusion.9.slot_ref, bf16[1024,1024]{1,0:T(8,128)(2,1)S(1)} %get-tuple-element.55.own_ref, bf16[1024,1024]{1,0:T(8,128)(2,1)} %collective-permute-done.5.pair_ref, f32[512,128]{1,0:T(8,128)S(1)} %convert_add_fusion.1.low_ref, ...), custom_call_target="tpu_custom_call" | custom-call | flops 100000000 | bytes 10000000 | tf_op jit(solution)/shard_map/final_sum/pallas_call | solution.py:492
  (86 shorter events, 2.3 us)
Async XLA Ops:
  6.5 3.9 %copy-start = (s32[48]{0:T(128)S(1)}, s32[48]{0:T(128)}, u32[]{:S(2)}) copy-start(s32[48]{0:T(128)} %param.33) | copy-start | bytes 580
  6.5 4.5 %copy-start.14 = (s32[16]{0:T(128)S(1)}, s32[16]{0:T(128)}, u32[]{:S(2)}) copy-start(s32[16]{0:T(128)} %param.32) | copy-start | bytes 196
  6.5 148.2 %reduce-scatter.2.cloned.1.call-start = ((), (), s32[]{:S(2)}) async-start(), calls=%async_computation.1 | async-start | bytes 7077888 | tf_op jit(solution)/shard_map/reduce_scatter | solution.py:574
  11.1 1.1 copy-start.5
  19.7 0.7 slice-start
  19.7 0.7 slice-start.1
  19.7 0.9 slice-start.2
  19.7 4.1 %copy-start.15 = (f32[32]{0:T(128)S(1)}, f32[32]{0:T(128)}, u32[]{:S(2)}) copy-start(f32[32]{0:T(128)} %param.22) | copy-start | bytes 388
  19.7 4.2 %copy-start.16 = (f32[32]{0:T(128)S(1)}, f32[32]{0:T(128)}, u32[]{:S(2)}) copy-start(f32[32]{0:T(128)} %param.23) | copy-start | bytes 388
  19.7 4.3 %copy-start.13 = (bf16[2048]{0:T(1024)(128)(2,1)S(1)}, bf16[2048]{0:T(1024)(128)(2,1)}, u32[]{:S(2)}) copy-start(bf16[2048]{0:T(1024)(128)(2,1)} %param.27) | copy-start | bytes 12292
  19.7 4.4 %copy-start.17 = (s32[16]{0:T(128)S(1)}, s32[16]{0:T(128)}, u32[]{:S(2)}) copy-start(s32[16]{0:T(128)} %param.31) | copy-start | bytes 196
  19.7 7.2 %copy-start.9 = (bf16[1024,256]{1,0:T(8,128)(2,1)S(1)}, bf16[1024,256]{1,0:T(8,128)(2,1)}, u32[]{:S(2)}) copy-start(bf16[1024,256]{1,0:T(8,128)(2,1)} %b_ref.1) | copy-start | bytes 1572868
  19.8 7.2 %copy-start.10 = (f32[32,1024]{1,0:T(8,128)S(1)}, f32[32,1024]{1,0:T(8,128)}, u32[]{:S(2)}) copy-start(f32[32,1024]{1,0:T(8,128)} %raw_ref.1) | copy-start | bytes 393220
  19.8 7.1 %copy-start.11 = (bf16[4,2048]{1,0:T(4,128)(2,1)S(1)}, bf16[4,2048]{1,0:T(4,128)(2,1)}, u32[]{:S(2)}) copy-start(bf16[4,2048]{1,0:T(4,128)(2,1)} %xt_ref.1) | copy-start | bytes 49156
  19.8 7.1 %copy-start.12 = (bf16[4,256]{1,0:T(4,128)(2,1)S(1)}, bf16[4,256]{1,0:T(4,128)(2,1)}, u32[]{:S(2)}) copy-start(bf16[4,256]{1,0:T(4,128)(2,1)} %bt_ref.1) | copy-start | bytes 6148
  20.6 6.3 %collective-permute-start = (bf16[16,2560]{1,0:T(8,128)(2,1)S(1)}, bf16[16,2560]{1,0:T(8,128)(2,1)S(1)}, u32[]{:S(2)}, u32[]{:S(2)}) collective-permute-start(bf16[16,2560]{1,0:T(8,128)(2,1)S(1)} %pad_maximum_fusion), channel_id=1, source_target_pairs={{0,4},{4,8},{8,12},{12,16},{16,20},{20,24},{24,28},{1,5},{5,9},{9,... | collective-permute-start | bytes 245768 | tf_op jit(solution)/shard_map/ppermute | solution.py:516
  26.9 20.2 %copy-start.4 = (bf16[1024,256]{1,0:T(8,128)(2,1)S(1)}, bf16[1024,256]{1,0:T(8,128)(2,1)}, u32[]{:S(2)}) copy-start(bf16[1024,256]{1,0:T(8,128)(2,1)} %refs_3_.7) | copy-start | bytes 1572868
  26.9 20.2 %copy-start.8 = (bf16[4,256]{1,0:T(4,128)(2,1)S(1)}, bf16[4,256]{1,0:T(4,128)(2,1)}, u32[]{:S(2)}) copy-start(bf16[4,256]{1,0:T(4,128)(2,1)} %refs_11_.7) | copy-start | bytes 6148
  45.6 11.4 %collective-permute-start.1 = (bf16[144,1024]{1,0:T(8,128)(2,1)S(1)}, bf16[144,1024]{1,0:T(8,128)(2,1)S(1)}, u32[]{:S(2)}, u32[]{:S(2)}) collective-permute-start(bf16[144,1024]{1,0:T(8,128)(2,1)S(1)} %get-tuple-element.53), channel_id=1, source_target_pairs={{0,4},{4,0},{8,12},{12,8},{16,20},{20,16},{24,28},{28,24},{1,5},{5... | collective-permute-start | bytes 884744 | tf_op jit(solution)/shard_map/ppermute | solution.py:520
  57.3 25.3 %collective-permute-start.2 = (bf16[144,1024]{1,0:T(8,128)(2,1)S(1)}, bf16[144,1024]{1,0:T(8,128)(2,1)S(1)}, u32[]{:S(2)}, u32[]{:S(2)}) collective-permute-start(bf16[144,1024]{1,0:T(8,128)(2,1)S(1)} %maximum_maximum_fusion), channel_id=1, source_target_pairs={{0,8},{4,12},{8,16},{12,20},{16,24},{20,28},{1,9},{5,13},{9,17},{1... | collective-permute-start | bytes 884744 | tf_op jit(solution)/shard_map/ppermute | solution.py:516
  82.8 9.6 %collective-permute-start.3 = (bf16[144,1024]{1,0:T(8,128)(2,1)S(1)}, bf16[144,1024]{1,0:T(8,128)(2,1)S(1)}, u32[]{:S(2)}, u32[]{:S(2)}) collective-permute-start(bf16[144,1024]{1,0:T(8,128)(2,1)S(1)} %maximum_maximum_fusion.1), channel_id=1, source_target_pairs={{0,16},{4,20},{8,24},{12,28},{1,17},{5,21},{9,25},{13,29},{2,18},{... | collective-permute-start | bytes 884744 | tf_op jit(solution)/shard_map/ppermute | solution.py:516
  92.7 12.1 %collective-permute-start.4 = (bf16[128,1024]{1,0:T(8,128)(2,1)S(1)}, bf16[128,1024]{1,0:T(8,128)(2,1)S(1)}, u32[]{:S(2)}, u32[]{:S(2)}) collective-permute-start(bf16[128,1024]{1,0:T(8,128)(2,1)S(1)} %get-tuple-element.75), channel_id=1, source_target_pairs={{0,4},{4,0},{8,12},{12,8},{16,20},{20,16},{24,28},{28,24},{1,5},{5... | collective-permute-start | bytes 786440 | tf_op jit(solution)/shard_map/ppermute | solution.py:520
  110.5 21.0 %copy-start.2 = (bf16[1024,2048]{1,0:T(8,128)(2,1)}, bf16[1024,2048]{1,0:T(8,128)(2,1)S(1)}, u32[]{:S(2)}) copy-start(bf16[1024,2048]{1,0:T(8,128)(2,1)S(1)} %finish_norm.1.y_ref) | copy-start | bytes 12582916
  117.5 0.8 copy-start.7
  118.3 37.6 %collective-permute-start.15 = (bf16[1024,256]{1,0:T(8,128)(2,1)}, bf16[1024,256]{1,0:T(8,128)(2,1)}, u32[]{:S(2)}, u32[]{:S(2)}) collective-permute-start(bf16[1024,256]{1,0:T(8,128)(2,1)} %get-tuple-element.64), channel_id=1, source_target_pairs={{0,1},{1,0},{2,3},{3,2},{4,5},{5,4},{6,7},{7,6},{8,9},{9,8},{10,11... | collective-permute-start | bytes 1572872 | tf_op jit(solution)/shard_map/ppermute | solution.py:520
  124.5 6.9 %copy-start.6 = (bf16[1024,256]{1,0:T(8,128)(2,1)}, bf16[1024,256]{1,0:T(8,128)(2,1)S(1)}, u32[]{:S(2)}) copy-start(bf16[1024,256]{1,0:T(8,128)(2,1)S(1)} %get-tuple-element.61) | copy-start | bytes 1572868
  124.5 41.4 %collective-permute-start.13 = (bf16[1024,256]{1,0:T(8,128)(2,1)}, bf16[1024,256]{1,0:T(8,128)(2,1)}, u32[]{:S(2)}, u32[]{:S(2)}) collective-permute-start(bf16[1024,256]{1,0:T(8,128)(2,1)} %get-tuple-element.62), channel_id=1, source_target_pairs={{0,1},{1,0},{2,3},{3,2},{4,5},{5,4},{6,7},{7,6},{8,9},{9,8},{10,11... | collective-permute-start | bytes 1572872 | tf_op jit(solution)/shard_map/ppermute | solution.py:520
  131.5 49.6 %collective-permute-start.11 = (bf16[1024,256]{1,0:T(8,128)(2,1)}, bf16[1024,256]{1,0:T(8,128)(2,1)}, u32[]{:S(2)}, u32[]{:S(2)}) collective-permute-start(bf16[1024,256]{1,0:T(8,128)(2,1)} %get-tuple-element.60), channel_id=1, source_target_pairs={{0,1},{1,0},{2,3},{3,2},{4,5},{5,4},{6,7},{7,6},{8,9},{9,8},{10,11... | collective-permute-start | bytes 1572872 | tf_op jit(solution)/shard_map/ppermute | solution.py:520
  137.7 45.1 %collective-permute-start.9 = (bf16[1024,256]{1,0:T(8,128)(2,1)}, bf16[1024,256]{1,0:T(8,128)(2,1)}, u32[]{:S(2)}, u32[]{:S(2)}) collective-permute-start(bf16[1024,256]{1,0:T(8,128)(2,1)} %get-tuple-element.58), channel_id=1, source_target_pairs={{0,1},{1,0},{2,3},{3,2},{4,5},{5,4},{6,7},{7,6},{8,9},{9,8},{10,11... | collective-permute-start | bytes 1572872 | tf_op jit(solution)/shard_map/ppermute | solution.py:520
  153.6 65.7 %collective-permute-start.5 = (bf16[1024,1024]{1,0:T(8,128)(2,1)}, bf16[1024,1024]{1,0:T(8,128)(2,1)}, u32[]{:S(2)}, u32[]{:S(2)}) collective-permute-start(bf16[1024,1024]{1,0:T(8,128)(2,1)} %get-tuple-element.56), channel_id=1, source_target_pairs={{0,1},{1,0},{2,3},{3,2},{4,5},{5,4},{6,7},{7,6},{8,9},{9,8},{10,11... | collective-permute-start | bytes 6291464 | tf_op jit(solution)/shard_map/ppermute | solution.py:520
  154.8 22.3 %copy-start.3 = (bf16[1024,2048]{1,0:T(8,128)(2,1)S(1)}, bf16[1024,2048]{1,0:T(8,128)(2,1)}, u32[]{:S(2)}) copy-start(bf16[1024,2048]{1,0:T(8,128)(2,1)} %copy-done.2) | copy-start | bytes 12582916
  156.0 17.6 %collective-permute-start.6 = (bf16[1,1536,128]{2,1,0:T(8,128)(2,1)S(1)}, bf16[1,1536,128]{2,1,0:T(8,128)(2,1)S(1)}, u32[]{:S(2)}, u32[]{:S(2)}) collective-permute-start(bf16[1,1536,128]{2,1,0:T(8,128)(2,1)S(1)} %slice.65), channel_id=1, source_target_pairs={{0,4},{4,8},{8,12},{12,16},{16,20},{20,24},{24,28},{1,5},{5,9},{9,... | collective-permute-start | bytes 1179656 | tf_op jit(solution)/shard_map/ppermute | solution.py:516
  165.9 41.6 %collective-permute-start.16 = (bf16[1024,256]{1,0:T(8,128)(2,1)S(1)}, bf16[1024,256]{1,0:T(8,128)(2,1)S(1)}, u32[]{:S(2)}, u32[]{:S(2)}) collective-permute-start(bf16[1024,256]{1,0:T(8,128)(2,1)S(1)} %add_convert_fusion), channel_id=1, source_target_pairs={{0,2},{1,3},{2,0},{3,1},{4,6},{5,7},{6,4},{7,5},{8,10},{9,11},{10,... | collective-permute-start | bytes 1572872 | tf_op jit(solution)/shard_map/ppermute | solution.py:520
  173.6 33.9 %collective-permute-start.14 = (bf16[1024,256]{1,0:T(8,128)(2,1)S(1)}, bf16[1024,256]{1,0:T(8,128)(2,1)S(1)}, u32[]{:S(2)}, u32[]{:S(2)}) collective-permute-start(bf16[1024,256]{1,0:T(8,128)(2,1)S(1)} %add_convert_fusion.1), channel_id=1, source_target_pairs={{0,2},{1,3},{2,0},{3,1},{4,6},{5,7},{6,4},{7,5},{8,10},{9,11},{10,... | collective-permute-start | bytes 1572872 | tf_op jit(solution)/shard_map/ppermute | solution.py:520
  181.1 1.6 collective-permute-start.7
  182.7 24.8 %collective-permute-start.12 = (bf16[1024,256]{1,0:T(8,128)(2,1)S(1)}, bf16[1024,256]{1,0:T(8,128)(2,1)S(1)}, u32[]{:S(2)}, u32[]{:S(2)}) collective-permute-start(bf16[1024,256]{1,0:T(8,128)(2,1)S(1)} %add_convert_fusion.2), channel_id=1, source_target_pairs={{0,2},{1,3},{2,0},{3,1},{4,6},{5,7},{6,4},{7,5},{8,10},{9,11},{10,... | collective-permute-start | bytes 1572872 | tf_op jit(solution)/shard_map/ppermute | solution.py:520
  182.8 23.0 %collective-permute-start.8 = (bf16[512,128]{1,0:T(8,128)(2,1)S(1)}, bf16[512,128]{1,0:T(8,128)(2,1)S(1)}, u32[]{:S(2)}, u32[]{:S(2)}) collective-permute-start(bf16[512,128]{1,0:T(8,128)(2,1)S(1)} %get-tuple-element.65), channel_id=1, source_target_pairs={{0,2},{1,3},{2,0},{3,1},{4,6},{5,7},{6,4},{7,5},{8,10},{9,11},{10,... | collective-permute-start | bytes 393224 | tf_op jit(solution)/shard_map/ppermute | solution.py:520
  205.7 13.5 %collective-permute-start.10 = (bf16[1024,256]{1,0:T(8,128)(2,1)S(1)}, bf16[1024,256]{1,0:T(8,128)(2,1)S(1)}, u32[]{:S(2)}, u32[]{:S(2)}) collective-permute-start(bf16[1024,256]{1,0:T(8,128)(2,1)S(1)} %add_convert_fusion.3), channel_id=1, source_target_pairs={{0,2},{1,3},{2,0},{3,1},{4,6},{5,7},{6,4},{7,5},{8,10},{9,11},{10,... | collective-permute-start | bytes 1572872 | tf_op jit(solution)/shard_map/ppermute | solution.py:520
  219.3 7.3 %copy-start.1 = (s32[48]{0:T(128)S(1)}, s32[48]{0:T(128)}, u32[]{:S(2)}) copy-start(s32[48]{0:T(128)} %param.33) | copy-start | bytes 580
Sparse Core Ops, SparseCore 0:
  19.9 134.7 reduce-scatter.1

commit v2 on v1

v2 whole, which is shorter than its diff:
```python
import functools

import jax
import jax.numpy as jnp
from jax import lax
from jax.experimental import pallas as pl
from jax.experimental.pallas import tpu as pltpu
from jax.sharding import PartitionSpec as P

P_SIZE = 64
N = 128
K = 4
Q = 128
TURN_DEV = 2
HALO = 16
LANES = 128
PIECES = 4
Y_UNITS = 4
Y_FIRST = 2

F32 = jnp.float32
BF16 = jnp.bfloat16
epsilon = 1e-05
MIB = 1024 * 1024


def params(mib=28):
    return pltpu.CompilerParams(vmem_limit_bytes=mib * MIB)


def cost(microseconds):
    return pl.CostEstimate(flops=int(microseconds * 1e5), bytes_accessed=1, transcendentals=0)


def silu(v):
    half = 0.5 * v
    return half + half * jnp.tanh(half)


def conv_rows(current, previous, taps):
    rows = current.shape[0]
    joined = jnp.concatenate([previous, current], axis=0)
    total = taps[K - 1 : K] * current
    for back in range(1, K):
        total = total + taps[K - 1 - back : K - back] * pltpu.roll(joined, back, 0)[8 : 8 + rows]
    return silu(total).astype(BF16)


def two_terms(v):
    high = v.astype(BF16).astype(F32)
    return high, v - high


def column_of(row):
    size = row.shape[1]
    here = lax.broadcasted_iota(jnp.int32, (size, size), 0)
    there = lax.broadcasted_iota(jnp.int32, (size, size), 1)
    return jnp.sum(jnp.where(here == there, row, 0.0), axis=1, keepdims=True)


def pad_rows(stack):
    rows = stack.shape[0]
    if rows % LANES:
        fill = jnp.zeros((LANES - rows % LANES, stack.shape[1]), F32)
        stack = jnp.concatenate([stack, fill], axis=0)
    return stack


def edge_kernel(x_ref, b_ref, c_ref, out_ref):
    place = 0
    for ref in (x_ref, b_ref, c_ref):
        out_ref[:, place : place + ref.shape[1]] = ref[...]
        place += ref.shape[1]


def sequence_edge(*arrays):
    tokens = arrays[0].shape[0]
    width = sum(array.shape[1] for array in arrays)
    return pl.pallas_call(
        edge_kernel,
        grid=(1,),
        in_specs=[
            pl.BlockSpec((HALO, array.shape[1]), lambda i: (tokens // HALO - 1, 0)) for array in arrays
        ],
        out_specs=pl.BlockSpec((HALO, width), lambda i: (0, 0)),
        out_shape=jax.ShapeDtypeStruct((HALO, width), BF16),
        compiler_params=params(62),
        cost_estimate=cost(1),
        name="sequence_edge",
    )(*arrays)


def turn_home(place, bits, slot, count, panel_index, tenants, me):
    relative = 0
    for order, bit in enumerate(bits):
        relative = relative + bit * (1 - (place >> (len(bits) - 1 - order)) % 2)
    panel = panel_index[tenants[TURN_DEV * (relative ^ me) + slot]]
    owned = lax.div(panel, count) == me
    return jnp.where(owned, lax.rem(panel, count), 0), owned


def place_panel(in_ref, out_ref, first, owned):
    rows = slice(first, first + in_ref.shape[1])

    @pl.when(owned)
    def _():
        out_ref[0, rows, :] = in_ref[0]

    @pl.when(jnp.logical_not(owned))
    def _():
        out_ref[0, rows, :] = jnp.zeros_like(in_ref[0])


def panel_kernel(homes, index_ref, tenant_ref, me_ref, *refs):
    place = pl.program_id(0)
    half = pl.num_programs(0) // 2
    ins = list(refs[: sum(len(job) for job in homes)])
    outs = refs[len(ins) :]
    for number, job in enumerate(homes):
        send_ref, keep_ref = outs[2 * number : 2 * number + 2]
        for slot, home in enumerate(job):
            in_ref = ins.pop(0)
            owned = home(place, index_ref, tenant_ref, me_ref[0])[1]
            first = slot * in_ref.shape[1]

            @pl.when(place < half)
            def _(in_ref=in_ref, send_ref=send_ref, owned=owned, first=first):
                place_panel(in_ref, send_ref, first, owned)

            @pl.when(place >= half)
            def _(in_ref=in_ref, keep_ref=keep_ref, owned=owned, first=first):
                place_panel(in_ref, keep_ref, first, owned)


def pack_panels(jobs, panel_index, tenants, me, devices):
    half = devices // 2
    homes, ins, in_specs, out_specs, out_shape = [], [], [], [], []
    for panels, bits, slots in jobs:
        count, rows, width = panels.shape
        homes.append([])
        for slot in slots:

            def home(place, index, tenant, own, bits=bits, slot=slot, count=count):
                return turn_home(place, bits, slot, count, index, tenant, own)

            def at(q, index, tenant, own, home=home):
                return (home(q, index, tenant, own[0])[0], 0, 0)

            homes[-1].append(home)
            ins.append(panels)
            in_specs.append(pl.BlockSpec((1, rows, width), at))
        block = (1, len(slots) * rows, width)
        out_specs.append(pl.BlockSpec(block, lambda q, index, tenant, own: (jnp.minimum(q, half - 1), 0, 0)))
        out_specs.append(pl.BlockSpec(block, lambda q, index, tenant, own: (jnp.maximum(q - half, 0), 0, 0)))
        out_shape += [jax.ShapeDtypeStruct((half,) + block[1:], BF16)] * 2
    outs = pl.pallas_call(
        functools.partial(panel_kernel, homes),
        grid_spec=pltpu.PrefetchScalarGridSpec(
            num_scalar_prefetch=3, grid=(devices,), in_specs=in_specs, out_specs=out_specs
        ),
        out_shape=out_shape,
        compiler_params=params(62),
        cost_estimate=cost(5),
        name="pack_panels",
    )(panel_index, tenants, me, *ins)
    return [outs[2 * job : 2 * job + 2] for job in range(len(jobs))]


def state_kernel(
    parity_ref, x_ref, b_ref, even_ref, odd_ref, raw_ref, rate_ref, xt_ref, bt_ref, spread_ref,
    xc_ref, bc_ref, run_ref, shifted_ref, before_ref, start_ref, keep_ref, send_ref,
    x_prev, b_prev, weight, x_weighted, state, decay_product,
):
    block = pl.program_id(0)
    inner = x_ref.shape[1]
    bc_width = b_ref.shape[1]
    groups = bc_width // N
    width = inner // groups

    @pl.when(block == 0)
    def _():
        halo = jnp.where(parity_ref[0] == 1, even_ref[...], odd_ref[...])
        x_prev[...] = halo[:, :inner].astype(F32)[8:]
        b_prev[...] = halo[:, inner : inner + bc_width].astype(F32)[8:]
        state[...] = jnp.zeros_like(state)
        decay_product[...] = jnp.ones_like(decay_product)

    raw = raw_ref[...]
    step = jnp.maximum(raw, 0.0) + jnp.log1p(jnp.exp(-jnp.abs(raw)))
    change = -step * jnp.exp(column_of(rate_ref[...]))
    heads = raw.shape[0]
    first = change.astype(BF16)
    rest = change - first.astype(F32)
    second = rest.astype(BF16)
    third = (rest - second.astype(F32)).astype(BF16)
    upper = (
        lax.broadcasted_iota(jnp.int32, (Q, Q), 0) <= lax.broadcasted_iota(jnp.int32, (Q, Q), 1)
    ).astype(F32).astype(BF16)
    sums = jnp.dot(jnp.concatenate([first, second, third], axis=0), upper, preferred_element_type=F32)
    run = sums[:heads] + sums[heads : 2 * heads] + sums[2 * heads :]
    run_ref[...] = run
    shifted_ref[...] = jnp.log(step) - run
    last = run[:, Q - 1 : Q]
    tail = jnp.exp(last - run) * step
    whole = jnp.broadcast_to(jnp.exp(last), (heads, Q))
    columns = pad_rows(jnp.concatenate([*two_terms(tail), *two_terms(whole)], axis=0)).T
    spread = spread_ref[...]
    weight[...] = jnp.dot(columns[:, : 2 * heads].astype(BF16), spread, preferred_element_type=F32)
    decay_row = jnp.dot(
        columns[:16, 2 * heads : 4 * heads].astype(BF16), spread, preferred_element_type=F32
    )[:8]

    bc = conv_rows(b_ref[...].astype(F32), b_prev[...], bt_ref[...].astype(F32))
    b_prev[...] = b_ref[Q - HALO :, :].astype(F32)[8:]
    bc_ref[...] = bc

    def conv_lanes(part, carried):
        lanes = pl.ds(pl.multiple_of(part * LANES, LANES), LANES)
        current = x_ref[:, lanes].astype(F32)
        xc = conv_rows(current, x_prev[:, lanes], xt_ref[:, lanes].astype(F32))
        x_prev[:, lanes] = current[Q - 8 :]
        xc_ref[:, lanes] = xc
        x_weighted[:, lanes] = (xc.astype(F32) * weight[:, lanes]).astype(BF16)
        return carried

    lax.fori_loop(0, inner // LANES, conv_lanes, 0, unroll=16)

    start_ref[...] = decay_product[...]
    decay_product[...] = decay_product[...] * decay_row
    for group in range(groups):
        lanes = slice(group * width, (group + 1) * width)
        fresh = lax.dot_general(
            bc[:, group * N : (group + 1) * N],
            x_weighted[:, lanes],
            (((0,), (0,)), ((), ())),
            preferred_element_type=F32,
        )
        held = state[:, lanes]
        before_ref[:, lanes] = held.astype(BF16)
        state[:, lanes] = held * decay_row[:1, lanes] + fresh

    @pl.when(block == pl.num_programs(0) - 1)
    def _():
        half = inner // 2
        row = lax.broadcasted_iota(jnp.int32, (HALO, half), 0)
        for out_ref, place in ((keep_ref, parity_ref[0]), (send_ref, 1 - parity_ref[0])):
            lanes = pl.ds(pl.multiple_of(place * half, LANES), half)
            out_ref[:N] = state[:, lanes].astype(BF16)
            high, low = two_terms(decay_product[:1, lanes])
            out_ref[N:] = jnp.where(row == 0, high, jnp.where(row == 1, low, 0.0)).astype(BF16)


def local_states(parity, x, b, halos, raw, rate, x_taps, b_taps, spread):
    tokens, inner = x.shape
    bc_width = b.shape[1]
    heads = raw.shape[0]
    blocks = tokens // Q
    half = inner // 2
    whole = lambda c, p: (0, 0)
    rows = lambda c, p: (c, 0)
    columns = lambda c, p: (0, c)
    return pl.pallas_call(
        state_kernel,
        grid_spec=pltpu.PrefetchScalarGridSpec(
            num_scalar_prefetch=1,
            grid=(blocks,),
            in_specs=[
                pl.BlockSpec((Q, inner), rows),
                pl.BlockSpec((Q, bc_width), rows),
                pl.BlockSpec(halos[0].shape, whole),
                pl.BlockSpec(halos[0].shape, whole),
                pl.BlockSpec((heads, Q), columns),
                pl.BlockSpec((1, heads), whole),
                pl.BlockSpec((K, inner), whole),
                pl.BlockSpec((K, bc_width), whole),
                pl.BlockSpec(spread.shape, whole),
            ],
            out_specs=[
                pl.BlockSpec((Q, inner), rows),
                pl.BlockSpec((Q, bc_width), rows),
                pl.BlockSpec((heads, Q), columns),
                pl.BlockSpec((heads, Q), columns),
                pl.BlockSpec((N, inner), rows),
                pl.BlockSpec((8, inner), rows),
                pl.BlockSpec((N + HALO, half), whole),
                pl.BlockSpec((N + HALO, half), whole),
            ],
            scratch_shapes=[
                pltpu.VMEM((8, inner), F32),
                pltpu.VMEM((8, bc_width), F32),
                pltpu.VMEM((Q, inner), F32),
                pltpu.VMEM((Q, inner), BF16),
                pltpu.VMEM((N, inner), F32),
                pltpu.VMEM((8, inner), F32),
            ],
        ),
        out_shape=[
            jax.ShapeDtypeStruct((tokens, inner), BF16),
            jax.ShapeDtypeStruct((tokens, bc_width), BF16),
            jax.ShapeDtypeStruct((heads, tokens), F32),
            jax.ShapeDtypeStruct((heads, tokens), F32),
            jax.ShapeDtypeStruct((blocks * N, inner), BF16),
            jax.ShapeDtypeStruct((blocks * 8, inner), F32),
            jax.ShapeDtypeStruct((N + HALO, half), BF16),
            jax.ShapeDtypeStruct((N + HALO, half), BF16),
        ],
        compiler_params=params(62),
        cost_estimate=cost(150000),
        name="local_states",
    )(parity, x, b, *halos, raw, rate, x_taps, b_taps, spread)


def mix_kernel(
    first, has_alias, parity_ref, *refs
):
    (
        xc_ref, bc_ref, c_ref, c_prev_ref, even_ref, odd_ref, run_ref, shifted_ref, before_ref, start_ref,
        gate_ref, skip_ref, ct_ref, spread_ref,
    ) = refs[:14]
    refs = refs[14 + (3 if has_alias else 0) :]
    part_ref, scale_ref, cc_ref, rise = refs
    block = pl.program_id(0) + first
    inner = xc_ref.shape[1]
    bc_width = c_ref.shape[1]
    groups = bc_width // N
    width = inner // groups
    heads = run_ref.shape[0]

    at = slice(inner + bc_width, inner + 2 * bc_width)
    c_halo = jnp.where(parity_ref[0] == 1, even_ref[:, at], odd_ref[:, at]).astype(F32)[8:]
    c_before = jnp.where(block == 0, c_halo, c_prev_ref[...].astype(F32)[8:])
    cc = conv_rows(c_ref[...].astype(F32), c_before, ct_ref[...].astype(F32))
    cc_ref[...] = cc
    run = run_ref[...]
    columns = pad_rows(jnp.concatenate([*two_terms(jnp.exp(run)), run], axis=0)).T
    rise[...] = jnp.dot(
        columns[:, : 2 * heads].astype(BF16), spread_ref[...], preferred_element_type=F32
    )
    skips = jnp.broadcast_to(jnp.concatenate(two_terms(skip_ref[...]), axis=1), (16, 2 * heads))
    skip = jnp.dot(skips.astype(BF16), spread_ref[...], preferred_element_type=F32)[:1]
    causal = lax.broadcasted_iota(jnp.int32, (Q, Q), 0) >= lax.broadcasted_iota(jnp.int32, (Q, Q), 1)
    left = lax.broadcasted_iota(jnp.int32, (Q, LANES), 1) < P_SIZE
    for group in range(groups):
        state_lanes = slice(group * N, (group + 1) * N)
        scores = lax.dot_general(
            cc[:, state_lanes],
            bc_ref[:, state_lanes],
            (((1,), (1,)), ((), ())),
            preferred_element_type=F32,
        )
        scores = jnp.where(causal, scores, 0.0)
        for pair in range(width // LANES):
            lanes = slice(group * width + pair * LANES, group * width + (pair + 1) * LANES)
            mixing = []
            for head in (lanes.start // P_SIZE, lanes.start // P_SIZE + 1):
                gap = columns[:, 2 * heads + head : 2 * heads + head + 1] + shifted_ref[head : head + 1, :]
                mixing.append((scores * jnp.exp(jnp.where(causal, gap, 0.0))).astype(BF16))
            x = xc_ref[:, lanes].astype(F32)
            x_pair = jnp.concatenate(
                [jnp.where(left, x, 0.0).astype(BF16), jnp.where(left, 0.0, x).astype(BF16)], axis=0
            )
            y = jnp.dot(jnp.concatenate(mixing, axis=1), x_pair, preferred_element_type=F32)
            carried = jnp.dot(cc[:, state_lanes], before_ref[:, lanes], preferred_element_type=F32)
            rise_part = rise[:, lanes]
            y = y + rise_part * carried + skip[:, lanes] * x
            gate = silu(gate_ref[:, lanes].astype(F32))
            part_ref[:, lanes] = (y * gate).astype(BF16)
            scale_ref[:, lanes] = (gate * rise_part * start_ref[:1, lanes]).astype(BF16)


def mix(
    first, count, parity, xc, bc, c, halos, run, shifted, before, start, gate, skip, c_taps, spread, held
):
    tokens, inner = xc.shape
    bc_width = c.shape[1]
    heads = run.shape[0]
    whole = lambda i, p: (0, 0)
    rows = lambda i, p: (first + i, 0)
    columns = lambda i, p: (0, first + i)
    per_block = Q // HALO
    any_spec = pl.BlockSpec(memory_space=pl.ANY)
    aliased = list(held) if held is not None else []
    return pl.pallas_call(
        functools.partial(mix_kernel, first, bool(aliased)),
        grid_spec=pltpu.PrefetchScalarGridSpec(
            num_scalar_prefetch=1,
            grid=(count,),
            in_specs=[
                pl.BlockSpec((Q, inner), rows),
                pl.BlockSpec((Q, bc_width), rows),
                pl.BlockSpec((Q, bc_width), rows),
                pl.BlockSpec(
                    (HALO, bc_width), lambda i, p: (jnp.maximum((first + i) * per_block - 1, 0), 0)
                ),
                pl.BlockSpec(halos[0].shape, whole),
                pl.BlockSpec(halos[0].shape, whole),
                pl.BlockSpec((heads, Q), columns),
                pl.BlockSpec((heads, Q), columns),
                pl.BlockSpec((N, inner), rows),
                pl.BlockSpec((8, inner), rows),
                pl.BlockSpec((Q, inner), rows),
                pl.BlockSpec((1, heads), whole),
                pl.BlockSpec((K, bc_width), whole),
                pl.BlockSpec(spread.shape, whole),
            ]
            + [any_spec] * len(aliased),
            out_specs=[
                pl.BlockSpec((Q, inner), rows),
                pl.BlockSpec((Q, inner), rows),
                pl.BlockSpec((Q, bc_width), rows),
            ],
            scratch_shapes=[pltpu.VMEM((Q, inner), F32)],
        ),
        out_shape=[
            jax.ShapeDtypeStruct((tokens, inner), BF16),
            jax.ShapeDtypeStruct((tokens, inner), BF16),
            jax.ShapeDtypeStruct((tokens, bc_width), BF16),
        ],
        input_output_aliases={15 + i: i for i in range(len(aliased))},
        compiler_params=params(62),
        cost_estimate=cost(count * 25000),
        name="mix",
    )(parity, xc, bc, c, c, *halos, run, shifted, before, start, gate, skip, c_taps, spread, *aliased)


def project_unit(y_ref, w_ref, send_ref, keep_ref, step, units):
    @pl.when(step < units)
    def _():
        send_ref[...] = jnp.dot(y_ref[...], w_ref[...], preferred_element_type=F32).astype(BF16)

    @pl.when(step >= units)
    def _():
        keep_ref[...] = jnp.dot(y_ref[...], w_ref[...], preferred_element_type=F32).astype(BF16)


def norm_kernel(
    tiles, parity_ref, place_ref, part_ref, scale_ref, cc_ref, keep_state_ref, got_ref, gain_ref, w_ref,
    out_ref, send_ref, keep_ref, state,
):
    inner = part_ref.shape[1]
    groups = cc_ref.shape[1] // N
    width = inner // groups
    half = inner // 2
    step = pl.program_id(0)
    tile = part_ref.shape[0]

    @pl.when(step == 0)
    def _():
        for ref, place in ((keep_state_ref, parity_ref[0]), (got_ref, 1 - parity_ref[0])):
            state[:, pl.ds(pl.multiple_of(place * half, LANES), half)] = ref[...]

    @pl.when(step < tiles)
    def _():
        rows = pl.ds(pl.multiple_of(step * tile, tile), tile)
        for group in range(groups):
            lanes = slice(group * width, (group + 1) * width)
            carried = jnp.dot(
                cc_ref[:, group * N : (group + 1) * N], state[:, lanes], preferred_element_type=F32
            )
            gated = part_ref[:, lanes].astype(F32) + scale_ref[:, lanes].astype(F32) * carried
            mean = jnp.sum(gated * gated, axis=1, keepdims=True) * (1.0 / width)
            normed = gated * lax.rsqrt(mean + epsilon) * gain_ref[:, lanes].astype(F32)
            out_ref[rows, lanes] = normed.astype(BF16)

    @pl.when(step >= tiles)
    def _():
        project_unit(out_ref, w_ref, send_ref, keep_ref, step - tiles, pl.num_programs(0) // 2 - tiles // 2)


def norm_project(parity, head, blocks, part, scale, cc, keep, got, gain, weight, width):
    tokens, inner = part.shape
    tile = 2 * Q
    tiles = tokens // tile
    units = len(blocks) // 2
    place = place_of(blocks)
    whole = lambda i, p, q: (0, 0)
    rows = lambda i, p, q: (jnp.minimum(i, tiles - 1), 0)
    return pl.pallas_call(
        functools.partial(norm_kernel, tiles),
        grid_spec=pltpu.PrefetchScalarGridSpec(
            num_scalar_prefetch=2,
            grid=(tiles + 2 * units,),
            in_specs=[
                pl.BlockSpec((tile, inner), rows),
                pl.BlockSpec((tile, inner), rows),
                pl.BlockSpec((tile, cc.shape[1]), rows),
                pl.BlockSpec(keep.shape, whole),
                pl.BlockSpec(got.shape, whole),
                pl.BlockSpec((1, inner), whole),
                pl.BlockSpec((inner, width), lambda i, p, q: (0, place(jnp.maximum(i - tiles, 0), q[0]))),
            ],
            out_specs=[
                pl.BlockSpec((tokens, inner), whole),
                pl.BlockSpec((tokens, width), lambda i, p, q: (0, jnp.clip(i - tiles, 0, units - 1))),
                pl.BlockSpec((tokens, width), lambda i, p, q: (0, jnp.maximum(i - tiles - units, 0))),
            ],
            scratch_shapes=[pltpu.VMEM((N, inner), BF16)],
        ),
        out_shape=[
            jax.ShapeDtypeStruct((tokens, inner), BF16),
            jax.ShapeDtypeStruct((tokens, units * width), BF16),
            jax.ShapeDtypeStruct((tokens, units * width), BF16),
        ],
        compiler_params=params(62),
        cost_estimate=cost(11),
        name="norm_project",
    )(parity, head, part, scale, cc, keep, got, gain, weight)


def add_kernel(left_ref, right_ref, out_ref):
    out_ref[...] = (left_ref[...].astype(F32) + right_ref[...].astype(F32)).astype(BF16)


def add_columns(left, right, first, count, unit):
    tokens = left.shape[0]
    tile = 512
    spec = pl.BlockSpec((tile, unit), lambda i, j: (i, first + j))
    return pl.pallas_call(
        add_kernel,
        grid=(tokens // tile, count),
        in_specs=[spec, spec],
        out_specs=pl.BlockSpec((tile, unit), lambda i, j: (i, j)),
        out_shape=jax.ShapeDtypeStruct((tokens, count * unit), BF16),
        compiler_params=params(62),
        cost_estimate=cost(1),
        name="add_columns",
    )(left, right)


def place_of(blocks):
    def column(step, head):
        column = (head ^ blocks[0][0]) * Y_UNITS + blocks[0][1]
        for index, (bits, unit) in enumerate(blocks[1:], 1):
            column = jnp.where(step == index, (head ^ bits) * Y_UNITS + unit, column)
        return column

    return column


def project_kernel(apart, head_ref, y_ref, w_ref, *outs):
    step = pl.program_id(0)
    if not apart:
        outs[0][...] = jnp.dot(y_ref[...], w_ref[...], preferred_element_type=F32).astype(BF16)
        return
    for unit, out_ref in enumerate(outs):

        @pl.when(step == unit)
        def _(out_ref=out_ref):
            out_ref[...] = jnp.dot(y_ref[...], w_ref[...], preferred_element_type=F32).astype(BF16)


def project(head, blocks, y, weight, width, apart):
    tokens, inner = y.shape
    units = len(blocks)
    place = place_of(blocks)
    if apart:
        out_specs = [pl.BlockSpec((tokens, width), lambda i, p: (0, 0))] * units
        out_shape = [jax.ShapeDtypeStruct((tokens, width), BF16)] * units
    else:
        out_specs = [pl.BlockSpec((tokens, width), lambda i, p: (0, i))]
        out_shape = [jax.ShapeDtypeStruct((tokens, units * width), BF16)]
    return pl.pallas_call(
        functools.partial(project_kernel, apart),
        grid_spec=pltpu.PrefetchScalarGridSpec(
            num_scalar_prefetch=1,
            grid=(units,),
            in_specs=[
                pl.BlockSpec((tokens, inner), lambda i, p: (0, 0)),
                pl.BlockSpec((inner, width), lambda i, p: (0, place(i, p[0]))),
            ],
            out_specs=out_specs,
        ),
        out_shape=out_shape,
        compiler_params=params(62),
        cost_estimate=cost(1),
        name="project",
    )(head, y, weight)


def both_kernel(units, head_ref, y_ref, w_ref, send_ref, keep_ref):
    project_unit(y_ref, w_ref, send_ref, keep_ref, pl.program_id(0), units)


def project_both(head, blocks, y, weight, width):
    tokens, inner = y.shape
    units = len(blocks) // 2
    place = place_of(blocks)
    return pl.pallas_call(
        functools.partial(both_kernel, units),
        grid_spec=pltpu.PrefetchScalarGridSpec(
            num_scalar_prefetch=1,
            grid=(2 * units,),
            in_specs=[
                pl.BlockSpec((tokens, inner), lambda i, p: (0, 0)),
                pl.BlockSpec((inner, width), lambda i, p: (0, place(i, p[0]))),
            ],
            out_specs=[
                pl.BlockSpec((tokens, width), lambda i, p: (0, jnp.minimum(i, units - 1))),
                pl.BlockSpec((tokens, width), lambda i, p: (0, jnp.maximum(i - units, 0))),
            ],
        ),
        out_shape=[jax.ShapeDtypeStruct((tokens, units * width), BF16)] * 2,
        compiler_params=params(62),
        cost_estimate=cost(1),
        name="project_both",
    )(head, y, weight)


def block_slot(block, starts, me, tokens):
    place = me * tokens + block * Q
    slot = 0
    for turn in range(TURN_DEV):
        slot = slot + (starts[TURN_DEV * me + turn] <= place).astype(jnp.int32)
    return slot


def chosen(slot, refs):
    panel = refs[0][...]
    for index in range(1, len(refs)):
        panel = jnp.where(slot == index, refs[index][...], panel)
    return panel


def low_kernel(tokens, start_ref, me_ref, y_ref, *refs):
    panels, out_ref = refs[:-1], refs[-1]
    slot = block_slot(pl.program_id(0), start_ref, me_ref[0], tokens)
    low = lax.dot_general(
        y_ref[...], chosen(slot, panels), (((1,), (1,)), ((), ())), preferred_element_type=F32
    )
    fold = low.shape[0] // 2
    out_ref[...] = jnp.concatenate([low[:fold], low[fold:]], axis=1)


def low_part(starts, me, y, panels):
    tokens, inner = y.shape
    rows = lambda i, s, m: (i, 0)
    whole = lambda i, s, m: (0, 0)
    return pl.pallas_call(
        functools.partial(low_kernel, tokens),
        grid_spec=pltpu.PrefetchScalarGridSpec(
            num_scalar_prefetch=2,
            grid=(tokens // Q,),
            in_specs=[pl.BlockSpec((Q, inner), rows)]
            + [pl.BlockSpec(panel.shape, whole) for panel in panels],
            out_specs=pl.BlockSpec((Q // 2, LANES), rows),
        ),
        out_shape=jax.ShapeDtypeStruct((tokens // 2, LANES), F32),
        compiler_params=params(),
        cost_estimate=cost(4),
        name="low_part",
    )(starts, me, y, *panels)


def held_kernel(counts, unit, *refs):
    own, pair = refs[:Y_UNITS], refs[Y_UNITS : 2 * Y_UNITS]
    parts, out_ref = list(refs[2 * Y_UNITS : -1]), refs[-1]
    for block in range(Y_UNITS):
        total = own[block][...].astype(F32) + pair[block][...].astype(F32)
        for _ in range(counts[block]):
            total = total + parts.pop(0)[...].astype(F32)
        out_ref[:, block * unit : (block + 1) * unit] = total


def held_sum(own, pair, parts, unit):
    tokens = own.shape[0]
    tile = 2 * Q
    column = lambda at: pl.BlockSpec((tile, unit), lambda i: (i, at))
    here = [[(array, at) for array, at, block in parts if block == unit_at] for unit_at in range(Y_UNITS)]
    return pl.pallas_call(
        functools.partial(held_kernel, [len(each) for each in here], unit),
        grid=(tokens // tile,),
        in_specs=[column(block) for block in range(Y_UNITS)]
        + [column(0)] * Y_UNITS
        + [column(at) for each in here for _, at in each],
        out_specs=pl.BlockSpec((tile, Y_UNITS * unit), lambda i: (i, 0)),
        out_shape=jax.ShapeDtypeStruct((tokens, Y_UNITS * unit), F32),
        compiler_params=params(),
        cost_estimate=cost(3),
        name="held_sum",
    )(*[own] * Y_UNITS, *pair, *[array for each in here for array, _ in each])


def final_kernel(tokens, first, unit, start_ref, me_ref, low_ref, held_ref, *refs):
    panels, parts, out_ref = refs[: TURN_DEV + 1], refs[TURN_DEV + 1 : -1], refs[-1]
    rank = LANES // 2
    slot = block_slot(pl.program_id(0), start_ref, me_ref[0], tokens)
    low = low_ref[...].astype(BF16)
    low = jnp.concatenate([low[:, :rank], low[:, rank:]], axis=0)
    total = held_ref[...] + jnp.dot(low, chosen(slot, panels), preferred_element_type=F32)
    start = first * unit
    out_ref[:, :start] = total[:, :start].astype(BF16)
    rest = total[:, start:]
    for part in parts:
        rest = rest + part[...].astype(F32)
    out_ref[:, start:] = rest.astype(BF16)


def final_sum(starts, me, low, held, panels, parts, first, unit):
    tokens, features = held.shape
    rows = lambda i, s, m: (i, 0)
    whole = lambda i, s, m: (0, 0)
    return pl.pallas_call(
        functools.partial(final_kernel, tokens, first, unit),
        grid_spec=pltpu.PrefetchScalarGridSpec(
            num_scalar_prefetch=2,
            grid=(tokens // Q,),
            in_specs=[pl.BlockSpec((Q // 2, LANES), rows), pl.BlockSpec((Q, features), rows)]
            + [pl.BlockSpec(panel.shape, whole) for panel in panels]
            + [pl.BlockSpec((Q, part.shape[1]), rows) for part in parts],
            out_specs=pl.BlockSpec((Q, features), rows),
        ),
        out_shape=jax.ShapeDtypeStruct((tokens, features), BF16),
        compiler_params=params(),
        cost_estimate=cost(3),
        name="final_sum",
    )(starts, me, low, held, *panels, *parts)


def shift_up(block, axis, distance):
    devices = range(lax.axis_size(axis))
    route = [(i, i + distance) for i in devices if i + distance in devices]
    return lax.ppermute(block, axis, route)


def swap(block, axis, bits):
    return lax.ppermute(block, axis, [(i, i ^ bits) for i in range(lax.axis_size(axis))])


def after(value, *earlier):
    return lax.optimization_barrier((value, *earlier))[0]


def neighbour_edge(edge):
    size = lax.axis_size("ctx")
    even = lax.ppermute(edge, "ctx", [(i, i ^ 1) for i in range(size)])
    odd = lax.ppermute(edge, "ctx", [(i, i + 1 if i % 2 else i - 1) for i in range(1, size - 1)])
    return even, odd


class Route:
    def __init__(self, bits, send, keep):
        self.bits, self.send, self.keep = list(bits), send, keep
        self.got = None

    def merge(self, *earlier):
        half = self.keep.shape[0] // 2
        got = after(self.got, *earlier) if earlier else self.got
        self.send = self.keep[:half] + got[:half]
        self.keep = self.keep[half:] + got[half:]
        self.got = None
        return self.send

    def step(self, *earlier):
        if not self.bits:
            return
        if self.got is not None:
            self.merge(*earlier)
        send = after(self.send, *earlier) if earlier else self.send
        self.got = swap(send, "ctx", self.bits.pop(0))

    def end(self, *earlier):
        while self.bits:
            self.step(*earlier)
        keep, got = self.keep, self.got
        if earlier:
            keep = after(keep, *earlier)
        return keep[0] + got[0]


def unpacked(packed):
    decay = packed[N : N + 1].astype(F32) + packed[N + 1 : N + 2].astype(F32)
    return packed[:N].astype(F32), decay


def packed(state, decay):
    high = decay.astype(BF16)
    low = (decay - high.astype(F32)).astype(BF16)
    fill = jnp.zeros((HALO - 2, state.shape[1]), BF16)
    return jnp.concatenate([state.astype(BF16), high, low, fill], axis=0)


def local(
    input_x_channels,
    input_b_channels,
    input_c_channels,
    input_gate_channels,
    raw_step_sizes,
    log_decay_rate,
    head_skip_coeff,
    x_conv_taps,
    b_conv_taps,
    c_conv_taps,
    gated_norm_gain,
    output_weight,
    adapter_down_panels,
    adapter_up_panels,
    turn_first_token,
    tenant_of_turn,
    tenant_panel_index,
):
    tokens, inner = input_x_channels.shape
    heads = log_decay_rate.shape[0]
    blocks = tokens // Q
    features = adapter_up_panels.shape[2]
    unit = features // Y_UNITS
    ctx = lax.axis_index("ctx").astype(jnp.int32)
    head = lax.axis_index("head").astype(jnp.int32)
    devices = lax.axis_size("ctx")
    parity = ctx % 2
    first = parity == 0
    me = ctx[None]
    parity_arg, head_arg = parity[None], head[None]
    down = jnp.swapaxes(adapter_down_panels, 1, 2)
    up = adapter_up_panels
    outer = [1 << bit for bit in range(1, devices.bit_length() - 1)]
    near, far = [1] + outer, outer + [1]

    edge = sequence_edge(input_x_channels, input_b_channels, input_c_channels)
    halos = neighbour_edge(edge)

    slots = range(TURN_DEV)
    packs = pack_panels(
        [(down, near, slots[1:]), (down, far, slots[:1]), (up, near, slots)],
        tenant_panel_index, tenant_of_turn, me, devices,
    )
    down_late, down_early, ups = [
        Route(bits, *pack) for bits, pack in zip((near, far, near), packs)
    ]
    down_late.step()
    down_early.step()

    lane_head = jnp.arange(inner) // P_SIZE
    spread = (jnp.arange(2 * heads)[:, None] % heads == lane_head[None, :]).astype(BF16)
    xc, bc, run, shifted, before, start, keep, send = local_states(
        after(parity_arg, packs[0][0]),
        input_x_channels,
        input_b_channels,
        halos,
        raw_step_sizes,
        log_decay_rate[None],
        x_conv_taps,
        b_conv_taps,
        spread,
    )
    count = blocks // PIECES

    def mix_piece(piece, held, *earlier):
        return mix(
            piece * count, count, after(parity_arg, *earlier), xc, bc, input_c_channels, halos, run, shifted,
            before, start, input_gate_channels, head_skip_coeff[None], c_conv_taps, spread, held,
        )

    got = swap(send, "ctx", 1)
    held = mix_piece(0, None, send)
    got = after(got, held[2])
    own_state, own_decay = unpacked(keep)
    got_state, got_decay = unpacked(got)
    first_state = jnp.where(first, own_state, got_state)
    first_decay = jnp.where(first, own_decay, got_decay)
    total = jnp.where(first, got_state, own_state)
    total_decay = jnp.where(first, got_decay, own_decay)
    total, total_decay = total + total_decay * first_state, total_decay * first_decay
    early = [down_late.got, down_early.got]
    ups.step(got)
    incoming = jnp.zeros_like(total)
    incoming_decay = jnp.ones_like(total_decay)
    piece = 1
    for bit in outer:
        sent = packed(total, total_decay)
        got = swap(sent, "ctx", bit)
        if piece < PIECES - 1:
            held = mix_piece(piece, held, sent, *early)
            merged = [held[2]]
            if bit == outer[-1]:
                merged += [route.merge(sent) for route in (down_late, down_early)]
            got = after(got, *merged)
            piece += 1
        state, decay = unpacked(got)
        upper = (ctx & bit) != 0
        incoming = jnp.where(upper, incoming + incoming_decay * state, incoming)
        incoming_decay = jnp.where(upper, incoming_decay * decay, incoming_decay)
        total, total_decay = (
            jnp.where(upper, total + total_decay * state, state + decay * total),
            total_decay * decay,
        )
    incoming_second = first_state + first_decay * incoming
    back_sent = jnp.where(first, incoming_second, incoming).astype(BF16)
    kept = jnp.where(first, incoming, incoming_second).astype(BF16)
    back = swap(back_sent, "ctx", 1)
    for route in (down_late, down_early):
        route.step(back_sent)
    while piece < PIECES:
        held = mix_piece(piece, held, back_sent, ups.got)
        piece += 1
    part, scale, cc = held

    chips = range(1, lax.axis_size("head") // 2)
    first, later = range(Y_FIRST), range(Y_FIRST, Y_UNITS)

    def sides(units):
        return [(2 * chip ^ core, at) for core in (1, 0) for chip in chips for at in units]

    parts = []

    def send_both(mine, to_pair, units, *earlier):
        from_pair = swap(after(to_pair, *earlier), "head", 1)
        sums = []
        for chip in chips:
            both = add_columns(mine, from_pair, (chip - 1) * len(units), len(units), unit)
            arrived = swap(both, "head", 2 * chip)
            parts.extend((arrived, at - units.start, at) for at in units)
            sums.append(both)
        return sums

    routes = (down_late, down_early, ups)
    y_normed, to_pair, mine = norm_project(
        parity_arg, head_arg, sides(first), part, scale, cc, kept, back,
        gated_norm_gain[None], output_weight, unit,
    )
    sums = send_both(mine, to_pair, first, *[route.got for route in routes])
    for route in routes:
        route.step(*sums)
    to_pair, mine = project_both(after(head_arg, *sums), sides(later), y_normed, output_weight, unit)
    sums = send_both(
        mine, to_pair, later, *[arrived for arrived, _, _ in parts], *[route.got for route in routes]
    )
    down_second = down_late.end(*sums)
    down_first = down_early.end(*sums)
    down_before = shift_up(down_second, "ctx", 1)
    ups.step(*sums)
    to_pair = project(
        after(head_arg, *sums), [(1, at) for at in range(Y_UNITS)], y_normed, output_weight, unit, True
    )
    pair = [swap(each, "head", 1) for each in to_pair]
    (own,) = project(
        after(head_arg, *to_pair, down_before, ups.got),
        [(0, at) for at in range(Y_UNITS)], y_normed, output_weight, unit, False,
    )
    up_own = ups.end(*to_pair)
    rank = up.shape[1]
    up_first, up_second = up_own[:rank], up_own[rank:]
    up_before = shift_up(up_second, "ctx", 1)
    low = low_part(
        after(turn_first_token, own, up_before), me, y_normed, [down_before, down_first, down_second]
    )
    low = low + swap(low, "head", 1)
    low_sent = low.astype(BF16)
    for chip in chips:
        low = low + swap(low_sent, "head", 2 * chip).astype(F32)
    here = [each for each in parts if each[2] in first]
    held = held_sum(own, pair, here, unit)
    last = [arrived for arrived, at, _ in parts[len(here) :] if at == 0]
    return final_sum(
        turn_first_token, me, low, held, [up_before, up_first, up_second], last, Y_FIRST, unit
    )


def solution(mesh):
    in_specs = (
        P("ctx", "head"),
        P("ctx", "head"),
        P("ctx", "head"),
        P("ctx", "head"),
        P("head", "ctx"),
        P("head"),
        P("head"),
        P(None, "head"),
        P(None, "head"),
        P(None, "head"),
        P("head"),
        P("head", None),
        P("ctx", "head", None),
        P("ctx", None, "head"),
        P(),
        P(),
        P(),
    )
    out_specs = P("ctx", "head")
    return jax.shard_map(local, mesh=mesh, in_specs=in_specs, out_specs=out_specs, check_vma=False)
```

time: 233 us -> 195 us (0.84)
  the two profiles are of different devices: /device:TPU:18 before, /device:TPU:0 now
where the time goes in v2:
time: 195 us
  Pallas kernels  108 us (55%)
  starting transfers between devices  34.3 us (18%)
  waiting for transfers between devices  26.9 us (14%)
  other arithmetic  17.9 us (9%)
  local copies, waits for them, and re-layouts  6.88 us (4%)
    ppermute x23, waiting for transfers between devices, swap(): lax.ppermute(block, axis, [(i, i ^ bits) for i in range(lax.axis_size(axi...  26.8 us
    ppermute x23, starting transfers between devices, swap(): lax.ppermute(block, axis, [(i, i ^ bits) for i in range(lax.axis_size(axi...  24.2 us
    pallas_call x4, Pallas kernels, mix(): pl.pallas_call(functools.partial(mix_kernel, first, bool(aliased)), grid_...  23 us
    pallas_call x2, Pallas kernels, project(): pl.pallas_call(functools.partial(project_kernel, apart), grid_spec=pltpu....  17.6 us
    pallas_call x1, Pallas kernels, local_states(): pl.pallas_call(state_kernel, grid_spec=pltpu.PrefetchScalarGridSpec(num_s...  16.3 us
    pallas_call x1, Pallas kernels, norm_project(): pl.pallas_call(functools.partial(norm_kernel, tiles), grid_spec=pltpu.Pre...  14.4 us
    add x5, other arithmetic, merge(): self.keep = self.keep[half:] + got[half:]  10.6 us
    pallas_call x1, Pallas kernels, project_both(): pl.pallas_call(functools.partial(both_kernel, units), grid_spec=pltpu.Pre...  8.83 us
  transfers between devices with their start and end apart: 27, of which 15 were waited for; matrix products, arithmetic and copies ran while one was open for 10% of the time, Pallas kernels for 48%

profile of v2, /device:TPU:0, one launch (start us, length us, event | category | flops | bytes accessed | tf_op | source)
XLA Modules:
  0.0 194.6 jit_solution(4601876404213233387)
XLA Ops:
  0.0 1.5 sequence_edge.1
  1.5 2.9 %collective-permute-start = (bf16[16,2560]{1,0:T(8,128)(2,1)}, bf16[16,2560]{1,0:T(8,128)(2,1)S(1)}, u32[]{:S(2)}, u32[]{:S(2)}) collective-permute-start(bf16[16,2560]{1,0:T(8,128)(2,1)} %sequence_edge.1), channel_id=1, source_target_pairs={{0,4},{4,0},{8,12},{12,8},{16,20},{20,16},{24,28},{28,24},{1,5},{5... | collective-permute-start | bytes 245768 | tf_op jit(solution)/shard_map/ppermute | solution.py:735
  5.1 6.6 %pack_panels.1 = (bf16[4,64,2048]{2,1,0:T(8,128)(2,1)}, bf16[4,64,2048]{2,1,0:T(8,128)(2,1)}, bf16[4,64,2048]{2,1,0:T(8,128)(2,1)}, bf16[4,64,2048]{2,1,0:T(8,12...) custom-call(s32[48]{0:T(128)} %index_ref.1, s32[16]{0:T(128)} %tenant_ref.1, s32[1]{0:T(128)} %bitcast.me_ref, ...), custom_call_target="tpu_custom_call" | custom-call | flops 500000 | bytes 1 | tf_op jit(solution)/shard_map/pack_panels/pallas_call | solution.py:156
  11.7 4.9 %collective-permute-start.4 = (bf16[4,64,2048]{2,1,0:T(8,128)(2,1)}, bf16[4,64,2048]{2,1,0:T(8,128)(2,1)S(1)}, u32[]{:S(2)}, u32[]{:S(2)}) collective-permute-start(bf16[4,64,2048]{2,1,0:T(8,128)(2,1)} %get-tuple-element.70), channel_id=1, source_target_pairs={{0,4},{4,0},{8,12},{12,8},{16,20},{20,16},{24,28},{28,24},{1,5},{5... | collective-permute-start | bytes 3145736 | tf_op jit(solution)/shard_map/ppermute | solution.py:726
  16.6 2.4 %collective-permute-start.5 = (bf16[4,64,2048]{2,1,0:T(8,128)(2,1)}, bf16[4,64,2048]{2,1,0:T(8,128)(2,1)}, u32[]{:S(2)}, u32[]{:S(2)}) collective-permute-start(bf16[4,64,2048]{2,1,0:T(8,128)(2,1)} %get-tuple-element.83), channel_id=1, source_target_pairs={{0,8},{4,12},{8,0},{12,4},{16,24},{20,28},{24,16},{28,20},{1,9},{5... | collective-permute-start | bytes 3145736 | tf_op jit(solution)/shard_map/ppermute | solution.py:726
  20.5 16.3 %local_states.1 = (bf16[1024,2048]{1,0:T(8,128)(2,1)}, bf16[1024,256]{1,0:T(8,128)(2,1)}, f32[32,1024]{1,0:T(8,128)}, f32[32,1024]{1,0:T(8,128)}, bf16[1024,2048...) custom-call(s32[1]{0:T(128)} %bitcast.2.parity_ref, ...), custom_call_target="tpu_custom_call" | custom-call | flops 15000000512 | bytes 1 | tf_op jit(solution)/shard_map/local_states/pallas_call | solution.py:262
  37.0 5.7 %mix.4 = (bf16[1024,2048]{1,0:T(8,128)(2,1)}, bf16[1024,2048]{1,0:T(8,128)(2,1)}, bf16[1024,256]{1,0:T(8,128)(2,1)}) custom-call(s32[1]{0:T(128)} %bitcast.2.parity_ref, bf16[1024,2048]{1,0:T(8,128)(2,1)} %get-tuple-element.75.refs_0_, bf16[1024,256]{1,0:T(8,128)(2,1)} %get-tuple-element.76.refs_1_, bf16[1024,256]{1,0:T(8,128)(2,1)} %refs_3_.9, ...), custom_call_target="tpu_custom_call" | custom-call | flops 5000000000 | bytes 1 | tf_op jit(solution)/shard_map/mix/pallas_call | solution.py:383
  42.7 3.0 %collective-permute-done.2 = bf16[144,1024]{1,0:T(8,128)(2,1)S(1)} collective-permute-done((bf16[144,1024]{1,0:T(8,128)(2,1)}, bf16[144,1024]{1,0:T(8,128)(2,1)S(1)}, u32[]{:S(2)}, u32[]{:S(2)}) %collective-permute-start.2) | collective-permute-done | bytes 294944 | tf_op jit(solution)/shard_map/ppermute | solution.py:726
  46.7 2.4 %collective-permute-start.3 = (bf16[144,1024]{1,0:T(8,128)(2,1)}, bf16[144,1024]{1,0:T(8,128)(2,1)S(1)}, u32[]{:S(2)}, u32[]{:S(2)}) collective-permute-start(bf16[144,1024]{1,0:T(8,128)(2,1)} %maximum_maximum_fusion), channel_id=1, source_target_pairs={{0,8},{4,12},{8,0},{12,4},{16,24},{20,28},{24,16},{28,20},{1,9},{5... | collective-permute-start | bytes 884744 | tf_op jit(solution)/shard_map/ppermute | solution.py:726
  49.1 1.7 collective-permute-start.7
  50.8 6.0 %mix.5 = (bf16[1024,2048]{1,0:T(8,128)(2,1)}, bf16[1024,2048]{1,0:T(8,128)(2,1)}, bf16[1024,256]{1,0:T(8,128)(2,1)}) custom-call(s32[1]{0:T(128)} %bitcast.2.parity_ref, bf16[1024,2048]{1,0:T(8,128)(2,1)} %get-tuple-element.75.refs_0_, bf16[1024,256]{1,0:T(8,128)(2,1)} %get-tuple-element.76.refs_1_, ...), custom_call_target="tpu_custom_call", output_to_operand_aliasing={{0}: (15, {}), {1}: (16, {}), {2}: (17, {})} | custom-call | flops 5000000000 | bytes 1 | tf_op jit(solution)/shard_map/mix/pallas_call | solution.py:383
  57.2 1.2 collective-permute-start.6
  58.5 3.3 %slice_add_fusion.2 = (bf16[2,64,2048]{2,1,0:T(8,128)(2,1)}, bf16[2,64,2048]{2,1,0:T(8,128)(2,1)}, bf16[2,64,2048]{2,1,0:T(8,128)(2,1)}, bf16[2,64,2048]{2,1,0:T(8,128)(2,1)S(1)}) fusion(bf16[4,64,2048]{2,1,0:T(8,128)(2,1)} %collective-permute-done.5, bf16[4,64,2048]{2,1,0:T(8,128)(2,1)} %get-tuple-element.95, bf16[4,64,2048]{2,1,0:T(8,128)(2,1)} %copy-done.7, ...), kind=kLoop, calls=%fused_computation.12 | loop fusion | flops 1048576 | bytes 6291456 | tf_op jit(solution)/shard_map/add | solution.py:749
  61.8 5.6 %mix.6 = (bf16[1024,2048]{1,0:T(8,128)(2,1)}, bf16[1024,2048]{1,0:T(8,128)(2,1)}, bf16[1024,256]{1,0:T(8,128)(2,1)}) custom-call(s32[1]{0:T(128)} %bitcast.2.parity_ref, bf16[1024,2048]{1,0:T(8,128)(2,1)} %get-tuple-element.75.refs_0_, bf16[1024,256]{1,0:T(8,128)(2,1)} %get-tuple-element.76.refs_1_, ...), custom_call_target="tpu_custom_call", output_to_operand_aliasing={{0}: (15, {}), {1}: (16, {}), {2}: (17, {})} | custom-call | flops 5000000000 | bytes 1 | tf_op jit(solution)/shard_map/mix/pallas_call | solution.py:383
  67.5 3.9 %collective-permute-done.6 = bf16[144,1024]{1,0:T(8,128)(2,1)} collective-permute-done((bf16[144,1024]{1,0:T(8,128)(2,1)S(1)}, bf16[144,1024]{1,0:T(8,128)(2,1)}, u32[]{:S(2)}, u32[]{:S(2)}) %collective-permute-start.6) | collective-permute-done | bytes 294944 | tf_op jit(solution)/shard_map/ppermute | solution.py:726
  71.3 2.0 %select_convert_fusion = (bf16[128,1024]{1,0:T(8,128)(2,1)}, bf16[128,1024]{1,0:T(8,128)(2,1)}) fusion(f32[1024]{0:T(1024)S(1)} %bitcast.25, f32[1024]{0:T(1024)S(1)} %bitcast.26, pred[]{:T(512)S(6)} %ne.85, pred[]{:T(512)S(6)} %ne.84, pred[]{:T(512)S(6)} %eq.44, bf16[144,1024]{1,0:T(8,128)(2,1)} %collective-permute-done.6, ...), kind=kLoop, calls=%fused_computation.14 | loop fusion | flops 1966080 | bytes 1581059 | tf_op jit(solution)/shard_map/convert_element_type | solution.py:888
  73.3 2.9 %collective-permute-start.9 = (bf16[2,64,2048]{2,1,0:T(8,128)(2,1)}, bf16[2,64,2048]{2,1,0:T(8,128)(2,1)S(1)}, u32[]{:S(2)}, u32[]{:S(2)}) collective-permute-start(bf16[2,64,2048]{2,1,0:T(8,128)(2,1)} %get-tuple-element.108), channel_id=1, source_target_pairs={{0,8},{4,12},{8,0},{12,4},{16,24},{20,28},{24,16},{28,20},{1,9},{5... | collective-permute-start | bytes 1572872 | tf_op jit(solution)/shard_map/ppermute | solution.py:726
  76.8 0.9 collective-permute-start.8
  77.7 5.7 %mix.7 = (bf16[1024,2048]{1,0:T(8,128)(2,1)}, bf16[1024,2048]{1,0:T(8,128)(2,1)}, bf16[1024,256]{1,0:T(8,128)(2,1)}) custom-call(s32[1]{0:T(128)} %bitcast.2.parity_ref, bf16[1024,2048]{1,0:T(8,128)(2,1)} %get-tuple-element.75.refs_0_, bf16[1024,256]{1,0:T(8,128)(2,1)} %get-tuple-element.76.refs_1_, ...), custom_call_target="tpu_custom_call", output_to_operand_aliasing={{0}: (15, {}), {1}: (16, {}), {2}: (17, {})} | custom-call | flops 5000000000 | bytes 1 | tf_op jit(solution)/shard_map/mix/pallas_call | solution.py:383
  83.4 1.3 collective-permute-done.8.got_ref
  85.4 14.4 %norm_project.1 = (bf16[1024,2048]{1,0:T(8,128)(2,1)}, bf16[1024,512]{1,0:T(8,128)(2,1)}, bf16[1024,512]{1,0:T(8,128)(2,1)}) custom-call(s32[1]{0:T(128)} %bitcast.2.parity_ref, s32[1]{0:T(128)} %bitcast.1.place_ref.head_ref, bf16[1024,2048]{1,0:T(8,128)(2,1)} %get-tuple-element.103.part_ref, bf16[1024,2048]{1,0:T(8,128)(2,1)} %get-tuple-element.104.scale_ref, ...), custom_call_target="tpu_custom_call" | custom-call | flops 1100000 | bytes 1 | tf_op jit(solution)/shard_map/norm_project/pallas_call | solution.py:478
  101.5 2.9 %collective-permute-done.11.right_ref = bf16[1024,512]{1,0:T(8,128)(2,1)S(1)} collective-permute-done((bf16[1024,512]{1,0:T(8,128)(2,1)}, bf16[1024,512]{1,0:T(8,128)(2,1)S(1)}, u32[]{:S(2)}, u32[]{:S(2)}) %collective-permute-start.11) | collective-permute-done | bytes 1048608 | tf_op jit(solution)/shard_map/ppermute | solution.py:726
  104.4 1.0 copy-done.5
  105.3 3.7 %add_columns.2 = bf16[1024,512]{1,0:T(8,128)(2,1)} custom-call(bf16[1024,512]{1,0:T(8,128)(2,1)} %get-tuple-element.106.left_ref, bf16[1024,512]{1,0:T(8,128)(2,1)} %copy-done.5), custom_call_target="tpu_custom_call" | custom-call | flops 100000 | bytes 1 | tf_op jit(solution)/shard_map/add_columns/pallas_call | solution.py:518
  109.0 1.5 collective-permute-start.12
  110.6 2.6 %slice_add_fusion = (bf16[2,128,1024]{2,1,0:T(8,128)(2,1)}, bf16[2,128,1024]{2,1,0:T(8,128)(2,1)}) fusion(bf16[4,128,1024]{2,1,0:T(8,128)(2,1)} %collective-permute-done.7, bf16[4,128,1024]{2,1,0:T(8,128)(2,1)} %get-tuple-element.119), kind=kLoop, calls=%fused_computation.10 | loop fusion | flops 524288 | bytes 3145728 | tf_op jit(solution)/shard_map/add | solution.py:749
  113.4 2.0 %slice_add_fusion.6 = (bf16[1,64,2048]{2,1,0:T(8,128)(2,1)}, bf16[1,64,2048]{2,1,0:T(8,128)(2,1)}) fusion(bf16[2,64,2048]{2,1,0:T(8,128)(2,1)} %get-tuple-element.145, bf16[2,64,2048]{2,1,0:T(8,128)(2,1)} %copy-done.12), kind=kLoop, calls=%fused_computation.23 | loop fusion | flops 262144 | bytes 1572864 | tf_op jit(solution)/shard_map/add | solution.py:749
  117.1 1.5 collective-permute-start.13
  118.6 8.8 %project_both.1 = (bf16[1024,512]{1,0:T(8,128)(2,1)}, bf16[1024,512]{1,0:T(8,128)(2,1)}) custom-call(s32[1]{0:T(128)} %bitcast.1.place_ref.head_ref, bf16[1024,2048]{1,0:T(8,128)(2,1)} %get-tuple-element.112.y_ref, bf16[2048,4096]{1,0:T(8,128)(2,1)} %w_ref.7), custom_call_target="tpu_custom_call" | custom-call | flops 100000 | bytes 1 | tf_op jit(solution)/shard_map/project_both/pallas_call | solution.py:588
  127.4 3.2 %collective-permute-done.13 = bf16[1,64,2048]{2,1,0:T(8,128)(2,1)} collective-permute-done((bf16[1,64,2048]{2,1,0:T(8,128)(2,1)}, bf16[1,64,2048]{2,1,0:T(8,128)(2,1)}, u32[]{:S(2)}, u32[]{:S(2)}) %collective-permute-start.13) | collective-permute-done | bytes 262176 | tf_op jit(solution)/shard_map/ppermute | solution.py:726
  130.6 2.2 %collective-permute-done.15 = bf16[2,128,1024]{2,1,0:T(8,128)(2,1)} collective-permute-done((bf16[2,128,1024]{2,1,0:T(8,128)(2,1)}, bf16[2,128,1024]{2,1,0:T(8,128)(2,1)}, u32[]{:S(2)}, u32[]{:S(2)}) %collective-permute-start.15) | collective-permute-done | bytes 524320 | tf_op jit(solution)/shard_map/ppermute | solution.py:726
  132.8 1.7 collective-permute-done.12.refs_8_.refs_9_
  134.5 3.0 %collective-permute-done.16.right_ref = bf16[1024,512]{1,0:T(8,128)(2,1)} collective-permute-done((bf16[1024,512]{1,0:T(8,128)(2,1)}, bf16[1024,512]{1,0:T(8,128)(2,1)}, u32[]{:S(2)}, u32[]{:S(2)}) %collective-permute-start.16) | collective-permute-done | bytes 1048608 | tf_op jit(solution)/shard_map/ppermute | solution.py:726
  137.5 3.7 %add_columns.3 = bf16[1024,512]{1,0:T(8,128)(2,1)} custom-call(bf16[1024,512]{1,0:T(8,128)(2,1)} %get-tuple-element.113.left_ref, bf16[1024,512]{1,0:T(8,128)(2,1)} %collective-permute-done.16.right_ref), custom_call_target="tpu_custom_call" | custom-call | flops 100000 | bytes 1 | tf_op jit(solution)/shard_map/add_columns/pallas_call | solution.py:518
  141.2 1.5 collective-permute-start.26
  142.7 1.9 slice_add_fusion.7
  144.8 1.0 add_bitcast_fusion.1.refs_2_
  145.8 3.6 %collective-permute-start.17 = (bf16[64,2048]{1,0:T(8,128)(2,1)S(1)}, bf16[64,2048]{1,0:T(8,128)(2,1)}, u32[]{:S(2)}, u32[]{:S(2)}) collective-permute-start(bf16[64,2048]{1,0:T(8,128)(2,1)S(1)} %add_bitcast_fusion.1.refs_2_), channel_id=1, source_target_pairs={{0,4},{4,8},{8,12},{12,16},{16,20},{20,24},{24,28},{1,5},{5,9},{9,... | collective-permute-start | bytes 786440 | tf_op jit(solution)/shard_map/ppermute | solution.py:722
  149.4 9.0 %project.2 = (bf16[1024,256]{1,0:T(8,128)(2,1)}, bf16[1024,256]{1,0:T(8,128)(2,1)}, bf16[1024,256]{1,0:T(8,128)(2,1)}, bf16[1024,256]{1,0:T(8,128)(2,1)}) custom-call(s32[1]{0:T(128)} %bitcast.1.place_ref.head_ref, bf16[1024,2048]{1,0:T(8,128)(2,1)} %get-tuple-element.112.y_ref, bf16[2048,4096]{1,0:T(8,128)(2,1)} %w_ref.7), custom_call_target="tpu_custom_call" | custom-call | flops 100000 | bytes 1 | tf_op jit(solution)/shard_map/project/pallas_call | solution.py:562
  159.2 1.0 add.131
  160.2 2.9 %collective-permute-start.19 = (bf16[64,1024]{1,0:T(8,128)(2,1)S(1)}, bf16[64,1024]{1,0:T(8,128)(2,1)S(1)}, u32[]{:S(2)}, u32[]{:S(2)}) collective-permute-start(bf16[64,1024]{1,0:T(8,128)(2,1)S(1)} %get-tuple-element.158.refs_2_), channel_id=1, source_target_pairs={{0,4},{4,8},{8,12},{12,16},{16,20},{20,24},{24,28},{1,5},{5,9},{9,... | collective-permute-start | bytes 393224 | tf_op jit(solution)/shard_map/ppermute | solution.py:722
  163.1 1.1 add_bitcast_fusion.refs_1_
  164.2 8.6 %project.3.refs_0_.refs_1_.refs_2_.refs_3_ = bf16[1024,1024]{1,0:T(8,128)(2,1)} custom-call(s32[1]{0:T(128)} %bitcast.1.place_ref.head_ref, bf16[1024,2048]{1,0:T(8,128)(2,1)} %get-tuple-element.112.y_ref, bf16[2048,4096]{1,0:T(8,128)(2,1)} %w_ref.7), custom_call_target="tpu_custom_call" | custom-call | flops 100000 | bytes 1 | tf_op jit(solution)/shard_map/project/pallas_call | solution.py:562
  172.8 2.2 %copy-done = bf16[1024,2048]{1,0:T(8,128)(2,1)S(1)} copy-done((bf16[1024,2048]{1,0:T(8,128)(2,1)S(1)}, bf16[1024,2048]{1,0:T(8,128)(2,1)}, u32[]{:S(2)}) %copy-start) | copy-done | bytes 4194328
  175.0 4.8 %low_part.1 = f32[512,128]{1,0:T(8,128)S(1)} custom-call(s32[16]{0:T(128)S(1)} %copy-done.2, s32[1]{0:T(128)} %bitcast.me_ref, bf16[1024,2048]{1,0:T(8,128)(2,1)S(1)} %copy-done, bf16[64,2048]{1,0:T(8,128)(2,1)} %collective-permute-done.17.refs_0_, bf16[64,2048]{1,0:T(8,128)(2,1)S(1)} %add_bitcast_fusion.refs_1_, bf16[64,2048]{1,0:T(8,128)(2,1)S(1)} %add_bitcast_fusion.1.refs_2_), custom_call_target="tpu_custom_call" | custom-call | flops 400000 | bytes 1 | tf_op jit(solution)/shard_map/low_part/pallas_call | solution.py:638
  184.4 1.0 held_sum.1.held_ref
  185.5 2.3 %collective-permute-done.21 = bf16[512,128]{1,0:T(8,128)(2,1)S(1)} collective-permute-done((bf16[512,128]{1,0:T(8,128)(2,1)S(1)}, bf16[512,128]{1,0:T(8,128)(2,1)S(1)}, u32[]{:S(2)}, u32[]{:S(2)}) %collective-permute-start.21) | collective-permute-done | bytes 131104 | tf_op jit(solution)/shard_map/ppermute | solution.py:726
  187.8 6.8 %final_sum.1 = bf16[1024,1024]{1,0:T(8,128)(2,1)} custom-call(s32[16]{0:T(128)S(1)} %copy-done.2, s32[1]{0:T(128)} %bitcast.me_ref, f32[512,128]{1,0:T(8,128)S(1)} %convert_add_fusion.1.low_ref, f32[1024,1024]{1,0:T(8,128)S(1)} %held_sum.1.held_ref, bf16[64,1024]{1,0:T(8,128)(2,1)S(1)} %collective-permute-done.19.refs_0_, ...), custom_call_target="tpu_custom_call" | custom-call | flops 300000 | bytes 1 | tf_op jit(solution)/shard_map/final_sum/pallas_call | solution.py:702
  (86 shorter events, 14.2 us)
Async XLA Ops:
  1.5 18.3 %collective-permute-start = (bf16[16,2560]{1,0:T(8,128)(2,1)}, bf16[16,2560]{1,0:T(8,128)(2,1)S(1)}, u32[]{:S(2)}, u32[]{:S(2)}) collective-permute-start(bf16[16,2560]{1,0:T(8,128)(2,1)} %sequence_edge.1), channel_id=1, source_target_pairs={{0,4},{4,0},{8,12},{12,8},{16,20},{20,16},{24,28},{28,24},{1,5},{5... | collective-permute-start | bytes 245768 | tf_op jit(solution)/shard_map/ppermute | solution.py:735
  4.4 15.4 %collective-permute-start.1 = (bf16[16,2560]{1,0:T(8,128)(2,1)}, bf16[16,2560]{1,0:T(8,128)(2,1)S(1)}, u32[]{:S(2)}, u32[]{:S(2)}) collective-permute-start(bf16[16,2560]{1,0:T(8,128)(2,1)} %sequence_edge.1), channel_id=1, source_target_pairs={{4,8},{8,4},{12,16},{16,12},{20,24},{24,20},{5,9},{9,5},{13,17},{1... | collective-permute-start | bytes 245768 | tf_op jit(solution)/shard_map/ppermute | solution.py:736
  11.7 39.1 %collective-permute-start.4 = (bf16[4,64,2048]{2,1,0:T(8,128)(2,1)}, bf16[4,64,2048]{2,1,0:T(8,128)(2,1)S(1)}, u32[]{:S(2)}, u32[]{:S(2)}) collective-permute-start(bf16[4,64,2048]{2,1,0:T(8,128)(2,1)} %get-tuple-element.70), channel_id=1, source_target_pairs={{0,4},{4,0},{8,12},{12,8},{16,20},{20,16},{24,28},{28,24},{1,5},{5... | collective-permute-start | bytes 3145736 | tf_op jit(solution)/shard_map/ppermute | solution.py:726
  16.6 34.3 %collective-permute-start.5 = (bf16[4,64,2048]{2,1,0:T(8,128)(2,1)}, bf16[4,64,2048]{2,1,0:T(8,128)(2,1)}, u32[]{:S(2)}, u32[]{:S(2)}) collective-permute-start(bf16[4,64,2048]{2,1,0:T(8,128)(2,1)} %get-tuple-element.83), channel_id=1, source_target_pairs={{0,8},{4,12},{8,0},{12,4},{16,24},{20,28},{24,16},{28,20},{1,9},{5... | collective-permute-start | bytes 3145736 | tf_op jit(solution)/shard_map/ppermute | solution.py:726
  19.8 0.6 copy-start.8
  19.9 0.7 copy-start.9
  36.9 8.8 %collective-permute-start.2 = (bf16[144,1024]{1,0:T(8,128)(2,1)}, bf16[144,1024]{1,0:T(8,128)(2,1)S(1)}, u32[]{:S(2)}, u32[]{:S(2)}) collective-permute-start(bf16[144,1024]{1,0:T(8,128)(2,1)} %get-tuple-element.73), channel_id=1, source_target_pairs={{0,4},{4,0},{8,12},{12,8},{16,20},{20,16},{24,28},{28,24},{1,5},{5... | collective-permute-start | bytes 884744 | tf_op jit(solution)/shard_map/ppermute | solution.py:726
  37.0 8.7 %copy-start.3 = (bf16[144,1024]{1,0:T(8,128)(2,1)S(1)}, bf16[144,1024]{1,0:T(8,128)(2,1)}, u32[]{:S(2)}) copy-start(bf16[144,1024]{1,0:T(8,128)(2,1)} %get-tuple-element.72) | copy-start | bytes 884740
  46.7 10.2 %collective-permute-start.3 = (bf16[144,1024]{1,0:T(8,128)(2,1)}, bf16[144,1024]{1,0:T(8,128)(2,1)S(1)}, u32[]{:S(2)}, u32[]{:S(2)}) collective-permute-start(bf16[144,1024]{1,0:T(8,128)(2,1)} %maximum_maximum_fusion), channel_id=1, source_target_pairs={{0,8},{4,12},{8,0},{12,4},{16,24},{20,28},{24,16},{28,20},{1,9},{5... | collective-permute-start | bytes 884744 | tf_op jit(solution)/shard_map/ppermute | solution.py:726
  49.1 28.6 %collective-permute-start.7 = (bf16[4,128,1024]{2,1,0:T(8,128)(2,1)}, bf16[4,128,1024]{2,1,0:T(8,128)(2,1)}, u32[]{:S(2)}, u32[]{:S(2)}) collective-permute-start(bf16[4,128,1024]{2,1,0:T(8,128)(2,1)} %get-tuple-element.99), channel_id=1, source_target_pairs={{0,4},{4,0},{8,12},{12,8},{16,20},{20,16},{24,28},{28,24},{1,5},{5... | collective-permute-start | bytes 3145736 | tf_op jit(solution)/shard_map/ppermute | solution.py:726
  50.8 6.0 %copy-start.7 = (bf16[4,64,2048]{2,1,0:T(8,128)(2,1)}, bf16[4,64,2048]{2,1,0:T(8,128)(2,1)S(1)}, u32[]{:S(2)}) copy-start(bf16[4,64,2048]{2,1,0:T(8,128)(2,1)S(1)} %collective-permute-done.4) | copy-start | bytes 3145732
  57.2 14.1 %collective-permute-start.6 = (bf16[144,1024]{1,0:T(8,128)(2,1)S(1)}, bf16[144,1024]{1,0:T(8,128)(2,1)}, u32[]{:S(2)}, u32[]{:S(2)}) collective-permute-start(bf16[144,1024]{1,0:T(8,128)(2,1)S(1)} %maximum_maximum_fusion.1), channel_id=1, source_target_pairs={{0,16},{4,20},{8,24},{12,28},{16,0},{20,4},{24,8},{28,12},{1,17},{... | collective-permute-start | bytes 884744 | tf_op jit(solution)/shard_map/ppermute | solution.py:726
  61.8 14.4 %copy-start.14 = (bf16[2048]{0:T(1024)(128)(2,1)S(1)}, bf16[2048]{0:T(1024)(128)(2,1)}, u32[]{:S(2)}) copy-start(bf16[2048]{0:T(1024)(128)(2,1)} %param.27) | copy-start | bytes 12292
  73.3 26.6 %collective-permute-start.10 = (bf16[2,64,2048]{2,1,0:T(8,128)(2,1)}, bf16[2,64,2048]{2,1,0:T(8,128)(2,1)S(1)}, u32[]{:S(2)}, u32[]{:S(2)}) collective-permute-start(bf16[2,64,2048]{2,1,0:T(8,128)(2,1)} %get-tuple-element.109), channel_id=1, source_target_pairs={{0,16},{4,20},{8,24},{12,28},{16,0},{20,4},{24,8},{28,12},{1,17},{... | collective-permute-start | bytes 1572872 | tf_op jit(solution)/shard_map/ppermute | solution.py:726
  73.3 26.6 %collective-permute-start.9 = (bf16[2,64,2048]{2,1,0:T(8,128)(2,1)}, bf16[2,64,2048]{2,1,0:T(8,128)(2,1)S(1)}, u32[]{:S(2)}, u32[]{:S(2)}) collective-permute-start(bf16[2,64,2048]{2,1,0:T(8,128)(2,1)} %get-tuple-element.108), channel_id=1, source_target_pairs={{0,8},{4,12},{8,0},{12,4},{16,24},{20,28},{24,16},{28,20},{1,9},{5... | collective-permute-start | bytes 1572872 | tf_op jit(solution)/shard_map/ppermute | solution.py:726
  76.8 7.9 %collective-permute-start.8 = (bf16[128,1024]{1,0:T(8,128)(2,1)}, bf16[128,1024]{1,0:T(8,128)(2,1)S(1)}, u32[]{:S(2)}, u32[]{:S(2)}) collective-permute-start(bf16[128,1024]{1,0:T(8,128)(2,1)} %get-tuple-element.150), channel_id=1, source_target_pairs={{0,4},{4,0},{8,12},{12,8},{16,20},{20,16},{24,28},{28,24},{1,5},{5... | collective-permute-start | bytes 786440 | tf_op jit(solution)/shard_map/ppermute | solution.py:726
  84.7 0.7 copy-start.13
  99.9 0.8 copy-start.12
  100.7 0.8 copy-start.10
  101.5 2.9 %collective-permute-start.11 = (bf16[1024,512]{1,0:T(8,128)(2,1)}, bf16[1024,512]{1,0:T(8,128)(2,1)S(1)}, u32[]{:S(2)}, u32[]{:S(2)}) collective-permute-start(bf16[1024,512]{1,0:T(8,128)(2,1)} %get-tuple-element.110), channel_id=1, source_target_pairs={{0,1},{1,0},{2,3},{3,2},{4,5},{5,4},{6,7},{7,6},{8,9},{9,8},{10,11... | collective-permute-start | bytes 3145736 | tf_op jit(solution)/shard_map/ppermute | solution.py:726
  104.4 1.0 copy-start.5
  109.0 7.3 %copy-start.11 = (bf16[2,64,2048]{2,1,0:T(8,128)(2,1)S(1)}, bf16[2,64,2048]{2,1,0:T(8,128)(2,1)}, u32[]{:S(2)}) copy-start(bf16[2,64,2048]{2,1,0:T(8,128)(2,1)} %copy-done.10) | copy-start | bytes 1572868
  109.0 25.4 %collective-permute-start.12 = (bf16[1024,512]{1,0:T(8,128)(2,1)}, bf16[1024,512]{1,0:T(8,128)(2,1)S(1)}, u32[]{:S(2)}, u32[]{:S(2)}) collective-permute-start(bf16[1024,512]{1,0:T(8,128)(2,1)} %add_columns.2), channel_id=1, source_target_pairs={{0,2},{1,3},{2,0},{3,1},{4,6},{5,7},{6,4},{7,5},{8,10},{9,11},{10,... | collective-permute-start | bytes 3145736 | tf_op jit(solution)/shard_map/ppermute | solution.py:726
  113.2 19.6 %collective-permute-start.15 = (bf16[2,128,1024]{2,1,0:T(8,128)(2,1)}, bf16[2,128,1024]{2,1,0:T(8,128)(2,1)}, u32[]{:S(2)}, u32[]{:S(2)}) collective-permute-start(bf16[2,128,1024]{2,1,0:T(8,128)(2,1)} %get-tuple-element.121), channel_id=1, source_target_pairs={{0,8},{4,12},{8,0},{12,4},{16,24},{20,28},{24,16},{28,20},{1,9},{5... | collective-permute-start | bytes 1572872 | tf_op jit(solution)/shard_map/ppermute | solution.py:726
  115.5 11.9 %collective-permute-start.14 = (bf16[1,64,2048]{2,1,0:T(8,128)(2,1)}, bf16[1,64,2048]{2,1,0:T(8,128)(2,1)}, u32[]{:S(2)}, u32[]{:S(2)}) collective-permute-start(bf16[1,64,2048]{2,1,0:T(8,128)(2,1)} %get-tuple-element.118), channel_id=1, source_target_pairs={{0,4},{4,0},{8,12},{12,8},{16,20},{20,16},{24,28},{28,24},{1,5},{5... | collective-permute-start | bytes 786440 | tf_op jit(solution)/shard_map/ppermute | solution.py:726
  117.1 13.5 %collective-permute-start.13 = (bf16[1,64,2048]{2,1,0:T(8,128)(2,1)}, bf16[1,64,2048]{2,1,0:T(8,128)(2,1)}, u32[]{:S(2)}, u32[]{:S(2)}) collective-permute-start(bf16[1,64,2048]{2,1,0:T(8,128)(2,1)} %get-tuple-element.116), channel_id=1, source_target_pairs={{0,16},{4,20},{8,24},{12,28},{16,0},{20,4},{24,8},{28,12},{1,17},{... | collective-permute-start | bytes 786440 | tf_op jit(solution)/shard_map/ppermute | solution.py:726
  118.6 24.1 %copy-start.4 = (bf16[2,128,1024]{2,1,0:T(8,128)(2,1)S(1)}, bf16[2,128,1024]{2,1,0:T(8,128)(2,1)}, u32[]{:S(2)}) copy-start(bf16[2,128,1024]{2,1,0:T(8,128)(2,1)} %get-tuple-element.143) | copy-start | bytes 1572868
  134.4 3.0 %collective-permute-start.16 = (bf16[1024,512]{1,0:T(8,128)(2,1)}, bf16[1024,512]{1,0:T(8,128)(2,1)}, u32[]{:S(2)}, u32[]{:S(2)}) collective-permute-start(bf16[1024,512]{1,0:T(8,128)(2,1)} %get-tuple-element.122), channel_id=1, source_target_pairs={{0,1},{1,0},{2,3},{3,2},{4,5},{5,4},{6,7},{7,6},{8,9},{9,8},{10,11... | collective-permute-start | bytes 3145736 | tf_op jit(solution)/shard_map/ppermute | solution.py:726
  141.2 46.6 %collective-permute-start.26 = (bf16[1024,512]{1,0:T(8,128)(2,1)}, bf16[1024,512]{1,0:T(8,128)(2,1)}, u32[]{:S(2)}, u32[]{:S(2)}) collective-permute-start(bf16[1024,512]{1,0:T(8,128)(2,1)} %add_columns.3), channel_id=1, source_target_pairs={{0,2},{1,3},{2,0},{3,1},{4,6},{5,7},{6,4},{7,5},{8,10},{9,11},{10,... | collective-permute-start | bytes 3145736 | tf_op jit(solution)/shard_map/ppermute | solution.py:726
  144.5 14.6 %collective-permute-start.18 = (bf16[1,128,1024]{2,1,0:T(8,128)(2,1)}, bf16[1,128,1024]{2,1,0:T(8,128)(2,1)}, u32[]{:S(2)}, u32[]{:S(2)}) collective-permute-start(bf16[1,128,1024]{2,1,0:T(8,128)(2,1)} %get-tuple-element.130), channel_id=1, source_target_pairs={{0,16},{4,20},{8,24},{12,28},{16,0},{20,4},{24,8},{28,12},{1,17},{... | collective-permute-start | bytes 786440 | tf_op jit(solution)/shard_map/ppermute | solution.py:726
  145.8 13.4 %copy-start.6 = (bf16[1,128,1024]{2,1,0:T(8,128)(2,1)S(1)}, bf16[1,128,1024]{2,1,0:T(8,128)(2,1)}, u32[]{:S(2)}) copy-start(bf16[1,128,1024]{2,1,0:T(8,128)(2,1)} %get-tuple-element.132) | copy-start | bytes 786436
  145.8 18.4 %collective-permute-start.17 = (bf16[64,2048]{1,0:T(8,128)(2,1)S(1)}, bf16[64,2048]{1,0:T(8,128)(2,1)}, u32[]{:S(2)}, u32[]{:S(2)}) collective-permute-start(bf16[64,2048]{1,0:T(8,128)(2,1)S(1)} %add_bitcast_fusion.1.refs_2_), channel_id=1, source_target_pairs={{0,4},{4,8},{8,12},{12,16},{16,20},{20,24},{24,28},{1,5},{5,9},{9,... | collective-permute-start | bytes 786440 | tf_op jit(solution)/shard_map/ppermute | solution.py:722
  160.2 12.6 %collective-permute-start.19 = (bf16[64,1024]{1,0:T(8,128)(2,1)S(1)}, bf16[64,1024]{1,0:T(8,128)(2,1)S(1)}, u32[]{:S(2)}, u32[]{:S(2)}) collective-permute-start(bf16[64,1024]{1,0:T(8,128)(2,1)S(1)} %get-tuple-element.158.refs_2_), channel_id=1, source_target_pairs={{0,4},{4,8},{8,12},{12,16},{16,20},{20,24},{24,28},{1,5},{5,9},{9,... | collective-permute-start | bytes 393224 | tf_op jit(solution)/shard_map/ppermute | solution.py:722
  164.2 8.6 %copy-start.2 = (s32[16]{0:T(128)S(1)}, s32[16]{0:T(128)}, u32[]{:S(2)}) copy-start(s32[16]{0:T(128)} %start_ref.2) | copy-start | bytes 196
  172.8 2.2 %copy-start = (bf16[1024,2048]{1,0:T(8,128)(2,1)S(1)}, bf16[1024,2048]{1,0:T(8,128)(2,1)}, u32[]{:S(2)}) copy-start(bf16[1024,2048]{1,0:T(8,128)(2,1)} %get-tuple-element.112.y_ref) | copy-start | bytes 12582916
  175.0 4.9 %copy-start.18 = (bf16[1024,256]{1,0:T(8,128)(2,1)S(1)}, bf16[1024,256]{1,0:T(8,128)(2,1)}, u32[]{:S(2)}) copy-start(bf16[1024,256]{1,0:T(8,128)(2,1)} %get-tuple-element.124) | copy-start | bytes 1572868
  175.0 5.4 %copy-start.17 = (bf16[1024,256]{1,0:T(8,128)(2,1)S(1)}, bf16[1024,256]{1,0:T(8,128)(2,1)}, u32[]{:S(2)}) copy-start(bf16[1024,256]{1,0:T(8,128)(2,1)} %get-tuple-element.125) | copy-start | bytes 1572868
  175.0 5.5 %copy-start.16 = (bf16[1024,256]{1,0:T(8,128)(2,1)S(1)}, bf16[1024,256]{1,0:T(8,128)(2,1)}, u32[]{:S(2)}) copy-start(bf16[1024,256]{1,0:T(8,128)(2,1)} %get-tuple-element.126) | copy-start | bytes 1572868
  175.0 6.4 %copy-start.15 = (bf16[1024,256]{1,0:T(8,128)(2,1)S(1)}, bf16[1024,256]{1,0:T(8,128)(2,1)}, u32[]{:S(2)}) copy-start(bf16[1024,256]{1,0:T(8,128)(2,1)} %get-tuple-element.127) | copy-start | bytes 1572868
  175.0 9.4 %copy-start.1 = (bf16[1024,1024]{1,0:T(8,128)(2,1)S(1)}, bf16[1024,1024]{1,0:T(8,128)(2,1)}, u32[]{:S(2)}) copy-start(bf16[1024,1024]{1,0:T(8,128)(2,1)} %project.3.refs_0_.refs_1_.refs_2_.refs_3_) | copy-start | bytes 6291460
  179.8 1.6 collective-permute-start.20
  179.9 2.3 %collective-permute-start.22 = (bf16[1024,256]{1,0:T(8,128)(2,1)S(1)}, bf16[1024,256]{1,0:T(8,128)(2,1)S(1)}, u32[]{:S(2)}, u32[]{:S(2)}) collective-permute-start(bf16[1024,256]{1,0:T(8,128)(2,1)S(1)} %copy-done.18), channel_id=1, source_target_pairs={{0,1},{1,0},{2,3},{3,2},{4,5},{5,4},{6,7},{7,6},{8,9},{9,8},{10,11... | collective-permute-start | bytes 1572872 | tf_op jit(solution)/shard_map/ppermute | solution.py:726
  180.4 2.5 %collective-permute-start.23 = (bf16[1024,256]{1,0:T(8,128)(2,1)S(1)}, bf16[1024,256]{1,0:T(8,128)(2,1)S(1)}, u32[]{:S(2)}, u32[]{:S(2)}) collective-permute-start(bf16[1024,256]{1,0:T(8,128)(2,1)S(1)} %copy-done.17), channel_id=1, source_target_pairs={{0,1},{1,0},{2,3},{3,2},{4,5},{5,4},{6,7},{7,6},{8,9},{9,8},{10,11... | collective-permute-start | bytes 1572872 | tf_op jit(solution)/shard_map/ppermute | solution.py:726
  180.5 3.2 %collective-permute-start.24 = (bf16[1024,256]{1,0:T(8,128)(2,1)S(1)}, bf16[1024,256]{1,0:T(8,128)(2,1)S(1)}, u32[]{:S(2)}, u32[]{:S(2)}) collective-permute-start(bf16[1024,256]{1,0:T(8,128)(2,1)S(1)} %copy-done.16), channel_id=1, source_target_pairs={{0,1},{1,0},{2,3},{3,2},{4,5},{5,4},{6,7},{7,6},{8,9},{9,8},{10,11... | collective-permute-start | bytes 1572872 | tf_op jit(solution)/shard_map/ppermute | solution.py:726
  181.4 3.0 %collective-permute-start.25 = (bf16[1024,256]{1,0:T(8,128)(2,1)S(1)}, bf16[1024,256]{1,0:T(8,128)(2,1)S(1)}, u32[]{:S(2)}, u32[]{:S(2)}) collective-permute-start(bf16[1024,256]{1,0:T(8,128)(2,1)S(1)} %copy-done.15), channel_id=1, source_target_pairs={{0,1},{1,0},{2,3},{3,2},{4,5},{5,4},{6,7},{7,6},{8,9},{9,8},{10,11... | collective-permute-start | bytes 1572872 | tf_op jit(solution)/shard_map/ppermute | solution.py:726
  182.2 5.5 %collective-permute-start.21 = (bf16[512,128]{1,0:T(8,128)(2,1)S(1)}, bf16[512,128]{1,0:T(8,128)(2,1)S(1)}, u32[]{:S(2)}, u32[]{:S(2)}) collective-permute-start(bf16[512,128]{1,0:T(8,128)(2,1)S(1)} %get-tuple-element.135), channel_id=1, source_target_pairs={{0,2},{1,3},{2,0},{3,1},{4,6},{5,7},{6,4},{7,5},{8,10},{9,11},{10,... | collective-permute-start | bytes 393224 | tf_op jit(solution)/shard_map/ppermute | solution.py:726

commit v3 on v2

--- a/solution.py
+++ b/solution.py
@@ -2,6 +2,8 @@
 
 import jax
 import jax.numpy as jnp
+import ml_dtypes
+import numpy as np
 from jax import lax
 from jax.experimental import pallas as pl
 from jax.experimental.pallas import tpu as pltpu
@@ -14,7 +16,9 @@
 TURN_DEV = 2
 HALO = 16
 LANES = 128
-PIECES = 4
+PIECES = 2
+STATE_BLOCKS = 2
+FINAL_BLOCKS = 2
 Y_UNITS = 4
 Y_FIRST = 2
 
@@ -90,79 +94,74 @@
     )(*arrays)
 
 
-def turn_home(place, bits, slot, count, panel_index, tenants, me):
+def panel_home(place, panel_index, tenants, me, *, bits, slot, count):
     relative = 0
     for order, bit in enumerate(bits):
-        relative = relative + bit * (1 - (place >> (len(bits) - 1 - order)) % 2)
+        relative += bit * (1 - (place >> (len(bits) - 1 - order)) % 2)
     panel = panel_index[tenants[TURN_DEV * (relative ^ me) + slot]]
     owned = lax.div(panel, count) == me
     return jnp.where(owned, lax.rem(panel, count), 0), owned
 
 
-def place_panel(in_ref, out_ref, first, owned):
-    rows = slice(first, first + in_ref.shape[1])
-
-    @pl.when(owned)
-    def _():
-        out_ref[0, rows, :] = in_ref[0]
-
-    @pl.when(jnp.logical_not(owned))
-    def _():
-        out_ref[0, rows, :] = jnp.zeros_like(in_ref[0])
-
-
-def panel_kernel(homes, index_ref, tenant_ref, me_ref, *refs):
-    place = pl.program_id(0)
-    half = pl.num_programs(0) // 2
-    ins = list(refs[: sum(len(job) for job in homes)])
-    outs = refs[len(ins) :]
+def panel_kernel(homes, devices, index_ref, tenant_ref, me_ref, *refs):
+    ins, outs = refs[: len(homes)], refs[len(homes) : 3 * len(homes)]
+    zeros, sems = refs[-2:]
+    zeros[...] = jnp.zeros_like(zeros)
+    half = devices // 2
+    started = []
     for number, job in enumerate(homes):
-        send_ref, keep_ref = outs[2 * number : 2 * number + 2]
-        for slot, home in enumerate(job):
-            in_ref = ins.pop(0)
-            owned = home(place, index_ref, tenant_ref, me_ref[0])[1]
-            first = slot * in_ref.shape[1]
-
-            @pl.when(place < half)
-            def _(in_ref=in_ref, send_ref=send_ref, owned=owned, first=first):
-                place_panel(in_ref, send_ref, first, owned)
-
-            @pl.when(place >= half)
-            def _(in_ref=in_ref, keep_ref=keep_ref, owned=owned, first=first):
-                place_panel(in_ref, keep_ref, first, owned)
+        in_ref = ins[number]
+        rows, width = in_ref.shape[1:]
+        for place in range(devices):
+            out_ref = outs[2 * number + (place >= half)]
+            for slot, home in enumerate(job):
+                local, owned = home(place, index_ref, tenant_ref, me_ref[0])
+                out = out_ref.at[place % half, pl.ds(slot * rows, rows), :]
+                sem = sems.at[len(started)]
+                own = pltpu.make_async_copy(in_ref.at[local], out, sem)
+                none = pltpu.make_async_copy(zeros.at[pl.ds(0, rows), pl.ds(0, width)], out, sem)
+
+                @pl.when(owned)
+                def _(own=own):
+                    own.start()
+
+                @pl.when(jnp.logical_not(owned))
+                def _(none=none):
+                    none.start()
+
+                started.append(none)
+    for copy in started:
+        copy.wait()
 
 
 def pack_panels(jobs, panel_index, tenants, me, devices):
     half = devices // 2
-    homes, ins, in_specs, out_specs, out_shape = [], [], [], [], []
+    homes, out_shape, copies = [], [], 0
     for panels, bits, slots in jobs:
         count, rows, width = panels.shape
-        homes.append([])
-        for slot in slots:
-
-            def home(place, index, tenant, own, bits=bits, slot=slot, count=count):
-                return turn_home(place, bits, slot, count, index, tenant, own)
-
-            def at(q, index, tenant, own, home=home):
-                return (home(q, index, tenant, own[0])[0], 0, 0)
-
-            homes[-1].append(home)
-            ins.append(panels)
-            in_specs.append(pl.BlockSpec((1, rows, width), at))
-        block = (1, len(slots) * rows, width)
-        out_specs.append(pl.BlockSpec(block, lambda q, index, tenant, own: (jnp.minimum(q, half - 1), 0, 0)))
-        out_specs.append(pl.BlockSpec(block, lambda q, index, tenant, own: (jnp.maximum(q - half, 0), 0, 0)))
-        out_shape += [jax.ShapeDtypeStruct((half,) + block[1:], BF16)] * 2
+        homes.append(
+            [
+                functools.partial(panel_home, bits=bits, slot=slot, count=count)
+                for slot in slots
+            ]
+        )
+        out_shape += [jax.ShapeDtypeStruct((half, len(slots) * rows, width), BF16)] * 2
+        copies += devices * len(slots)
+    zero_shape = tuple(max(panels.shape[axis] for panels, _, _ in jobs) for axis in (1, 2))
     outs = pl.pallas_call(
-        functools.partial(panel_kernel, homes),
+        functools.partial(panel_kernel, homes, devices),
         grid_spec=pltpu.PrefetchScalarGridSpec(
-            num_scalar_prefetch=3, grid=(devices,), in_specs=in_specs, out_specs=out_specs
+            num_scalar_prefetch=3,
+            grid=(1,),
+            in_specs=[pl.BlockSpec(job[0].shape, lambda i, *_: (0, 0, 0)) for job in jobs],
+            out_specs=[pl.BlockSpec(memory_space=pl.ANY)] * len(out_shape),
+            scratch_shapes=[pltpu.VMEM(zero_shape, BF16), pltpu.SemaphoreType.DMA((copies,))],
         ),
         out_shape=out_shape,
         compiler_params=params(62),
         cost_estimate=cost(5),
         name="pack_panels",
-    )(panel_index, tenants, me, *ins)
+    )(panel_index, tenants, me, *[job[0] for job in jobs])
     return [outs[2 * job : 2 * job + 2] for job in range(len(jobs))]
 
 
@@ -193,51 +192,58 @@
     rest = change - first.astype(F32)
     second = rest.astype(BF16)
     third = (rest - second.astype(F32)).astype(BF16)
+    terms = jnp.concatenate([first, second, third], axis=0)
     upper = (
         lax.broadcasted_iota(jnp.int32, (Q, Q), 0) <= lax.broadcasted_iota(jnp.int32, (Q, Q), 1)
     ).astype(F32).astype(BF16)
-    sums = jnp.dot(jnp.concatenate([first, second, third], axis=0), upper, preferred_element_type=F32)
-    run = sums[:heads] + sums[heads : 2 * heads] + sums[2 * heads :]
-    run_ref[...] = run
-    shifted_ref[...] = jnp.log(step) - run
-    last = run[:, Q - 1 : Q]
-    tail = jnp.exp(last - run) * step
-    whole = jnp.broadcast_to(jnp.exp(last), (heads, Q))
-    columns = pad_rows(jnp.concatenate([*two_terms(tail), *two_terms(whole)], axis=0)).T
     spread = spread_ref[...]
-    weight[...] = jnp.dot(columns[:, : 2 * heads].astype(BF16), spread, preferred_element_type=F32)
-    decay_row = jnp.dot(
-        columns[:16, 2 * heads : 4 * heads].astype(BF16), spread, preferred_element_type=F32
-    )[:8]
+    parts = [slice(part * Q, (part + 1) * Q) for part in range(STATE_BLOCKS)]
+    decay_rows = []
+    for rows in parts:
+        sums = jnp.dot(terms[:, rows], upper, preferred_element_type=F32)
+        run = sums[:heads] + sums[heads : 2 * heads] + sums[2 * heads :]
+        run_ref[:, rows] = run
+        shifted_ref[:, rows] = jnp.log(step[:, rows]) - run
+        last = run[:, Q - 1 : Q]
+        tail = jnp.exp(last - run) * step[:, rows]
+        whole = jnp.broadcast_to(jnp.exp(last), (heads, Q))
+        columns = pad_rows(jnp.concatenate([*two_terms(tail), *two_terms(whole)], axis=0)).T
+        weight[rows, :] = jnp.dot(
+            columns[:, : 2 * heads].astype(BF16), spread, preferred_element_type=F32
+        )
+        decay_rows.append(
+            jnp.dot(columns[:16, 2 * heads : 4 * heads].astype(BF16), spread, preferred_element_type=F32)[:8]
+        )
 
     bc = conv_rows(b_ref[...].astype(F32), b_prev[...], bt_ref[...].astype(F32))
-    b_prev[...] = b_ref[Q - HALO :, :].astype(F32)[8:]
+    b_prev[...] = b_ref[STATE_BLOCKS * Q - HALO :, :].astype(F32)[8:]
     bc_ref[...] = bc
 
     def conv_lanes(part, carried):
         lanes = pl.ds(pl.multiple_of(part * LANES, LANES), LANES)
         current = x_ref[:, lanes].astype(F32)
         xc = conv_rows(current, x_prev[:, lanes], xt_ref[:, lanes].astype(F32))
-        x_prev[:, lanes] = current[Q - 8 :]
+        x_prev[:, lanes] = current[STATE_BLOCKS * Q - 8 :]
         xc_ref[:, lanes] = xc
         x_weighted[:, lanes] = (xc.astype(F32) * weight[:, lanes]).astype(BF16)
         return carried
 
     lax.fori_loop(0, inner // LANES, conv_lanes, 0, unroll=16)
 
-    start_ref[...] = decay_product[...]
-    decay_product[...] = decay_product[...] * decay_row
-    for group in range(groups):
-        lanes = slice(group * width, (group + 1) * width)
-        fresh = lax.dot_general(
-            bc[:, group * N : (group + 1) * N],
-            x_weighted[:, lanes],
-            (((0,), (0,)), ((), ())),
-            preferred_element_type=F32,
-        )
-        held = state[:, lanes]
-        before_ref[:, lanes] = held.astype(BF16)
-        state[:, lanes] = held * decay_row[:1, lanes] + fresh
+    for part, (rows, decay_row) in enumerate(zip(parts, decay_rows)):
+        start_ref[part * 8 : (part + 1) * 8, :] = decay_product[...]
+        decay_product[...] = decay_product[...] * decay_row
+        for group in range(groups):
+            lanes = slice(group * width, (group + 1) * width)
+            fresh = lax.dot_general(
+                bc[rows, group * N : (group + 1) * N],
+                x_weighted[rows, lanes],
+                (((0,), (0,)), ((), ())),
+                preferred_element_type=F32,
+            )
+            held = state[:, lanes]
+            before_ref[part * N : (part + 1) * N, lanes] = held.astype(BF16)
+            state[:, lanes] = held * decay_row[:1, lanes] + fresh
 
     @pl.when(block == pl.num_programs(0) - 1)
     def _():
@@ -256,6 +262,7 @@
     heads = raw.shape[0]
     blocks = tokens // Q
     half = inner // 2
+    span = STATE_BLOCKS * Q
     whole = lambda c, p: (0, 0)
     rows = lambda c, p: (c, 0)
     columns = lambda c, p: (0, c)
@@ -263,33 +270,33 @@
         state_kernel,
         grid_spec=pltpu.PrefetchScalarGridSpec(
             num_scalar_prefetch=1,
-            grid=(blocks,),
+            grid=(blocks // STATE_BLOCKS,),
             in_specs=[
-                pl.BlockSpec((Q, inner), rows),
-                pl.BlockSpec((Q, bc_width), rows),
+                pl.BlockSpec((span, inner), rows),
+                pl.BlockSpec((span, bc_width), rows),
                 pl.BlockSpec(halos[0].shape, whole),
                 pl.BlockSpec(halos[0].shape, whole),
-                pl.BlockSpec((heads, Q), columns),
+                pl.BlockSpec((heads, span), columns),
                 pl.BlockSpec((1, heads), whole),
                 pl.BlockSpec((K, inner), whole),
                 pl.BlockSpec((K, bc_width), whole),
                 pl.BlockSpec(spread.shape, whole),
             ],
             out_specs=[
-                pl.BlockSpec((Q, inner), rows),
-                pl.BlockSpec((Q, bc_width), rows),
-                pl.BlockSpec((heads, Q), columns),
-                pl.BlockSpec((heads, Q), columns),
-                pl.BlockSpec((N, inner), rows),
-                pl.BlockSpec((8, inner), rows),
+                pl.BlockSpec((span, inner), rows),
+                pl.BlockSpec((span, bc_width), rows),
+                pl.BlockSpec((heads, span), columns),
+                pl.BlockSpec((heads, span), columns),
+                pl.BlockSpec((STATE_BLOCKS * N, inner), rows),
+                pl.BlockSpec((STATE_BLOCKS * 8, inner), rows),
                 pl.BlockSpec((N + HALO, half), whole),
                 pl.BlockSpec((N + HALO, half), whole),
             ],
             scratch_shapes=[
                 pltpu.VMEM((8, inner), F32),
                 pltpu.VMEM((8, bc_width), F32),
-                pltpu.VMEM((Q, inner), F32),
-                pltpu.VMEM((Q, inner), BF16),
+                pltpu.VMEM((span, inner), F32),
+                pltpu.VMEM((span, inner), BF16),
                 pltpu.VMEM((N, inner), F32),
                 pltpu.VMEM((8, inner), F32),
             ],
@@ -507,26 +514,6 @@
     )(parity, head, part, scale, cc, keep, got, gain, weight)
 
 
-def add_kernel(left_ref, right_ref, out_ref):
-    out_ref[...] = (left_ref[...].astype(F32) + right_ref[...].astype(F32)).astype(BF16)
-
-
-def add_columns(left, right, first, count, unit):
-    tokens = left.shape[0]
-    tile = 512
-    spec = pl.BlockSpec((tile, unit), lambda i, j: (i, first + j))
-    return pl.pallas_call(
-        add_kernel,
-        grid=(tokens // tile, count),
-        in_specs=[spec, spec],
-        out_specs=pl.BlockSpec((tile, unit), lambda i, j: (i, j)),
-        out_shape=jax.ShapeDtypeStruct((tokens, count * unit), BF16),
-        compiler_params=params(62),
-        cost_estimate=cost(1),
-        name="add_columns",
-    )(left, right)
-
-
 def place_of(blocks):
     def column(step, head):
         column = (head ^ blocks[0][0]) * Y_UNITS + blocks[0][1]
@@ -537,72 +524,47 @@
     return column
 
 
-def project_kernel(apart, head_ref, y_ref, w_ref, *outs):
+def rest_kernel(counts, head_ref, y_ref, w_ref, *outs):
     step = pl.program_id(0)
-    if not apart:
-        outs[0][...] = jnp.dot(y_ref[...], w_ref[...], preferred_element_type=F32).astype(BF16)
-        return
-    for unit, out_ref in enumerate(outs):
-
-        @pl.when(step == unit)
+    start = 0
+    for count, out_ref in zip(counts, outs):
+
+        @pl.when((step >= start) & (step < start + count))
         def _(out_ref=out_ref):
             out_ref[...] = jnp.dot(y_ref[...], w_ref[...], preferred_element_type=F32).astype(BF16)
 
-
-def project(head, blocks, y, weight, width, apart):
+        start += count
+
+
+def project_rest(head, sides, y, weight, width, microseconds):
     tokens, inner = y.shape
-    units = len(blocks)
+    counts = [len(side) for side in sides]
+    blocks = [block for side in sides for block in side]
     place = place_of(blocks)
-    if apart:
-        out_specs = [pl.BlockSpec((tokens, width), lambda i, p: (0, 0))] * units
-        out_shape = [jax.ShapeDtypeStruct((tokens, width), BF16)] * units
-    else:
-        out_specs = [pl.BlockSpec((tokens, width), lambda i, p: (0, i))]
-        out_shape = [jax.ShapeDtypeStruct((tokens, units * width), BF16)]
+    out_specs, start = [], 0
+    for count in counts:
+        out_specs.append(
+            pl.BlockSpec(
+                (tokens, width),
+                lambda i, p, start=start, count=count: (0, jnp.clip(i - start, 0, count - 1)),
+            )
+        )
+        start += count
     return pl.pallas_call(
-        functools.partial(project_kernel, apart),
+        functools.partial(rest_kernel, counts),
         grid_spec=pltpu.PrefetchScalarGridSpec(
             num_scalar_prefetch=1,
-            grid=(units,),
+            grid=(len(blocks),),
             in_specs=[
                 pl.BlockSpec((tokens, inner), lambda i, p: (0, 0)),
                 pl.BlockSpec((inner, width), lambda i, p: (0, place(i, p[0]))),
             ],
             out_specs=out_specs,
         ),
-        out_shape=out_shape,
+        out_shape=[jax.ShapeDtypeStruct((tokens, count * width), BF16) for count in counts],
         compiler_params=params(62),
-        cost_estimate=cost(1),
-        name="project",
-    )(head, y, weight)
-
-
-def both_kernel(units, head_ref, y_ref, w_ref, send_ref, keep_ref):
-    project_unit(y_ref, w_ref, send_ref, keep_ref, pl.program_id(0), units)
-
-
-def project_both(head, blocks, y, weight, width):
-    tokens, inner = y.shape
-    units = len(blocks) // 2
-    place = place_of(blocks)
-    return pl.pallas_call(
-        functools.partial(both_kernel, units),
-        grid_spec=pltpu.PrefetchScalarGridSpec(
-            num_scalar_prefetch=1,
-            grid=(2 * units,),
-            in_specs=[
-                pl.BlockSpec((tokens, inner), lambda i, p: (0, 0)),
-                pl.BlockSpec((inner, width), lambda i, p: (0, place(i, p[0]))),
-            ],
-            out_specs=[
-                pl.BlockSpec((tokens, width), lambda i, p: (0, jnp.minimum(i, units - 1))),
-                pl.BlockSpec((tokens, width), lambda i, p: (0, jnp.maximum(i - units, 0))),
-            ],
-        ),
-        out_shape=[jax.ShapeDtypeStruct((tokens, units * width), BF16)] * 2,
-        compiler_params=params(62),
-        cost_estimate=cost(1),
-        name="project_both",
+        cost_estimate=cost(microseconds),
+        name="project_rest",
     )(head, y, weight)
 
 
@@ -623,29 +585,34 @@
 
 def low_kernel(tokens, start_ref, me_ref, y_ref, *refs):
     panels, out_ref = refs[:-1], refs[-1]
-    slot = block_slot(pl.program_id(0), start_ref, me_ref[0], tokens)
-    low = lax.dot_general(
-        y_ref[...], chosen(slot, panels), (((1,), (1,)), ((), ())), preferred_element_type=F32
-    )
-    fold = low.shape[0] // 2
-    out_ref[...] = jnp.concatenate([low[:fold], low[fold:]], axis=1)
+    fold = Q // 2
+    for block in range(FINAL_BLOCKS):
+        slot = block_slot(pl.program_id(0) * FINAL_BLOCKS + block, start_ref, me_ref[0], tokens)
+        low = lax.dot_general(
+            y_ref[block * Q : (block + 1) * Q, :],
+            chosen(slot, panels),
+            (((1,), (1,)), ((), ())),
+            preferred_element_type=F32,
+        )
+        out_ref[block * fold : (block + 1) * fold, :] = jnp.concatenate([low[:fold], low[fold:]], axis=1)
 
 
 def low_part(starts, me, y, panels):
     tokens, inner = y.shape
+    span = FINAL_BLOCKS * Q
     rows = lambda i, s, m: (i, 0)
     whole = lambda i, s, m: (0, 0)
     return pl.pallas_call(
         functools.partial(low_kernel, tokens),
         grid_spec=pltpu.PrefetchScalarGridSpec(
             num_scalar_prefetch=2,
-            grid=(tokens // Q,),
-            in_specs=[pl.BlockSpec((Q, inner), rows)]
+            grid=(tokens // span,),
+            in_specs=[pl.BlockSpec((span, inner), rows)]
             + [pl.BlockSpec(panel.shape, whole) for panel in panels],
-            out_specs=pl.BlockSpec((Q // 2, LANES), rows),
+            out_specs=pl.BlockSpec((span // 2, LANES), rows),
         ),
         out_shape=jax.ShapeDtypeStruct((tokens // 2, LANES), F32),
-        compiler_params=params(),
+        compiler_params=params(62),
         cost_estimate=cost(4),
         name="low_part",
     )(starts, me, y, *panels)
@@ -683,31 +650,34 @@
 def final_kernel(tokens, first, unit, start_ref, me_ref, low_ref, held_ref, *refs):
     panels, parts, out_ref = refs[: TURN_DEV + 1], refs[TURN_DEV + 1 : -1], refs[-1]
     rank = LANES // 2
-    slot = block_slot(pl.program_id(0), start_ref, me_ref[0], tokens)
-    low = low_ref[...].astype(BF16)
-    low = jnp.concatenate([low[:, :rank], low[:, rank:]], axis=0)
-    total = held_ref[...] + jnp.dot(low, chosen(slot, panels), preferred_element_type=F32)
     start = first * unit
-    out_ref[:, :start] = total[:, :start].astype(BF16)
-    rest = total[:, start:]
-    for part in parts:
-        rest = rest + part[...].astype(F32)
-    out_ref[:, start:] = rest.astype(BF16)
+    for block in range(FINAL_BLOCKS):
+        slot = block_slot(pl.program_id(0) * FINAL_BLOCKS + block, start_ref, me_ref[0], tokens)
+        low = low_ref[block * Q // 2 : (block + 1) * Q // 2, :].astype(BF16)
+        low = jnp.concatenate([low[:, :rank], low[:, rank:]], axis=0)
+        rows = slice(block * Q, (block + 1) * Q)
+        total = held_ref[rows, :] + jnp.dot(low, chosen(slot, panels), preferred_element_type=F32)
+        out_ref[rows, :start] = total[:, :start].astype(BF16)
+        rest = total[:, start:]
+        for part in parts:
+            rest = rest + part[rows, :].astype(F32)
+        out_ref[rows, start:] = rest.astype(BF16)
 
 
 def final_sum(starts, me, low, held, panels, parts, first, unit):
     tokens, features = held.shape
+    span = FINAL_BLOCKS * Q
     rows = lambda i, s, m: (i, 0)
     whole = lambda i, s, m: (0, 0)
     return pl.pallas_call(
         functools.partial(final_kernel, tokens, first, unit),
         grid_spec=pltpu.PrefetchScalarGridSpec(
             num_scalar_prefetch=2,
-            grid=(tokens // Q,),
-            in_specs=[pl.BlockSpec((Q // 2, LANES), rows), pl.BlockSpec((Q, features), rows)]
+            grid=(tokens // span,),
+            in_specs=[pl.BlockSpec((span // 2, LANES), rows), pl.BlockSpec((span, features), rows)]
             + [pl.BlockSpec(panel.shape, whole) for panel in panels]
-            + [pl.BlockSpec((Q, part.shape[1]), rows) for part in parts],
-            out_specs=pl.BlockSpec((Q, features), rows),
+            + [pl.BlockSpec((span, part.shape[1]), rows) for part in parts],
+            out_specs=pl.BlockSpec((span, features), rows),
         ),
         out_shape=jax.ShapeDtypeStruct((tokens, features), BF16),
         compiler_params=params(),
@@ -727,7 +697,7 @@
 
 
 def after(value, *earlier):
-    return lax.optimization_barrier((value, *earlier))[0]
+    return lax.optimization_barrier((value, *earlier))[0] if earlier else value
 
 
 def neighbour_edge(edge):
@@ -739,15 +709,14 @@
 
 class Route:
     def __init__(self, bits, send, keep):
-        self.bits, self.send, self.keep = list(bits), send, keep
+        self.bits, self.send, self.held, self.size = list(bits), send, [keep], keep.shape[0]
         self.got = None
 
     def merge(self, *earlier):
-        half = self.keep.shape[0] // 2
-        got = after(self.got, *earlier) if earlier else self.got
-        self.send = self.keep[:half] + got[:half]
-        self.keep = self.keep[half:] + got[half:]
-        self.got = None
+        self.held.append(after(self.got, *earlier))
+        half = self.size // 2
+        self.send = sum(each[each.shape[0] - self.size : each.shape[0] - half] for each in self.held)
+        self.size, self.got = half, None
         return self.send
 
     def step(self, *earlier):
@@ -755,16 +724,13 @@
             return
         if self.got is not None:
             self.merge(*earlier)
-        send = after(self.send, *earlier) if earlier else self.send
-        self.got = swap(send, "ctx", self.bits.pop(0))
+        self.got = swap(after(self.send, *earlier), "ctx", self.bits.pop(0))
 
     def end(self, *earlier):
         while self.bits:
             self.step(*earlier)
-        keep, got = self.keep, self.got
-        if earlier:
-            keep = after(keep, *earlier)
-        return keep[0] + got[0]
+        self.held.append(after(self.got, *earlier))
+        return sum(each[-1] for each in self.held)
 
 
 def unpacked(packed):
@@ -819,20 +785,24 @@
     halos = neighbour_edge(edge)
 
     slots = range(TURN_DEV)
-    packs = pack_panels(
-        [(down, near, slots[1:]), (down, far, slots[:1]), (up, near, slots)],
-        tenant_panel_index, tenant_of_turn, me, devices,
-    )
-    down_late, down_early, ups = [
-        Route(bits, *pack) for bits, pack in zip((near, far, near), packs)
-    ]
+
+    def pack(jobs, *earlier):
+        packs = pack_panels(jobs, tenant_panel_index, tenant_of_turn, after(me, *earlier), devices)
+        return [Route(bits, *each) for (_, bits, _), each in zip(jobs, packs)]
+
+    down_early, down_late, ups = pack(
+        [(down, far, slots[:1]), (down, near, slots[1:]), (up, near, slots)]
+    )
+    packed_first = down_early.send
+    down_early.step()
     down_late.step()
-    down_early.step()
-
-    lane_head = jnp.arange(inner) // P_SIZE
-    spread = (jnp.arange(2 * heads)[:, None] % heads == lane_head[None, :]).astype(BF16)
+
+    lane_head = np.arange(inner) // P_SIZE
+    spread = jnp.asarray(
+        (np.arange(2 * heads)[:, None] % heads == lane_head[None, :]).astype(ml_dtypes.bfloat16)
+    )
     xc, bc, run, shifted, before, start, keep, send = local_states(
-        after(parity_arg, packs[0][0]),
+        after(parity_arg, packed_first),
         input_x_channels,
         input_b_channels,
         halos,
@@ -860,21 +830,17 @@
     total = jnp.where(first, got_state, own_state)
     total_decay = jnp.where(first, got_decay, own_decay)
     total, total_decay = total + total_decay * first_state, total_decay * first_decay
-    early = [down_late.got, down_early.got]
     ups.step(got)
     incoming = jnp.zeros_like(total)
     incoming_decay = jnp.ones_like(total_decay)
-    piece = 1
     for bit in outer:
         sent = packed(total, total_decay)
         got = swap(sent, "ctx", bit)
-        if piece < PIECES - 1:
-            held = mix_piece(piece, held, sent, *early)
-            merged = [held[2]]
-            if bit == outer[-1]:
-                merged += [route.merge(sent) for route in (down_late, down_early)]
-            got = after(got, *merged)
-            piece += 1
+        if bit == outer[0]:
+            got = after(got, down_early.merge(sent), down_late.merge(sent))
+        if bit == outer[-1]:
+            held = mix_piece(1, held, sent)
+            got = after(got, held[2])
         state, decay = unpacked(got)
         upper = (ctx & bit) != 0
         incoming = jnp.where(upper, incoming + incoming_decay * state, incoming)
@@ -883,22 +849,19 @@
             jnp.where(upper, total + total_decay * state, state + decay * total),
             total_decay * decay,
         )
+    down_early.step(held[2])
+    down_late.step(held[2])
     incoming_second = first_state + first_decay * incoming
     back_sent = jnp.where(first, incoming_second, incoming).astype(BF16)
     kept = jnp.where(first, incoming, incoming_second).astype(BF16)
     back = swap(back_sent, "ctx", 1)
-    for route in (down_late, down_early):
-        route.step(back_sent)
-    while piece < PIECES:
-        held = mix_piece(piece, held, back_sent, ups.got)
-        piece += 1
     part, scale, cc = held
 
     chips = range(1, lax.axis_size("head") // 2)
     first, later = range(Y_FIRST), range(Y_FIRST, Y_UNITS)
 
-    def sides(units):
-        return [(2 * chip ^ core, at) for core in (1, 0) for chip in chips for at in units]
+    def side(units, core):
+        return [(2 * chip ^ core, at) for chip in chips for at in units]
 
     parts = []
 
@@ -906,7 +869,8 @@
         from_pair = swap(after(to_pair, *earlier), "head", 1)
         sums = []
         for chip in chips:
-            both = add_columns(mine, from_pair, (chip - 1) * len(units), len(units), unit)
+            columns = slice((chip - 1) * len(units) * unit, chip * len(units) * unit)
+            both = (mine[:, columns].astype(F32) + from_pair[:, columns].astype(F32)).astype(BF16)
             arrived = swap(both, "head", 2 * chip)
             parts.extend((arrived, at - units.start, at) for at in units)
             sums.append(both)
@@ -914,37 +878,41 @@
 
     routes = (down_late, down_early, ups)
     y_normed, to_pair, mine = norm_project(
-        parity_arg, head_arg, sides(first), part, scale, cc, kept, back,
+        parity_arg, head_arg, side(first, 1) + side(first, 0), part, scale, cc, kept, back,
         gated_norm_gain[None], output_weight, unit,
     )
-    sums = send_both(mine, to_pair, first, *[route.got for route in routes])
-    for route in routes:
-        route.step(*sums)
-    to_pair, mine = project_both(after(head_arg, *sums), sides(later), y_normed, output_weight, unit)
+    sums = send_both(mine, to_pair, first, down_early.got, down_late.got, ups.got)
+    down_late.step(*sums)
+    down_early.step(*sums)
+    ups.step(*sums)
+    to_pair, mine, *own_to_pair = project_rest(
+        after(head_arg, *sums),
+        [side(later, 1), side(later, 0)] + [[(1, at)] for at in range(Y_UNITS)],
+        y_normed, output_weight, unit, 1,
+    )
     sums = send_both(
-        mine, to_pair, later, *[arrived for arrived, _, _ in parts], *[route.got for route in routes]
-    )
+        mine, to_pair, later,
+        *[arrived for arrived, _, _ in parts], down_early.got, down_late.got, ups.got,
+    )
+    ups.step(*sums)
     down_second = down_late.end(*sums)
     down_first = down_early.end(*sums)
     down_before = shift_up(down_second, "ctx", 1)
-    ups.step(*sums)
-    to_pair = project(
-        after(head_arg, *sums), [(1, at) for at in range(Y_UNITS)], y_normed, output_weight, unit, True
-    )
-    pair = [swap(each, "head", 1) for each in to_pair]
-    (own,) = project(
-        after(head_arg, *to_pair, down_before, ups.got),
-        [(0, at) for at in range(Y_UNITS)], y_normed, output_weight, unit, False,
-    )
-    up_own = ups.end(*to_pair)
+    pair = [swap(after(each, *sums), "head", 1) for each in own_to_pair]
+    (own,) = project_rest(
+        after(head_arg, down_second, down_first),
+        [[(0, at) for at in range(Y_UNITS)]],
+        y_normed, output_weight, unit, 1,
+    )
+    up_own = ups.end(own)
     rank = up.shape[1]
     up_first, up_second = up_own[:rank], up_own[rank:]
     up_before = shift_up(up_second, "ctx", 1)
     low = low_part(
-        after(turn_first_token, own, up_before), me, y_normed, [down_before, down_first, down_second]
-    )
-    low = low + swap(low, "head", 1)
-    low_sent = low.astype(BF16)
+        after(turn_first_token, own, ups.got), me, y_normed, [down_before, down_first, down_second]
+    )
+    low = low + swap(after(low, up_before), "head", 1)
+    low_sent = after(low.astype(BF16), *[arrived for arrived, _, _ in parts])
     for chip in chips:
         low = low + swap(low_sent, "head", 2 * chip).astype(F32)
     here = [each for each in parts if each[2] in first]

time: 195 us -> 174 us (0.89)
  Pallas kernels: 108 us -> 89.8 us
  waiting for transfers between devices: 26.9 us -> 19.9 us
  other arithmetic: 17.9 us -> 23 us
  local copies, waits for them, and re-layouts: 6.88 us -> 3.67 us
    pallas_call x6 -> x3, Pallas kernels: 40.5 us -> 29.2 us  [the longest x2 23.5 us: project_rest(): pl.pallas_call(functools.partial(rest_kernel, counts), grid_spec=pltpu.Pr...]
    ppermute x23, waiting for transfers between devices: 26.8 us -> 19.9 us  [swap(): lax.ppermute(block, axis, [(i, i ^ bits) for i in range(lax.axis_size(axi...]
    pallas_call x4 -> x2, Pallas kernels: 23 us -> 17.9 us  [mix(): pl.pallas_call(functools.partial(mix_kernel, first, bool(aliased)), grid_...]
    convert_element_type x3 -> x4, other arithmetic: 2.83 us -> 7.88 us  [the longest x2 4.99 us: send_both(): (mine[:, columns].astype(F32) + from_pair[:, columns].astype(F32)).astype...]
    unnamed x38 -> x20, local copies, waits for them, and re-layouts: 6.17 us -> 2.97 us
    pallas_call x1, Pallas kernels: 6.82 us -> 4.72 us  [final_sum(): pl.pallas_call(functools.partial(final_kernel, tokens, first, unit), grid...]
  transfers between devices with their start and end apart: 27 -> 27, of which waited for: 15 -> 11; matrix products, arithmetic and copies ran while one was open for 10% -> 11% of each run, Pallas kernels for 48% -> 48%
where the time goes in v3:
time: 174 us; the launch traced here: 172 us
  Pallas kernels  89.8 us (52%)
  starting transfers between devices  35.7 us (21%)
  other arithmetic  23 us (13%)
  waiting for transfers between devices  19.9 us (11%)
  local copies, waits for them, and re-layouts  3.67 us (2%)
    ppermute x23, starting transfers between devices, swap(): lax.ppermute(block, axis, [(i, i ^ bits) for i in range(lax.axis_size(axi...  24.1 us
    pallas_call x2, Pallas kernels, project_rest(): pl.pallas_call(functools.partial(rest_kernel, counts), grid_spec=pltpu.Pr...  23.5 us
    ppermute x23, waiting for transfers between devices, swap(): lax.ppermute(block, axis, [(i, i ^ bits) for i in range(lax.axis_size(axi...  19.9 us
    pallas_call x2, Pallas kernels, mix(): pl.pallas_call(functools.partial(mix_kernel, first, bool(aliased)), grid_...  17.9 us
    pallas_call x1, Pallas kernels, local_states(): pl.pallas_call(state_kernel, grid_spec=pltpu.PrefetchScalarGridSpec(num_s...  15.3 us
    pallas_call x1, Pallas kernels, norm_project(): pl.pallas_call(functools.partial(norm_kernel, tiles), grid_spec=pltpu.Pre...  14.4 us
    add x5, other arithmetic, merge(): sum((each[each.shape[0] - self.size:each.shape[0] - half] for each in sel...  9.51 us
    ppermute x2, starting transfers between devices, shift_up(): return lax.ppermute(block, axis, route)  8.03 us
  transfers between devices with their start and end apart: 27, of which 11 were waited for; matrix products, arithmetic and copies ran while one was open for 11% of the time, Pallas kernels for 48%

profile of v3, /device:TPU:0, one launch (start us, length us, event | category | flops | bytes accessed | tf_op | source)
XLA Modules:
  0.0 172.3 jit_solution(18433091491688881410)
XLA Ops:
  0.0 1.5 sequence_edge.1
  1.5 2.9 %collective-permute-start.1 = (bf16[16,2560]{1,0:T(8,128)(2,1)}, bf16[16,2560]{1,0:T(8,128)(2,1)S(1)}, u32[]{:S(2)}, u32[]{:S(2)}) collective-permute-start(bf16[16,2560]{1,0:T(8,128)(2,1)} %sequence_edge.1), channel_id=1, source_target_pairs={{0,4},{4,0},{8,12},{12,8},{16,20},{20,16},{24,28},{28,24},{1,5},{5... | collective-permute-start | bytes 245768 | tf_op jit(solution)/shard_map/ppermute | solution.py:705
  5.1 5.7 %pack_panels.1 = (bf16[4,64,2048]{2,1,0:T(8,128)(2,1)}, bf16[4,64,2048]{2,1,0:T(8,128)(2,1)}, bf16[4,64,2048]{2,1,0:T(8,128)(2,1)}, bf16[4,64,2048]{2,1,0:T(8,12...) custom-call(s32[48]{0:T(128)} %index_ref.1, s32[16]{0:T(128)} %tenant_ref.1, s32[1]{0:T(128)} %bitcast.me_ref, ...), custom_call_target="tpu_custom_call" | custom-call | flops 500000 | bytes 1 | tf_op jit(solution)/shard_map/pack_panels/pallas_call | solution.py:151
  10.8 4.3 %collective-permute-start = (bf16[4,64,2048]{2,1,0:T(8,128)(2,1)}, bf16[4,64,2048]{2,1,0:T(8,128)(2,1)}, u32[]{:S(2)}, u32[]{:S(2)}) collective-permute-start(bf16[4,64,2048]{2,1,0:T(8,128)(2,1)} %get-tuple-element.68), channel_id=1, source_target_pairs={{0,4},{4,0},{8,12},{12,8},{16,20},{20,16},{24,28},{28,24},{1,5},{5... | collective-permute-start | bytes 3145736 | tf_op jit(solution)/shard_map/ppermute | solution.py:696
  15.1 1.6 collective-permute-start.5
  17.5 15.3 %local_states.1 = (bf16[1024,2048]{1,0:T(8,128)(2,1)}, bf16[1024,256]{1,0:T(8,128)(2,1)}, f32[32,1024]{1,0:T(8,128)}, f32[32,1024]{1,0:T(8,128)}, bf16[1024,2048...) custom-call(s32[1]{0:T(128)} %bitcast.3.parity_ref, ...), custom_call_target="tpu_custom_call" | custom-call | flops 15000000512 | bytes 1 | tf_op jit(solution)/shard_map/local_states/pallas_call | solution.py:269
  32.9 8.9 %mix.2 = (bf16[1024,2048]{1,0:T(8,128)(2,1)}, bf16[1024,2048]{1,0:T(8,128)(2,1)}, bf16[1024,256]{1,0:T(8,128)(2,1)}) custom-call(s32[1]{0:T(128)} %bitcast.3.parity_ref, bf16[1024,2048]{1,0:T(8,128)(2,1)} %get-tuple-element.73.refs_0_, bf16[1024,256]{1,0:T(8,128)(2,1)} %get-tuple-element.74.refs_1_, bf16[1024,256]{1,0:T(8,128)(2,1)} %refs_3_.3, ...), custom_call_target="tpu_custom_call" | custom-call | flops 10000000000 | bytes 1 | tf_op jit(solution)/shard_map/mix/pallas_call | solution.py:390
  41.8 2.5 %collective-permute-done.3 = bf16[144,1024]{1,0:T(8,128)(2,1)S(1)} collective-permute-done((bf16[144,1024]{1,0:T(8,128)(2,1)}, bf16[144,1024]{1,0:T(8,128)(2,1)S(1)}, u32[]{:S(2)}, u32[]{:S(2)}) %collective-permute-start.3) | collective-permute-done | bytes 294944 | tf_op jit(solution)/shard_map/ppermute | solution.py:696
  44.6 1.6 collective-permute-start.4
  46.2 1.7 %collective-permute-start.10 = (bf16[4,128,1024]{2,1,0:T(8,128)(2,1)}, bf16[4,128,1024]{2,1,0:T(8,128)(2,1)S(1)}, u32[]{:S(2)}, u32[]{:S(2)}) collective-permute-start(bf16[4,128,1024]{2,1,0:T(8,128)(2,1)} %get-tuple-element.98), channel_id=1, source_target_pairs={{0,4},{4,0},{8,12},{12,8},{16,20},{20,16},{24,28},{28,24},{1,5},{5... | collective-permute-start | bytes 3145736 | tf_op jit(solution)/shard_map/ppermute | solution.py:696
  47.9 2.0 %slice_add_fusion.2 = bf16[2,64,2048]{2,1,0:T(8,128)(2,1)} fusion(bf16[4,64,2048]{2,1,0:T(8,128)(2,1)} %collective-permute-done, bf16[4,64,2048]{2,1,0:T(8,128)(2,1)} %get-tuple-element.67), kind=kLoop, calls=%fused_computation.17 | loop fusion | flops 262144 | bytes 1572864 | tf_op jit(solution)/shard_map/add | solution.py:718
  50.0 2.0 %slice_add_fusion.1 = bf16[2,64,2048]{2,1,0:T(8,128)(2,1)} fusion(bf16[4,64,2048]{2,1,0:T(8,128)(2,1)} %collective-permute-done.5, bf16[4,64,2048]{2,1,0:T(8,128)(2,1)} %get-tuple-element.83), kind=kLoop, calls=%fused_computation.16 | loop fusion | flops 262144 | bytes 1572864 | tf_op jit(solution)/shard_map/add | solution.py:718
  52.4 0.8 maximum_maximum_fusion.1
  53.3 2.6 %collective-permute-start.7 = (bf16[144,1024]{1,0:T(8,128)(2,1)}, bf16[144,1024]{1,0:T(8,128)(2,1)}, u32[]{:S(2)}, u32[]{:S(2)}) collective-permute-start(bf16[144,1024]{1,0:T(8,128)(2,1)} %maximum_maximum_fusion.1), channel_id=1, source_target_pairs={{0,16},{4,20},{8,24},{12,28},{16,0},{20,4},{24,8},{28,12},{1,17},{... | collective-permute-start | bytes 884744 | tf_op jit(solution)/shard_map/ppermute | solution.py:696
  55.9 8.9 %mix.3 = (bf16[1024,2048]{1,0:T(8,128)(2,1)}, bf16[1024,2048]{1,0:T(8,128)(2,1)}, bf16[1024,256]{1,0:T(8,128)(2,1)}) custom-call(s32[1]{0:T(128)} %bitcast.3.parity_ref, bf16[1024,2048]{1,0:T(8,128)(2,1)} %get-tuple-element.73.refs_0_, bf16[1024,256]{1,0:T(8,128)(2,1)} %get-tuple-element.74.refs_1_, ...), custom_call_target="tpu_custom_call", output_to_operand_aliasing={{0}: (15, {}), {1}: (16, {}), {2}: (17, {})} | custom-call | flops 10000000000 | bytes 1 | tf_op jit(solution)/shard_map/mix/pallas_call | solution.py:390
  65.3 1.5 collective-permute-start.9
  66.8 1.9 %collective-permute-done.7 = bf16[144,1024]{1,0:T(8,128)(2,1)} collective-permute-done((bf16[144,1024]{1,0:T(8,128)(2,1)}, bf16[144,1024]{1,0:T(8,128)(2,1)}, u32[]{:S(2)}, u32[]{:S(2)}) %collective-permute-start.7) | collective-permute-done | bytes 294944 | tf_op jit(solution)/shard_map/ppermute | solution.py:696
  68.7 1.9 %select_convert_fusion = (bf16[128,1024]{1,0:T(8,128)(2,1)S(1)}, bf16[128,1024]{1,0:T(8,128)(2,1)}) fusion(f32[1024]{0:T(1024)S(1)} %bitcast.26, f32[1024]{0:T(1024)S(1)} %bitcast.25, pred[]{:T(512)S(6)} %ne.14, pred[]{:T(512)S(6)} %ne.13, pred[]{:T(512)S(6)} %eq.5, bf16[144,1024]{1,0:T(8,128)(2,1)} %collective-permute-done.7, ...), kind=kLoop, calls=%fused_computation.13 | loop fusion | flops 1966080 | bytes 1581059 | tf_op jit(solution)/shard_map/convert_element_type | solution.py:855
  70.6 0.9 collective-permute-start.8
  72.2 4.8 %collective-permute-done.8.got_ref = bf16[128,1024]{1,0:T(8,128)(2,1)S(1)} collective-permute-done((bf16[128,1024]{1,0:T(8,128)(2,1)S(1)}, bf16[128,1024]{1,0:T(8,128)(2,1)S(1)}, u32[]{:S(2)}, u32[]{:S(2)}) %collective-permute-start.8) | collective-permute-done | bytes 262176 | tf_op jit(solution)/shard_map/ppermute | solution.py:696
  77.7 14.4 %norm_project.1 = (bf16[1024,2048]{1,0:T(8,128)(2,1)}, bf16[1024,512]{1,0:T(8,128)(2,1)}, bf16[1024,512]{1,0:T(8,128)(2,1)}) custom-call(s32[1]{0:T(128)} %bitcast.3.parity_ref, s32[1]{0:T(128)} %bitcast.1.place_ref.head_ref, bf16[1024,2048]{1,0:T(8,128)(2,1)} %get-tuple-element.91.part_ref, bf16[1024,2048]{1,0:T(8,128)(2,1)} %get-tuple-element.92.scale_ref, ...), custom_call_target="tpu_custom_call" | custom-call | flops 1100000 | bytes 1 | tf_op jit(solution)/shard_map/norm_project/pallas_call | solution.py:485
  92.2 2.9 %collective-permute-done.11 = bf16[1024,512]{1,0:T(8,128)(2,1)S(1)} collective-permute-done((bf16[1024,512]{1,0:T(8,128)(2,1)}, bf16[1024,512]{1,0:T(8,128)(2,1)S(1)}, u32[]{:S(2)}, u32[]{:S(2)}) %collective-permute-start.11) | collective-permute-done | bytes 1048608 | tf_op jit(solution)/shard_map/ppermute | solution.py:696
  95.1 2.5 %add_convert_fusion.1 = bf16[1024,512]{1,0:T(8,128)(2,1)} fusion(bf16[1024,512]{1,0:T(8,128)(2,1)S(1)} %collective-permute-done.11, bf16[1024,512]{1,0:T(8,128)(2,1)} %get-tuple-element.94), kind=kLoop, calls=%fused_computation.1 | loop fusion | flops 2097152 | bytes 3145728 | tf_op jit(solution)/shard_map/convert_element_type | solution.py:873
  97.6 1.5 collective-permute-start.13
  99.1 1.3 slice_add_fusion
  100.4 2.2 %slice_add_fusion.4 = (bf16[1,64,2048]{2,1,0:T(8,128)(2,1)}, bf16[1,64,2048]{2,1,0:T(8,128)(2,1)}) fusion(bf16[2,64,2048]{2,1,0:T(8,128)(2,1)} %collective-permute-done.9, bf16[4,64,2048]{2,1,0:T(8,128)(2,1)} %collective-permute-done.5, bf16[4,64,2048]{2,1,0:T(8,128)(2,1)} %get-tuple-element.83, bf16[2,64,2048]{2,1,0:T(8,128)(2,1)} %collective-permute-done.6, ...), kind=kLoop, calls=%fused_computation.26 | loop fusion | flops 524288 | bytes 2097152 | tf_op jit(solution)/shard_map/add | solution.py:718
  102.7 0.9 collective-permute-start.14
  103.6 3.2 %collective-permute-start.12 = (bf16[1,64,2048]{2,1,0:T(8,128)(2,1)}, bf16[1,64,2048]{2,1,0:T(8,128)(2,1)}, u32[]{:S(2)}, u32[]{:S(2)}) collective-permute-start(bf16[1,64,2048]{2,1,0:T(8,128)(2,1)} %get-tuple-element.101), channel_id=1, source_target_pairs={{0,16},{4,20},{8,24},{12,28},{16,0},{20,4},{24,8},{28,12},{1,17},{... | collective-permute-start | bytes 786440 | tf_op jit(solution)/shard_map/ppermute | solution.py:696
  106.8 15.0 %project_rest.2 = (bf16[1024,512]{1,0:T(8,128)(2,1)}, bf16[1024,512]{1,0:T(8,128)(2,1)}, bf16[1024,256]{1,0:T(8,128)(2,1)}, bf16[1024,256]{1,0:T(8,128)(2,1)}, b...) custom-call(s32[1]{0:T(128)} %bitcast.1.place_ref.head_ref, bf16[1024,2048]{1,0:T(8,128)(2,1)} %get-tuple-element.103.y_ref, ...), custom_call_target="tpu_custom_call" | custom-call | flops 100000 | bytes 1 | tf_op jit(solution)/shard_map/project_rest/pallas_call | solution.py:553
  121.8 1.2 collective-permute-done.13.refs_8_.refs_9_
  123.0 2.9 %collective-permute-done.16 = bf16[1024,512]{1,0:T(8,128)(2,1)S(1)} collective-permute-done((bf16[1024,512]{1,0:T(8,128)(2,1)}, bf16[1024,512]{1,0:T(8,128)(2,1)S(1)}, u32[]{:S(2)}, u32[]{:S(2)}) %collective-permute-start.16) | collective-permute-done | bytes 1048608 | tf_op jit(solution)/shard_map/ppermute | solution.py:696
  125.9 2.5 %add_convert_fusion = bf16[1024,512]{1,0:T(8,128)(2,1)} fusion(bf16[1024,512]{1,0:T(8,128)(2,1)S(1)} %collective-permute-done.16, bf16[1024,512]{1,0:T(8,128)(2,1)} %get-tuple-element.104), kind=kLoop, calls=%fused_computation | loop fusion | flops 2097152 | bytes 3145728 | tf_op jit(solution)/shard_map/convert_element_type | solution.py:873
  128.4 1.5 collective-permute-start.21
  129.9 1.2 add_bitcast_fusion.1.refs_2_
  131.1 1.9 %slice_add_fusion.3 = bf16[1,128,1024]{2,1,0:T(8,128)(2,1)} fusion(bf16[2,128,1024]{2,1,0:T(8,128)(2,1)} %collective-permute-done.15, bf16[4,128,1024]{2,1,0:T(8,128)(2,1)} %copy-done.4, bf16[4,128,1024]{2,1,0:T(8,128)(2,1)} %get-tuple-element.108), kind=kLoop, calls=%fused_computation.23 | loop fusion | flops 262144 | bytes 1048576 | tf_op jit(solution)/shard_map/add | solution.py:718
  133.1 3.9 %collective-permute-start.18 = (bf16[64,2048]{1,0:T(8,128)(2,1)S(1)}, bf16[64,2048]{1,0:T(8,128)(2,1)}, u32[]{:S(2)}, u32[]{:S(2)}) collective-permute-start(bf16[64,2048]{1,0:T(8,128)(2,1)S(1)} %add_bitcast_fusion.1.refs_2_), channel_id=1, source_target_pairs={{0,4},{4,8},{8,12},{12,16},{16,20},{20,24},{24,28},{1,5},{5,9},{9,... | collective-permute-start | bytes 786440 | tf_op jit(solution)/shard_map/ppermute | solution.py:692
  137.0 1.9 %add_bitcast_fusion.refs_1_ = bf16[64,2048]{1,0:T(8,128)(2,1)} fusion(bf16[1,64,2048]{2,1,0:T(8,128)(2,1)S(1)} %collective-permute-done.14, bf16[2,64,2048]{2,1,0:T(8,128)(2,1)} %collective-permute-done.9, bf16[4,64,2048]{2,1,0:T(8,128)(2,1)} %collective-permute-done.5, bf16[4,64,2048]{2,1,0:T(8,128)(2,1)} %get-tuple-element.83), kind=kLoop, calls=%fused_computation.24 | loop fusion | flops 393216 | bytes 1310720 | tf_op jit(solution)/shard_map/add | solution.py:733
  138.8 8.6 %project_rest.3.refs_0_.refs_1_.refs_2_.refs_3_ = bf16[1024,1024]{1,0:T(8,128)(2,1)} custom-call(s32[1]{0:T(128)} %bitcast.1.place_ref.head_ref, bf16[1024,2048]{1,0:T(8,128)(2,1)} %get-tuple-element.103.y_ref, bf16[2048,4096]{1,0:T(8,128)(2,1)} %w_ref.5), custom_call_target="tpu_custom_call" | custom-call | flops 100000 | bytes 1 | tf_op jit(solution)/shard_map/project_rest/pallas_call | solution.py:553
  147.7 1.2 add_add_fusion
  148.9 4.1 %collective-permute-start.19 = (bf16[64,1024]{1,0:T(8,128)(2,1)S(1)}, bf16[64,1024]{1,0:T(8,128)(2,1)S(1)}, u32[]{:S(2)}, u32[]{:S(2)}) collective-permute-start(bf16[64,1024]{1,0:T(8,128)(2,1)S(1)} %get-tuple-element.140.refs_2_), channel_id=1, source_target_pairs={{0,4},{4,8},{8,12},{12,16},{16,20},{20,24},{24,28},{1,5},{5,9},{9,... | collective-permute-start | bytes 393224 | tf_op jit(solution)/shard_map/ppermute | solution.py:692
  153.0 5.8 %low_part.1 = f32[512,128]{1,0:T(8,128)} custom-call(s32[16]{0:T(128)} %start_ref.2, s32[1]{0:T(128)} %bitcast.me_ref, bf16[1024,2048]{1,0:T(8,128)(2,1)} %get-tuple-element.103.y_ref, bf16[64,2048]{1,0:T(8,128)(2,1)} %collective-permute-done.18.refs_0_, bf16[64,2048]{1,0:T(8,128)(2,1)} %add_bitcast_fusion.refs_1_, bf16[64,2048]{1,0:T(8,128)(2,1)} %copy-done.3), custom_call_target="tpu_custom_call" | custom-call | flops 400000 | bytes 1 | tf_op jit(solution)/shard_map/low_part/pallas_call | solution.py:605
  159.9 0.7 collective-permute-done.20
  160.7 1.0 fusion.5
  162.3 1.3 collective-permute-done.24.refs_5_
  163.6 1.6 copy-done
  165.2 1.0 held_sum.1.held_ref
  166.2 1.4 collective-permute-done.22
  167.6 4.7 %final_sum.1 = bf16[1024,1024]{1,0:T(8,128)(2,1)} custom-call(s32[16]{0:T(128)S(1)} %copy-done.1, s32[1]{0:T(128)} %bitcast.me_ref, f32[512,128]{1,0:T(8,128)S(1)} %convert_add_fusion.1.low_ref, f32[1024,1024]{1,0:T(8,128)S(1)} %held_sum.1.held_ref, bf16[64,1024]{1,0:T(8,128)(2,1)S(1)} %collective-permute-done.19.refs_0_, ...), custom_call_target="tpu_custom_call" | custom-call | flops 300000 | bytes 1 | tf_op jit(solution)/shard_map/final_sum/pallas_call | solution.py:672
  (62 shorter events, 6.3 us)
Async XLA Ops:
  1.5 15.3 %collective-permute-start.1 = (bf16[16,2560]{1,0:T(8,128)(2,1)}, bf16[16,2560]{1,0:T(8,128)(2,1)S(1)}, u32[]{:S(2)}, u32[]{:S(2)}) collective-permute-start(bf16[16,2560]{1,0:T(8,128)(2,1)} %sequence_edge.1), channel_id=1, source_target_pairs={{0,4},{4,0},{8,12},{12,8},{16,20},{20,16},{24,28},{28,24},{1,5},{5... | collective-permute-start | bytes 245768 | tf_op jit(solution)/shard_map/ppermute | solution.py:705
  4.4 12.4 %collective-permute-start.2 = (bf16[16,2560]{1,0:T(8,128)(2,1)}, bf16[16,2560]{1,0:T(8,128)(2,1)S(1)}, u32[]{:S(2)}, u32[]{:S(2)}) collective-permute-start(bf16[16,2560]{1,0:T(8,128)(2,1)} %sequence_edge.1), channel_id=1, source_target_pairs={{4,8},{8,4},{12,16},{16,12},{20,24},{24,20},{5,9},{9,5},{13,17},{1... | collective-permute-start | bytes 245768 | tf_op jit(solution)/shard_map/ppermute | solution.py:706
  10.8 37.1 %collective-permute-start = (bf16[4,64,2048]{2,1,0:T(8,128)(2,1)}, bf16[4,64,2048]{2,1,0:T(8,128)(2,1)}, u32[]{:S(2)}, u32[]{:S(2)}) collective-permute-start(bf16[4,64,2048]{2,1,0:T(8,128)(2,1)} %get-tuple-element.68), channel_id=1, source_target_pairs={{0,4},{4,0},{8,12},{12,8},{16,20},{20,16},{24,28},{28,24},{1,5},{5... | collective-permute-start | bytes 3145736 | tf_op jit(solution)/shard_map/ppermute | solution.py:696
  15.1 32.8 %collective-permute-start.5 = (bf16[4,64,2048]{2,1,0:T(8,128)(2,1)}, bf16[4,64,2048]{2,1,0:T(8,128)(2,1)}, u32[]{:S(2)}, u32[]{:S(2)}) collective-permute-start(bf16[4,64,2048]{2,1,0:T(8,128)(2,1)} %get-tuple-element.69), channel_id=1, source_target_pairs={{0,8},{4,12},{8,0},{12,4},{16,24},{20,28},{24,16},{28,20},{1,9},{5... | collective-permute-start | bytes 3145736 | tf_op jit(solution)/shard_map/ppermute | solution.py:696
  16.8 0.6 copy-start.8
  16.8 0.7 copy-start.9
  32.8 11.5 %collective-permute-start.3 = (bf16[144,1024]{1,0:T(8,128)(2,1)}, bf16[144,1024]{1,0:T(8,128)(2,1)S(1)}, u32[]{:S(2)}, u32[]{:S(2)}) collective-permute-start(bf16[144,1024]{1,0:T(8,128)(2,1)} %get-tuple-element.71), channel_id=1, source_target_pairs={{0,4},{4,0},{8,12},{12,8},{16,20},{20,16},{24,28},{28,24},{1,5},{5... | collective-permute-start | bytes 884744 | tf_op jit(solution)/shard_map/ppermute | solution.py:696
  32.9 11.4 %copy-start.2 = (bf16[144,1024]{1,0:T(8,128)(2,1)S(1)}, bf16[144,1024]{1,0:T(8,128)(2,1)}, u32[]{:S(2)}) copy-start(bf16[144,1024]{1,0:T(8,128)(2,1)} %get-tuple-element.81) | copy-start | bytes 884740
  44.6 7.6 %collective-permute-start.4 = (bf16[144,1024]{1,0:T(8,128)(2,1)S(1)}, bf16[144,1024]{1,0:T(8,128)(2,1)S(1)}, u32[]{:S(2)}, u32[]{:S(2)}) collective-permute-start(bf16[144,1024]{1,0:T(8,128)(2,1)S(1)} %maximum_maximum_fusion), channel_id=1, source_target_pairs={{0,8},{4,12},{8,0},{12,4},{16,24},{20,28},{24,16},{28,20},{1,9},{5... | collective-permute-start | bytes 884744 | tf_op jit(solution)/shard_map/ppermute | solution.py:696
  46.2 45.9 %collective-permute-start.10 = (bf16[4,128,1024]{2,1,0:T(8,128)(2,1)}, bf16[4,128,1024]{2,1,0:T(8,128)(2,1)S(1)}, u32[]{:S(2)}, u32[]{:S(2)}) collective-permute-start(bf16[4,128,1024]{2,1,0:T(8,128)(2,1)} %get-tuple-element.98), channel_id=1, source_target_pairs={{0,4},{4,0},{8,12},{12,8},{16,20},{20,16},{24,28},{28,24},{1,5},{5... | collective-permute-start | bytes 3145736 | tf_op jit(solution)/shard_map/ppermute | solution.py:696
  53.3 15.4 %collective-permute-start.7 = (bf16[144,1024]{1,0:T(8,128)(2,1)}, bf16[144,1024]{1,0:T(8,128)(2,1)}, u32[]{:S(2)}, u32[]{:S(2)}) collective-permute-start(bf16[144,1024]{1,0:T(8,128)(2,1)} %maximum_maximum_fusion.1), channel_id=1, source_target_pairs={{0,16},{4,20},{8,24},{12,28},{16,0},{20,4},{24,8},{28,12},{1,17},{... | collective-permute-start | bytes 884744 | tf_op jit(solution)/shard_map/ppermute | solution.py:696
  55.9 15.7 %copy-start.6 = (bf16[2048]{0:T(1024)(128)(2,1)S(1)}, bf16[2048]{0:T(1024)(128)(2,1)}, u32[]{:S(2)}) copy-start(bf16[2048]{0:T(1024)(128)(2,1)} %param.28) | copy-start | bytes 12292
  64.8 27.3 %collective-permute-start.6 = (bf16[2,64,2048]{2,1,0:T(8,128)(2,1)}, bf16[2,64,2048]{2,1,0:T(8,128)(2,1)}, u32[]{:S(2)}, u32[]{:S(2)}) collective-permute-start(bf16[2,64,2048]{2,1,0:T(8,128)(2,1)} %slice_add_fusion.2), channel_id=1, source_target_pairs={{0,8},{4,12},{8,0},{12,4},{16,24},{20,28},{24,16},{28,20},{1,9},{5... | collective-permute-start | bytes 1572872 | tf_op jit(solution)/shard_map/ppermute | solution.py:696
  65.3 26.9 %collective-permute-start.9 = (bf16[2,64,2048]{2,1,0:T(8,128)(2,1)}, bf16[2,64,2048]{2,1,0:T(8,128)(2,1)}, u32[]{:S(2)}, u32[]{:S(2)}) collective-permute-start(bf16[2,64,2048]{2,1,0:T(8,128)(2,1)} %slice_add_fusion.1), channel_id=1, source_target_pairs={{0,16},{4,20},{8,24},{12,28},{16,0},{20,4},{24,8},{28,12},{1,17},{... | collective-permute-start | bytes 1572872 | tf_op jit(solution)/shard_map/ppermute | solution.py:696
  70.6 6.4 %collective-permute-start.8 = (bf16[128,1024]{1,0:T(8,128)(2,1)S(1)}, bf16[128,1024]{1,0:T(8,128)(2,1)S(1)}, u32[]{:S(2)}, u32[]{:S(2)}) collective-permute-start(bf16[128,1024]{1,0:T(8,128)(2,1)S(1)} %get-tuple-element.137), channel_id=1, source_target_pairs={{0,4},{4,0},{8,12},{12,8},{16,20},{20,16},{24,28},{28,24},{1,5},{5... | collective-permute-start | bytes 786440 | tf_op jit(solution)/shard_map/ppermute | solution.py:696
  77.0 0.7 copy-start.5
  92.1 3.0 %copy-start.4 = (bf16[4,128,1024]{2,1,0:T(8,128)(2,1)}, bf16[4,128,1024]{2,1,0:T(8,128)(2,1)S(1)}, u32[]{:S(2)}) copy-start(bf16[4,128,1024]{2,1,0:T(8,128)(2,1)S(1)} %collective-permute-done.10) | copy-start | bytes 3145732
  92.1 2.9 %collective-permute-start.11 = (bf16[1024,512]{1,0:T(8,128)(2,1)}, bf16[1024,512]{1,0:T(8,128)(2,1)S(1)}, u32[]{:S(2)}, u32[]{:S(2)}) collective-permute-start(bf16[1024,512]{1,0:T(8,128)(2,1)} %get-tuple-element.99), channel_id=1, source_target_pairs={{0,1},{1,0},{2,3},{3,2},{4,5},{5,4},{6,7},{7,6},{8,9},{9,8},{10,11... | collective-permute-start | bytes 3145736 | tf_op jit(solution)/shard_map/ppermute | solution.py:696
  97.6 25.4 %collective-permute-start.13 = (bf16[1024,512]{1,0:T(8,128)(2,1)}, bf16[1024,512]{1,0:T(8,128)(2,1)S(1)}, u32[]{:S(2)}, u32[]{:S(2)}) collective-permute-start(bf16[1024,512]{1,0:T(8,128)(2,1)} %add_convert_fusion.1), channel_id=1, source_target_pairs={{0,2},{1,3},{2,0},{3,1},{4,6},{5,7},{6,4},{7,5},{8,10},{9,11},{10,... | collective-permute-start | bytes 3145736 | tf_op jit(solution)/shard_map/ppermute | solution.py:696
  100.4 21.5 %collective-permute-start.15 = (bf16[2,128,1024]{2,1,0:T(8,128)(2,1)S(1)}, bf16[2,128,1024]{2,1,0:T(8,128)(2,1)}, u32[]{:S(2)}, u32[]{:S(2)}) collective-permute-start(bf16[2,128,1024]{2,1,0:T(8,128)(2,1)S(1)} %slice_add_fusion), channel_id=1, source_target_pairs={{0,8},{4,12},{8,0},{12,4},{16,24},{20,28},{24,16},{28,20},{1,9},{5... | collective-permute-start | bytes 1572872 | tf_op jit(solution)/shard_map/ppermute | solution.py:696
  102.7 19.1 %collective-permute-start.14 = (bf16[1,64,2048]{2,1,0:T(8,128)(2,1)}, bf16[1,64,2048]{2,1,0:T(8,128)(2,1)S(1)}, u32[]{:S(2)}, u32[]{:S(2)}) collective-permute-start(bf16[1,64,2048]{2,1,0:T(8,128)(2,1)} %get-tuple-element.107), channel_id=1, source_target_pairs={{0,4},{4,0},{8,12},{12,8},{16,20},{20,16},{24,28},{28,24},{1,5},{5... | collective-permute-start | bytes 786440 | tf_op jit(solution)/shard_map/ppermute | solution.py:696
  103.6 18.2 %collective-permute-start.12 = (bf16[1,64,2048]{2,1,0:T(8,128)(2,1)}, bf16[1,64,2048]{2,1,0:T(8,128)(2,1)}, u32[]{:S(2)}, u32[]{:S(2)}) collective-permute-start(bf16[1,64,2048]{2,1,0:T(8,128)(2,1)} %get-tuple-element.101), channel_id=1, source_target_pairs={{0,16},{4,20},{8,24},{12,28},{16,0},{20,4},{24,8},{28,12},{1,17},{... | collective-permute-start | bytes 786440 | tf_op jit(solution)/shard_map/ppermute | solution.py:696
  123.0 2.9 %collective-permute-start.16 = (bf16[1024,512]{1,0:T(8,128)(2,1)}, bf16[1024,512]{1,0:T(8,128)(2,1)S(1)}, u32[]{:S(2)}, u32[]{:S(2)}) collective-permute-start(bf16[1024,512]{1,0:T(8,128)(2,1)} %get-tuple-element.111), channel_id=1, source_target_pairs={{0,1},{1,0},{2,3},{3,2},{4,5},{5,4},{6,7},{7,6},{8,9},{9,8},{10,11... | collective-permute-start | bytes 3145736 | tf_op jit(solution)/shard_map/ppermute | solution.py:696
  128.4 33.4 %collective-permute-start.21 = (bf16[1024,512]{1,0:T(8,128)(2,1)}, bf16[1024,512]{1,0:T(8,128)(2,1)}, u32[]{:S(2)}, u32[]{:S(2)}) collective-permute-start(bf16[1024,512]{1,0:T(8,128)(2,1)} %add_convert_fusion), channel_id=1, source_target_pairs={{0,2},{1,3},{2,0},{3,1},{4,6},{5,7},{6,4},{7,5},{8,10},{9,11},{10,... | collective-permute-start | bytes 3145736 | tf_op jit(solution)/shard_map/ppermute | solution.py:696
  131.1 16.3 %copy-start.3 = (bf16[64,2048]{1,0:T(8,128)(2,1)}, bf16[64,2048]{1,0:T(8,128)(2,1)S(1)}, u32[]{:S(2)}) copy-start(bf16[64,2048]{1,0:T(8,128)(2,1)S(1)} %add_bitcast_fusion.1.refs_2_) | copy-start | bytes 786436
  133.1 14.6 %collective-permute-start.17 = (bf16[1,128,1024]{2,1,0:T(8,128)(2,1)}, bf16[1,128,1024]{2,1,0:T(8,128)(2,1)S(1)}, u32[]{:S(2)}, u32[]{:S(2)}) collective-permute-start(bf16[1,128,1024]{2,1,0:T(8,128)(2,1)} %slice_add_fusion.3), channel_id=1, source_target_pairs={{0,16},{4,20},{8,24},{12,28},{16,0},{20,4},{24,8},{28,12},{1,17},{... | collective-permute-start | bytes 786440 | tf_op jit(solution)/shard_map/ppermute | solution.py:696
  133.1 20.0 %collective-permute-start.18 = (bf16[64,2048]{1,0:T(8,128)(2,1)S(1)}, bf16[64,2048]{1,0:T(8,128)(2,1)}, u32[]{:S(2)}, u32[]{:S(2)}) collective-permute-start(bf16[64,2048]{1,0:T(8,128)(2,1)S(1)} %add_bitcast_fusion.1.refs_2_), channel_id=1, source_target_pairs={{0,4},{4,8},{8,12},{12,16},{16,20},{20,24},{24,28},{1,5},{5,9},{9,... | collective-permute-start | bytes 786440 | tf_op jit(solution)/shard_map/ppermute | solution.py:692
  148.9 10.0 %collective-permute-start.19 = (bf16[64,1024]{1,0:T(8,128)(2,1)S(1)}, bf16[64,1024]{1,0:T(8,128)(2,1)S(1)}, u32[]{:S(2)}, u32[]{:S(2)}) collective-permute-start(bf16[64,1024]{1,0:T(8,128)(2,1)S(1)} %get-tuple-element.140.refs_2_), channel_id=1, source_target_pairs={{0,4},{4,8},{8,12},{12,16},{16,20},{20,24},{24,28},{1,5},{5,9},{9,... | collective-permute-start | bytes 393224 | tf_op jit(solution)/shard_map/ppermute | solution.py:692
  153.0 7.6 %copy-start.7 = (bf16[1024,256]{1,0:T(8,128)(2,1)S(1)}, bf16[1024,256]{1,0:T(8,128)(2,1)}, u32[]{:S(2)}) copy-start(bf16[1024,256]{1,0:T(8,128)(2,1)} %get-tuple-element.122) | copy-start | bytes 1572868
  158.8 1.7 %collective-permute-start.20 = (f32[512,128]{1,0:T(8,128)}, f32[512,128]{1,0:T(8,128)S(1)}, u32[]{:S(2)}, u32[]{:S(2)}) collective-permute-start(f32[512,128]{1,0:T(8,128)} %low_part.1), channel_id=1, source_target_pairs={{0,1},{1,0},{2,3},{3,2},{4,5},{5,4},{6,7},{7,6},{8,9},{9,8},{10,11... | collective-permute-start | bytes 786440 | tf_op jit(solution)/shard_map/ppermute | solution.py:696
  158.8 3.5 %collective-permute-start.26 = (bf16[1024,256]{1,0:T(8,128)(2,1)}, bf16[1024,256]{1,0:T(8,128)(2,1)S(1)}, u32[]{:S(2)}, u32[]{:S(2)}) collective-permute-start(bf16[1024,256]{1,0:T(8,128)(2,1)} %get-tuple-element.128), channel_id=1, source_target_pairs={{0,1},{1,0},{2,3},{3,2},{4,5},{5,4},{6,7},{7,6},{8,9},{9,8},{10,11... | collective-permute-start | bytes 1572872 | tf_op jit(solution)/shard_map/ppermute | solution.py:696
  159.4 3.0 %collective-permute-start.25 = (bf16[1024,256]{1,0:T(8,128)(2,1)}, bf16[1024,256]{1,0:T(8,128)(2,1)S(1)}, u32[]{:S(2)}, u32[]{:S(2)}) collective-permute-start(bf16[1024,256]{1,0:T(8,128)(2,1)} %get-tuple-element.126), channel_id=1, source_target_pairs={{0,1},{1,0},{2,3},{3,2},{4,5},{5,4},{6,7},{7,6},{8,9},{9,8},{10,11... | collective-permute-start | bytes 1572872 | tf_op jit(solution)/shard_map/ppermute | solution.py:696
  159.4 4.2 %collective-permute-start.24 = (bf16[1024,256]{1,0:T(8,128)(2,1)}, bf16[1024,256]{1,0:T(8,128)(2,1)S(1)}, u32[]{:S(2)}, u32[]{:S(2)}) collective-permute-start(bf16[1024,256]{1,0:T(8,128)(2,1)} %get-tuple-element.124), channel_id=1, source_target_pairs={{0,1},{1,0},{2,3},{3,2},{4,5},{5,4},{6,7},{7,6},{8,9},{9,8},{10,11... | collective-permute-start | bytes 1572872 | tf_op jit(solution)/shard_map/ppermute | solution.py:696
  160.6 3.0 %collective-permute-start.23 = (bf16[1024,256]{1,0:T(8,128)(2,1)S(1)}, bf16[1024,256]{1,0:T(8,128)(2,1)S(1)}, u32[]{:S(2)}, u32[]{:S(2)}) collective-permute-start(bf16[1024,256]{1,0:T(8,128)(2,1)S(1)} %copy-done.7), channel_id=1, source_target_pairs={{0,1},{1,0},{2,3},{3,2},{4,5},{5,4},{6,7},{7,6},{8,9},{9,8},{10,11... | collective-permute-start | bytes 1572872 | tf_op jit(solution)/shard_map/ppermute | solution.py:696
  161.7 5.9 %copy-start.1 = (s32[16]{0:T(128)S(1)}, s32[16]{0:T(128)}, u32[]{:S(2)}) copy-start(s32[16]{0:T(128)} %start_ref.2) | copy-start | bytes 196
  161.7 5.8 %collective-permute-start.22 = (bf16[512,128]{1,0:T(8,128)(2,1)S(1)}, bf16[512,128]{1,0:T(8,128)(2,1)S(1)}, u32[]{:S(2)}, u32[]{:S(2)}) collective-permute-start(bf16[512,128]{1,0:T(8,128)(2,1)S(1)} %get-tuple-element.120), channel_id=1, source_target_pairs={{0,2},{1,3},{2,0},{3,1},{4,6},{5,7},{6,4},{7,5},{8,10},{9,11},{10,... | collective-permute-start | bytes 393224 | tf_op jit(solution)/shard_map/ppermute | solution.py:696
  163.6 1.6 copy-start

commit v4 on v3

--- a/solution.py
+++ b/solution.py
@@ -158,7 +158,7 @@
             scratch_shapes=[pltpu.VMEM(zero_shape, BF16), pltpu.SemaphoreType.DMA((copies,))],
         ),
         out_shape=out_shape,
-        compiler_params=params(62),
+        compiler_params=params(50),
         cost_estimate=cost(5),
         name="pack_panels",
     )(panel_index, tenants, me, *[job[0] for job in jobs])
@@ -311,7 +311,7 @@
             jax.ShapeDtypeStruct((N + HALO, half), BF16),
             jax.ShapeDtypeStruct((N + HALO, half), BF16),
         ],
-        compiler_params=params(62),
+        compiler_params=params(50),
         cost_estimate=cost(150000),
         name="local_states",
     )(parity, x, b, *halos, raw, rate, x_taps, b_taps, spread)
@@ -424,7 +424,7 @@
             jax.ShapeDtypeStruct((tokens, bc_width), BF16),
         ],
         input_output_aliases={15 + i: i for i in range(len(aliased))},
-        compiler_params=params(62),
+        compiler_params=params(50),
         cost_estimate=cost(count * 25000),
         name="mix",
     )(parity, xc, bc, c, c, *halos, run, shifted, before, start, gate, skip, c_taps, spread, *aliased)
@@ -508,7 +508,7 @@
             jax.ShapeDtypeStruct((tokens, units * width), BF16),
             jax.ShapeDtypeStruct((tokens, units * width), BF16),
         ],
-        compiler_params=params(62),
+        compiler_params=params(50),
         cost_estimate=cost(11),
         name="norm_project",
     )(parity, head, part, scale, cc, keep, got, gain, weight)
@@ -562,7 +562,7 @@
             out_specs=out_specs,
         ),
         out_shape=[jax.ShapeDtypeStruct((tokens, count * width), BF16) for count in counts],
-        compiler_params=params(62),
+        compiler_params=params(46),
         cost_estimate=cost(microseconds),
         name="project_rest",
     )(head, y, weight)
@@ -612,7 +612,7 @@
             out_specs=pl.BlockSpec((span // 2, LANES), rows),
         ),
         out_shape=jax.ShapeDtypeStruct((tokens // 2, LANES), F32),
-        compiler_params=params(62),
+        compiler_params=params(46),
         cost_estimate=cost(4),
         name="low_part",
     )(starts, me, y, *panels)

time: 174 us -> 157 us (0.902)
  Pallas kernels: 89.8 us -> 78.4 us
  other arithmetic: 23 us -> 11.9 us
  waiting for transfers between devices: 19.9 us -> 29 us
  local copies, waits for them, and re-layouts: 3.67 us -> 0.19 us
    ppermute x23, waiting for transfers between devices: 19.9 us -> 28.7 us  [swap(): lax.ppermute(block, axis, [(i, i ^ bits) for i in range(lax.axis_size(axi...]
    convert_element_type x2, other arithmetic: 4.99 us -> 0.58 us  [send_both(): (mine[:, columns].astype(F32) + from_pair[:, columns].astype(F32)).astype...]
    pallas_call x2, Pallas kernels: 23.5 us -> 20 us  [project_rest(): pl.pallas_call(functools.partial(rest_kernel, counts), grid_spec=pltpu.Pr...]
    pallas_call x1, Pallas kernels: 5.79 us -> 2.67 us  [low_part(): pl.pallas_call(functools.partial(low_kernel, tokens), grid_spec=pltpu.Pre...]
    unnamed x20 -> x36, local copies, waits for them, and re-layouts: 2.97 us -> 0.08 us
    add x5, other arithmetic: 9.51 us -> 7.17 us  [merge(): sum((each[each.shape[0] - self.size:each.shape[0] - half] for each in sel...]
    ppermute x23, starting transfers between devices: 24.1 us -> 25.9 us  [swap(): lax.ppermute(block, axis, [(i, i ^ bits) for i in range(lax.axis_size(axi...]
  transfers between devices with their start and end apart: 27 -> 27, of which waited for: 11 -> 16; matrix products, arithmetic and copies ran while one was open for 11% -> 7% of each run, Pallas kernels for 48% -> 47%
where the time goes in v4:
time: 157 us; the launch traced here: 156 us
  Pallas kernels  78.4 us (50%)
  starting transfers between devices  36.1 us (23%)
  waiting for transfers between devices  29 us (18%)
  other arithmetic  11.9 us (8%)
    ppermute x23, waiting for transfers between devices, swap(): lax.ppermute(block, axis, [(i, i ^ bits) for i in range(lax.axis_size(axi...  28.7 us
    ppermute x23, starting transfers between devices, swap(): lax.ppermute(block, axis, [(i, i ^ bits) for i in range(lax.axis_size(axi...  25.9 us
    pallas_call x2, Pallas kernels, project_rest(): pl.pallas_call(functools.partial(rest_kernel, counts), grid_spec=pltpu.Pr...  20 us
    pallas_call x2, Pallas kernels, mix(): pl.pallas_call(functools.partial(mix_kernel, first, bool(aliased)), grid_...  16.8 us
    pallas_call x1, Pallas kernels, local_states(): pl.pallas_call(state_kernel, grid_spec=pltpu.PrefetchScalarGridSpec(num_s...  14.7 us
    pallas_call x1, Pallas kernels, norm_project(): pl.pallas_call(functools.partial(norm_kernel, tiles), grid_spec=pltpu.Pre...  13.5 us
    add x5, other arithmetic, merge(): sum((each[each.shape[0] - self.size:each.shape[0] - half] for each in sel...  7.17 us
    ppermute x2, starting transfers between devices, shift_up(): return lax.ppermute(block, axis, route)  6.67 us
  transfers between devices with their start and end apart: 27, of which 16 were waited for; matrix products, arithmetic and copies ran while one was open for 7% of the time, Pallas kernels for 47%

profile of v4, /device:TPU:0, one launch (start us, length us, event | category | flops | bytes accessed | tf_op | source)
XLA Modules:
  0.0 156.0 jit_solution(16222891433335191762)
XLA Ops:
  0.1 1.6 %sequence_edge.1 = bf16[16,2560]{1,0:T(8,128)(2,1)} custom-call(bf16[1024,2048]{1,0:T(8,128)(2,1)} %x_ref.3, bf16[1024,256]{1,0:T(8,128)(2,1)} %b_ref.3, bf16[1024,256]{1,0:T(8,128)(2,1)} %refs_3_.3), custom_call_target="tpu_custom_call" | custom-call | flops 100000 | bytes 1 | tf_op jit(solution)/shard_map/sequence_edge/pallas_call | solution.py:83
  1.7 3.0 %collective-permute-start.1 = (bf16[16,2560]{1,0:T(8,128)(2,1)}, bf16[16,2560]{1,0:T(8,128)(2,1)S(1)}, u32[]{:S(2)}, u32[]{:S(2)}) collective-permute-start(bf16[16,2560]{1,0:T(8,128)(2,1)} %sequence_edge.1), channel_id=1, source_target_pairs={{0,4},{4,0},{8,12},{12,8},{16,20},{20,16},{24,28},{28,24},{1,5},{5... | collective-permute-start | bytes 245768 | tf_op jit(solution)/shard_map/ppermute | solution.py:705
  4.6 0.7 collective-permute-start.2
  5.3 5.0 %pack_panels.1 = (bf16[4,64,2048]{2,1,0:T(8,128)(2,1)}, bf16[4,64,2048]{2,1,0:T(8,128)(2,1)S(1)}, bf16[4,64,2048]{2,1,0:T(8,128)(2,1)}, bf16[4,64,2048]{2,1,0:T(...) custom-call(s32[48]{0:T(128)S(1)} %copy-done.5, s32[16]{0:T(128)S(1)} %copy-done.6, ...), custom_call_target="tpu_custom_call" | custom-call | flops 500000 | bytes 1 | tf_op jit(solution)/shard_map/pack_panels/pallas_call | solution.py:151
  10.3 4.3 %collective-permute-start = (bf16[4,64,2048]{2,1,0:T(8,128)(2,1)}, bf16[4,64,2048]{2,1,0:T(8,128)(2,1)}, u32[]{:S(2)}, u32[]{:S(2)}) collective-permute-start(bf16[4,64,2048]{2,1,0:T(8,128)(2,1)} %get-tuple-element.68), channel_id=1, source_target_pairs={{0,4},{4,0},{8,12},{12,8},{16,20},{20,16},{24,28},{28,24},{1,5},{5... | collective-permute-start | bytes 3145736 | tf_op jit(solution)/shard_map/ppermute | solution.py:696
  14.7 1.6 %collective-permute-start.5 = (bf16[4,64,2048]{2,1,0:T(8,128)(2,1)}, bf16[4,64,2048]{2,1,0:T(8,128)(2,1)}, u32[]{:S(2)}, u32[]{:S(2)}) collective-permute-start(bf16[4,64,2048]{2,1,0:T(8,128)(2,1)} %get-tuple-element.69), channel_id=1, source_target_pairs={{0,8},{4,12},{8,0},{12,4},{16,24},{20,28},{24,16},{28,20},{1,9},{5... | collective-permute-start | bytes 3145736 | tf_op jit(solution)/shard_map/ppermute | solution.py:696
  16.4 14.7 %local_states.1 = (bf16[1024,2048]{1,0:T(8,128)(2,1)}, bf16[1024,256]{1,0:T(8,128)(2,1)S(1)}, f32[32,1024]{1,0:T(8,128)S(1)}, f32[32,1024]{1,0:T(8,128)S(1)}, bf...) custom-call(s32[1]{0:T(128)} %bitcast.3.parity_ref, ...), custom_call_target="tpu_custom_call" | custom-call | flops 15000000512 | bytes 1 | tf_op jit(solution)/shard_map/local_states/pallas_call | solution.py:269
  31.3 8.4 %mix.2 = (bf16[1024,2048]{1,0:T(8,128)(2,1)}, bf16[1024,2048]{1,0:T(8,128)(2,1)}, bf16[1024,256]{1,0:T(8,128)(2,1)S(1)}) custom-call(s32[1]{0:T(128)} %bitcast.3.parity_ref, bf16[1024,2048]{1,0:T(8,128)(2,1)} %get-tuple-element.73.refs_0_, bf16[1024,256]{1,0:T(8,128)(2,1)S(1)} %get-tuple-element.74.refs_1_, bf16[1024,256]{1,0:T(8,128)(2,1)S(1)} %copy-done.3, ...), custom_call_target="tpu_custom_call" | custom-call | flops 10000000000 | bytes 1 | tf_op jit(solution)/shard_map/mix/pallas_call | solution.py:390
  39.7 4.1 %collective-permute-done.3 = bf16[144,1024]{1,0:T(8,128)(2,1)S(1)} collective-permute-done((bf16[144,1024]{1,0:T(8,128)(2,1)S(1)}, bf16[144,1024]{1,0:T(8,128)(2,1)S(1)}, u32[]{:S(2)}, u32[]{:S(2)}) %collective-permute-start.3) | collective-permute-done | bytes 294944 | tf_op jit(solution)/shard_map/ppermute | solution.py:696
  44.1 1.6 %collective-permute-start.4 = (bf16[144,1024]{1,0:T(8,128)(2,1)S(1)}, bf16[144,1024]{1,0:T(8,128)(2,1)S(1)}, u32[]{:S(2)}, u32[]{:S(2)}) collective-permute-start(bf16[144,1024]{1,0:T(8,128)(2,1)S(1)} %maximum_maximum_fusion), channel_id=1, source_target_pairs={{0,8},{4,12},{8,0},{12,4},{16,24},{20,28},{24,16},{28,20},{1,9},{5... | collective-permute-start | bytes 884744 | tf_op jit(solution)/shard_map/ppermute | solution.py:696
  45.7 1.7 %collective-permute-start.10 = (bf16[4,128,1024]{2,1,0:T(8,128)(2,1)}, bf16[4,128,1024]{2,1,0:T(8,128)(2,1)}, u32[]{:S(2)}, u32[]{:S(2)}) collective-permute-start(bf16[4,128,1024]{2,1,0:T(8,128)(2,1)} %get-tuple-element.98), channel_id=1, source_target_pairs={{0,4},{4,0},{8,12},{12,8},{16,20},{20,16},{24,28},{28,24},{1,5},{5... | collective-permute-start | bytes 3145736 | tf_op jit(solution)/shard_map/ppermute | solution.py:696
  47.5 1.9 %slice_add_fusion.2 = bf16[2,64,2048]{2,1,0:T(8,128)(2,1)} fusion(bf16[4,64,2048]{2,1,0:T(8,128)(2,1)} %collective-permute-done, bf16[4,64,2048]{2,1,0:T(8,128)(2,1)S(1)} %copy-done.15), kind=kLoop, calls=%fused_computation.17 | loop fusion | flops 262144 | bytes 1572864 | tf_op jit(solution)/shard_map/add | solution.py:718
  49.4 1.9 %slice_add_fusion.1 = bf16[2,64,2048]{2,1,0:T(8,128)(2,1)} fusion(bf16[4,64,2048]{2,1,0:T(8,128)(2,1)} %collective-permute-done.5, bf16[4,64,2048]{2,1,0:T(8,128)(2,1)S(1)} %get-tuple-element.83), kind=kLoop, calls=%fused_computation.16 | loop fusion | flops 262144 | bytes 1572864 | tf_op jit(solution)/shard_map/add | solution.py:718
  52.1 2.7 %collective-permute-start.7 = (bf16[144,1024]{1,0:T(8,128)(2,1)S(1)}, bf16[144,1024]{1,0:T(8,128)(2,1)S(1)}, u32[]{:S(2)}, u32[]{:S(2)}) collective-permute-start(bf16[144,1024]{1,0:T(8,128)(2,1)S(1)} %maximum_maximum_fusion.1), channel_id=1, source_target_pairs={{0,16},{4,20},{8,24},{12,28},{16,0},{20,4},{24,8},{28,12},{1,17},{... | collective-permute-start | bytes 884744 | tf_op jit(solution)/shard_map/ppermute | solution.py:696
  54.8 8.4 %mix.3 = (bf16[1024,2048]{1,0:T(8,128)(2,1)}, bf16[1024,2048]{1,0:T(8,128)(2,1)}, bf16[1024,256]{1,0:T(8,128)(2,1)S(1)}) custom-call(s32[1]{0:T(128)} %bitcast.3.parity_ref, bf16[1024,2048]{1,0:T(8,128)(2,1)} %get-tuple-element.73.refs_0_, ...), custom_call_target="tpu_custom_call", output_to_operand_aliasing={{0}: (15, {}), {1}: (16, {}), {2}: (17, {})} | custom-call | flops 10000000000 | bytes 1 | tf_op jit(solution)/shard_map/mix/pallas_call | solution.py:390
  63.6 1.5 collective-permute-start.9
  65.1 2.3 %collective-permute-done.7 = bf16[144,1024]{1,0:T(8,128)(2,1)S(1)} collective-permute-done((bf16[144,1024]{1,0:T(8,128)(2,1)S(1)}, bf16[144,1024]{1,0:T(8,128)(2,1)S(1)}, u32[]{:S(2)}, u32[]{:S(2)}) %collective-permute-start.7) | collective-permute-done | bytes 294944 | tf_op jit(solution)/shard_map/ppermute | solution.py:696
  67.6 1.2 collective-permute-start.8
  68.9 6.1 %collective-permute-done.8.got_ref = bf16[128,1024]{1,0:T(8,128)(2,1)S(1)} collective-permute-done((bf16[128,1024]{1,0:T(8,128)(2,1)S(1)}, bf16[128,1024]{1,0:T(8,128)(2,1)S(1)}, u32[]{:S(2)}, u32[]{:S(2)}) %collective-permute-start.8) | collective-permute-done | bytes 262176 | tf_op jit(solution)/shard_map/ppermute | solution.py:696
  75.0 13.5 %norm_project.1 = (bf16[1024,2048]{1,0:T(8,128)(2,1)}, bf16[1024,512]{1,0:T(8,128)(2,1)S(1)}, bf16[1024,512]{1,0:T(8,128)(2,1)S(1)}) custom-call(s32[1]{0:T(128)} %bitcast.3.parity_ref, s32[1]{0:T(128)} %bitcast.1.place_ref.head_ref, bf16[1024,2048]{1,0:T(8,128)(2,1)} %get-tuple-element.91.part_ref, bf16[1024,2048]{1,0:T(8,128)(2,1)} %get-tuple-element.92.scale_ref, ...), custom_call_target="tpu_custom_call" | custom-call | flops 1100000 | bytes 1 | tf_op jit(solution)/shard_map/norm_project/pallas_call | solution.py:485
  88.7 2.7 %collective-permute-done.11 = bf16[1024,512]{1,0:T(8,128)(2,1)S(1)} collective-permute-done((bf16[1024,512]{1,0:T(8,128)(2,1)S(1)}, bf16[1024,512]{1,0:T(8,128)(2,1)S(1)}, u32[]{:S(2)}, u32[]{:S(2)}) %collective-permute-start.11) | collective-permute-done | bytes 1048608 | tf_op jit(solution)/shard_map/ppermute | solution.py:696
  91.6 1.6 %collective-permute-start.13 = (bf16[1024,512]{1,0:T(8,128)(2,1)S(1)}, bf16[1024,512]{1,0:T(8,128)(2,1)S(1)}, u32[]{:S(2)}, u32[]{:S(2)}) collective-permute-start(bf16[1024,512]{1,0:T(8,128)(2,1)S(1)} %add_convert_fusion.1), channel_id=1, source_target_pairs={{0,2},{1,3},{2,0},{3,1},{4,6},{5,7},{6,4},{7,5},{8,10},{9,11},{10,... | collective-permute-start | bytes 3145736 | tf_op jit(solution)/shard_map/ppermute | solution.py:696
  93.2 1.1 slice_add_fusion
  94.7 1.3 slice_add_fusion.4
  96.0 1.5 collective-permute-start.14
  97.5 2.6 %collective-permute-start.12 = (bf16[1,64,2048]{2,1,0:T(8,128)(2,1)S(1)}, bf16[1,64,2048]{2,1,0:T(8,128)(2,1)S(1)}, u32[]{:S(2)}, u32[]{:S(2)}) collective-permute-start(bf16[1,64,2048]{2,1,0:T(8,128)(2,1)S(1)} %get-tuple-element.101), channel_id=1, source_target_pairs={{0,16},{4,20},{8,24},{12,28},{16,0},{20,4},{24,8},{28,12},{1,17},{... | collective-permute-start | bytes 786440 | tf_op jit(solution)/shard_map/ppermute | solution.py:696
  100.1 13.3 %project_rest.2 = (bf16[1024,512]{1,0:T(8,128)(2,1)S(1)}, bf16[1024,512]{1,0:T(8,128)(2,1)S(1)}, bf16[1024,256]{1,0:T(8,128)(2,1)S(1)}, bf16[1024,256]{1,0:T(8,1...) custom-call(s32[1]{0:T(128)} %bitcast.1.place_ref.head_ref, ...), custom_call_target="tpu_custom_call" | custom-call | flops 100000 | bytes 1 | tf_op jit(solution)/shard_map/project_rest/pallas_call | solution.py:553
  113.7 3.2 %collective-permute-done.13.refs_8_.refs_9_ = bf16[1024,512]{1,0:T(8,128)(2,1)S(1)} collective-permute-done((bf16[1024,512]{1,0:T(8,128)(2,1)S(1)}, bf16[1024,512]{1,0:T(8,128)(2,1)S(1)}, u32[]{:S(2)}, u32[]{:S(2)}) %collective-permute-start.13) | collective-permute-done | bytes 1048608 | tf_op jit(solution)/shard_map/ppermute | solution.py:696
  116.9 2.7 %collective-permute-done.16 = bf16[1024,512]{1,0:T(8,128)(2,1)S(1)} collective-permute-done((bf16[1024,512]{1,0:T(8,128)(2,1)S(1)}, bf16[1024,512]{1,0:T(8,128)(2,1)S(1)}, u32[]{:S(2)}, u32[]{:S(2)}) %collective-permute-start.16) | collective-permute-done | bytes 1048608 | tf_op jit(solution)/shard_map/ppermute | solution.py:696
  119.9 1.6 %collective-permute-start.21 = (bf16[1024,512]{1,0:T(8,128)(2,1)S(1)}, bf16[1024,512]{1,0:T(8,128)(2,1)S(1)}, u32[]{:S(2)}, u32[]{:S(2)}) collective-permute-start(bf16[1024,512]{1,0:T(8,128)(2,1)S(1)} %add_convert_fusion), channel_id=1, source_target_pairs={{0,2},{1,3},{2,0},{3,1},{4,6},{5,7},{6,4},{7,5},{8,10},{9,11},{10,... | collective-permute-start | bytes 3145736 | tf_op jit(solution)/shard_map/ppermute | solution.py:696
  121.5 1.1 add_bitcast_fusion.1.refs_2_
  122.5 1.0 slice_add_fusion.3
  123.6 1.3 collective-permute-start.17
  124.9 3.3 %collective-permute-start.18 = (bf16[64,2048]{1,0:T(8,128)(2,1)S(1)}, bf16[64,2048]{1,0:T(8,128)(2,1)S(1)}, u32[]{:S(2)}, u32[]{:S(2)}) collective-permute-start(bf16[64,2048]{1,0:T(8,128)(2,1)S(1)} %add_bitcast_fusion.1.refs_2_), channel_id=1, source_target_pairs={{0,4},{4,8},{8,12},{12,16},{16,20},{20,24},{24,28},{1,5},{5,9},{9,... | collective-permute-start | bytes 786440 | tf_op jit(solution)/shard_map/ppermute | solution.py:692
  128.2 1.1 add_bitcast_fusion.refs_1_
  129.3 6.7 %project_rest.3.refs_0_.refs_1_.refs_2_.refs_3_ = bf16[1024,1024]{1,0:T(8,128)(2,1)S(1)} custom-call(s32[1]{0:T(128)} %bitcast.1.place_ref.head_ref, bf16[1024,2048]{1,0:T(8,128)(2,1)S(1)} %copy-done, bf16[2048,4096]{1,0:T(8,128)(2,1)} %w_ref.5), custom_call_target="tpu_custom_call" | custom-call | flops 100000 | bytes 1 | tf_op jit(solution)/shard_map/project_rest/pallas_call | solution.py:553
  136.0 2.0 %collective-permute-done.17 = bf16[1,128,1024]{2,1,0:T(8,128)(2,1)S(1)} collective-permute-done((bf16[1,128,1024]{2,1,0:T(8,128)(2,1)S(1)}, bf16[1,128,1024]{2,1,0:T(8,128)(2,1)S(1)}, u32[]{:S(2)}, u32[]{:S(2)}) %collective-permute-start.17) | collective-permute-done | bytes 262176 | tf_op jit(solution)/shard_map/ppermute | solution.py:696
  137.9 1.0 add_add_fusion
  139.0 3.4 %collective-permute-start.19 = (bf16[64,1024]{1,0:T(8,128)(2,1)S(1)}, bf16[64,1024]{1,0:T(8,128)(2,1)S(1)}, u32[]{:S(2)}, u32[]{:S(2)}) collective-permute-start(bf16[64,1024]{1,0:T(8,128)(2,1)S(1)} %get-tuple-element.140.refs_2_), channel_id=1, source_target_pairs={{0,4},{4,8},{8,12},{12,16},{16,20},{20,24},{24,28},{1,5},{5,9},{9,... | collective-permute-start | bytes 393224 | tf_op jit(solution)/shard_map/ppermute | solution.py:692
  142.4 2.7 %low_part.1 = f32[512,128]{1,0:T(8,128)S(1)} custom-call(s32[16]{0:T(128)S(1)} %copy-done.4, s32[1]{0:T(128)} %bitcast.me_ref, bf16[1024,2048]{1,0:T(8,128)(2,1)S(1)} %copy-done, bf16[64,2048]{1,0:T(8,128)(2,1)S(1)} %collective-permute-done.18.refs_0_, bf16[64,2048]{1,0:T(8,128)(2,1)S(1)} %add_bitcast_fusion.refs_1_, ...), custom_call_target="tpu_custom_call" | custom-call | flops 400000 | bytes 1 | tf_op jit(solution)/shard_map/low_part/pallas_call | solution.py:605
  146.3 0.5 collective-permute-done.20
  147.0 0.6 collective-permute-start.22
  147.6 0.7 collective-permute-done.25.refs_6_
  148.3 0.7 collective-permute-done.24.refs_5_
  149.0 0.7 collective-permute-done.23.refs_4_
  149.8 1.0 held_sum.1.held_ref
  150.8 2.0 %collective-permute-done.22 = bf16[512,128]{1,0:T(8,128)(2,1)S(1)} collective-permute-done((bf16[512,128]{1,0:T(8,128)(2,1)S(1)}, bf16[512,128]{1,0:T(8,128)(2,1)S(1)}, u32[]{:S(2)}, u32[]{:S(2)}) %collective-permute-start.22) | collective-permute-done | bytes 131104 | tf_op jit(solution)/shard_map/ppermute | solution.py:696
  152.8 3.2 %final_sum.1 = bf16[1024,1024]{1,0:T(8,128)(2,1)} custom-call(s32[16]{0:T(128)S(1)} %copy-done.4, s32[1]{0:T(128)} %bitcast.me_ref, f32[512,128]{1,0:T(8,128)S(1)} %convert_add_fusion.1.low_ref, f32[1024,1024]{1,0:T(8,128)S(1)} %held_sum.1.held_ref, bf16[64,1024]{1,0:T(8,128)(2,1)S(1)} %collective-permute-done.19.refs_0_, ...), custom_call_target="tpu_custom_call" | custom-call | flops 300000 | bytes 1 | tf_op jit(solution)/shard_map/final_sum/pallas_call | solution.py:672
  (78 shorter events, 4.9 us)
Async XLA Ops:
  0.0 16.3 %copy-start.13 = (bf16[64,2048]{1,0:T(8,128)(2,1)S(1)}, bf16[64,2048]{1,0:T(8,128)(2,1)}, u32[]{:S(2)}) copy-start(bf16[64,2048]{1,0:T(8,128)(2,1)} %constant.33.clone.spread_ref.refs_13_) | copy-start | bytes 786436
  0.0 16.3 %copy-start.2 = (bf16[1024,256]{1,0:T(8,128)(2,1)S(1)}, bf16[1024,256]{1,0:T(8,128)(2,1)}, u32[]{:S(2)}) copy-start(bf16[1024,256]{1,0:T(8,128)(2,1)} %b_ref.3) | copy-start | bytes 1572868
  0.0 5.3 %copy-start.1 = (bf16[6,64,1024]{2,1,0:T(8,128)(2,1)S(1)}, bf16[6,64,1024]{2,1,0:T(8,128)(2,1)}, u32[]{:S(2)}) copy-start(bf16[6,64,1024]{2,1,0:T(8,128)(2,1)} %refs_2_.3) | copy-start | bytes 2359300
  0.0 5.3 %copy-start.6 = (s32[16]{0:T(128)S(1)}, s32[16]{0:T(128)}, u32[]{:S(2)}) copy-start(s32[16]{0:T(128)} %tenant_ref.1) | copy-start | bytes 196
  0.0 5.3 %copy-start.5 = (s32[48]{0:T(128)S(1)}, s32[48]{0:T(128)}, u32[]{:S(2)}) copy-start(s32[48]{0:T(128)} %index_ref.1) | copy-start | bytes 580
  0.0 16.3 %copy-start.11 = (f32[32]{0:T(128)S(1)}, f32[32]{0:T(128)}, u32[]{:S(2)}) copy-start(f32[32]{0:T(128)} %param.23) | copy-start | bytes 388
  0.0 16.3 %copy-start.7 = (f32[32,1024]{1,0:T(8,128)S(1)}, f32[32,1024]{1,0:T(8,128)}, u32[]{:S(2)}) copy-start(f32[32,1024]{1,0:T(8,128)} %raw_ref.1) | copy-start | bytes 393220
  0.0 16.3 %copy-start.8 = (bf16[4,2048]{1,0:T(4,128)(2,1)S(1)}, bf16[4,2048]{1,0:T(4,128)(2,1)}, u32[]{:S(2)}) copy-start(bf16[4,2048]{1,0:T(4,128)(2,1)} %xt_ref.1) | copy-start | bytes 49156
  0.0 16.3 %copy-start.9 = (bf16[4,256]{1,0:T(4,128)(2,1)S(1)}, bf16[4,256]{1,0:T(4,128)(2,1)}, u32[]{:S(2)}) copy-start(bf16[4,256]{1,0:T(4,128)(2,1)} %bt_ref.1) | copy-start | bytes 6148
  1.7 14.7 %collective-permute-start.1 = (bf16[16,2560]{1,0:T(8,128)(2,1)}, bf16[16,2560]{1,0:T(8,128)(2,1)S(1)}, u32[]{:S(2)}, u32[]{:S(2)}) collective-permute-start(bf16[16,2560]{1,0:T(8,128)(2,1)} %sequence_edge.1), channel_id=1, source_target_pairs={{0,4},{4,0},{8,12},{12,8},{16,20},{20,16},{24,28},{28,24},{1,5},{5... | collective-permute-start | bytes 245768 | tf_op jit(solution)/shard_map/ppermute | solution.py:705
  4.6 11.7 %collective-permute-start.2 = (bf16[16,2560]{1,0:T(8,128)(2,1)}, bf16[16,2560]{1,0:T(8,128)(2,1)S(1)}, u32[]{:S(2)}, u32[]{:S(2)}) collective-permute-start(bf16[16,2560]{1,0:T(8,128)(2,1)} %sequence_edge.1), channel_id=1, source_target_pairs={{4,8},{8,4},{12,16},{16,12},{20,24},{24,20},{5,9},{9,5},{13,17},{1... | collective-permute-start | bytes 245768 | tf_op jit(solution)/shard_map/ppermute | solution.py:706
  10.3 37.1 %collective-permute-start = (bf16[4,64,2048]{2,1,0:T(8,128)(2,1)}, bf16[4,64,2048]{2,1,0:T(8,128)(2,1)}, u32[]{:S(2)}, u32[]{:S(2)}) collective-permute-start(bf16[4,64,2048]{2,1,0:T(8,128)(2,1)} %get-tuple-element.68), channel_id=1, source_target_pairs={{0,4},{4,0},{8,12},{12,8},{16,20},{20,16},{24,28},{28,24},{1,5},{5... | collective-permute-start | bytes 3145736 | tf_op jit(solution)/shard_map/ppermute | solution.py:696
  14.7 32.8 %collective-permute-start.5 = (bf16[4,64,2048]{2,1,0:T(8,128)(2,1)}, bf16[4,64,2048]{2,1,0:T(8,128)(2,1)}, u32[]{:S(2)}, u32[]{:S(2)}) collective-permute-start(bf16[4,64,2048]{2,1,0:T(8,128)(2,1)} %get-tuple-element.69), channel_id=1, source_target_pairs={{0,8},{4,12},{8,0},{12,4},{16,24},{20,28},{24,16},{28,20},{1,9},{5... | collective-permute-start | bytes 3145736 | tf_op jit(solution)/shard_map/ppermute | solution.py:696
  16.4 14.8 %copy-start.3 = (bf16[1024,256]{1,0:T(8,128)(2,1)S(1)}, bf16[1024,256]{1,0:T(8,128)(2,1)}, u32[]{:S(2)}) copy-start(bf16[1024,256]{1,0:T(8,128)(2,1)} %refs_3_.3) | copy-start | bytes 1572868
  16.4 14.8 %copy-start.10 = (bf16[4,256]{1,0:T(4,128)(2,1)S(1)}, bf16[4,256]{1,0:T(4,128)(2,1)}, u32[]{:S(2)}) copy-start(bf16[4,256]{1,0:T(4,128)(2,1)} %refs_12_.3) | copy-start | bytes 6148
  16.4 14.8 %copy-start.12 = (f32[32]{0:T(128)S(1)}, f32[32]{0:T(128)}, u32[]{:S(2)}) copy-start(f32[32]{0:T(128)} %param.24) | copy-start | bytes 388
  31.1 12.7 %collective-permute-start.3 = (bf16[144,1024]{1,0:T(8,128)(2,1)S(1)}, bf16[144,1024]{1,0:T(8,128)(2,1)S(1)}, u32[]{:S(2)}, u32[]{:S(2)}) collective-permute-start(bf16[144,1024]{1,0:T(8,128)(2,1)S(1)} %get-tuple-element.71), channel_id=1, source_target_pairs={{0,4},{4,0},{8,12},{12,8},{16,20},{20,16},{24,28},{28,24},{1,5},{5... | collective-permute-start | bytes 884744 | tf_op jit(solution)/shard_map/ppermute | solution.py:696
  31.2 16.2 %copy-start.15 = (bf16[4,64,2048]{2,1,0:T(8,128)(2,1)S(1)}, bf16[4,64,2048]{2,1,0:T(8,128)(2,1)}, u32[]{:S(2)}) copy-start(bf16[4,64,2048]{2,1,0:T(8,128)(2,1)} %get-tuple-element.67) | copy-start | bytes 3145732
  44.1 7.6 %collective-permute-start.4 = (bf16[144,1024]{1,0:T(8,128)(2,1)S(1)}, bf16[144,1024]{1,0:T(8,128)(2,1)S(1)}, u32[]{:S(2)}, u32[]{:S(2)}) collective-permute-start(bf16[144,1024]{1,0:T(8,128)(2,1)S(1)} %maximum_maximum_fusion), channel_id=1, source_target_pairs={{0,8},{4,12},{8,0},{12,4},{16,24},{20,28},{24,16},{28,20},{1,9},{5... | collective-permute-start | bytes 884744 | tf_op jit(solution)/shard_map/ppermute | solution.py:696
  45.7 42.7 %collective-permute-start.10 = (bf16[4,128,1024]{2,1,0:T(8,128)(2,1)}, bf16[4,128,1024]{2,1,0:T(8,128)(2,1)}, u32[]{:S(2)}, u32[]{:S(2)}) collective-permute-start(bf16[4,128,1024]{2,1,0:T(8,128)(2,1)} %get-tuple-element.98), channel_id=1, source_target_pairs={{0,4},{4,0},{8,12},{12,8},{16,20},{20,16},{24,28},{28,24},{1,5},{5... | collective-permute-start | bytes 3145736 | tf_op jit(solution)/shard_map/ppermute | solution.py:696
  52.1 15.3 %collective-permute-start.7 = (bf16[144,1024]{1,0:T(8,128)(2,1)S(1)}, bf16[144,1024]{1,0:T(8,128)(2,1)S(1)}, u32[]{:S(2)}, u32[]{:S(2)}) collective-permute-start(bf16[144,1024]{1,0:T(8,128)(2,1)S(1)} %maximum_maximum_fusion.1), channel_id=1, source_target_pairs={{0,16},{4,20},{8,24},{12,28},{16,0},{20,4},{24,8},{28,12},{1,17},{... | collective-permute-start | bytes 884744 | tf_op jit(solution)/shard_map/ppermute | solution.py:696
  54.7 14.1 %copy-start.17 = (bf16[2048]{0:T(1024)(128)(2,1)S(1)}, bf16[2048]{0:T(1024)(128)(2,1)}, u32[]{:S(2)}) copy-start(bf16[2048]{0:T(1024)(128)(2,1)} %param.28) | copy-start | bytes 12292
  63.2 25.3 %collective-permute-start.6 = (bf16[2,64,2048]{2,1,0:T(8,128)(2,1)}, bf16[2,64,2048]{2,1,0:T(8,128)(2,1)}, u32[]{:S(2)}, u32[]{:S(2)}) collective-permute-start(bf16[2,64,2048]{2,1,0:T(8,128)(2,1)} %slice_add_fusion.2), channel_id=1, source_target_pairs={{0,8},{4,12},{8,0},{12,4},{16,24},{20,28},{24,16},{28,20},{1,9},{5... | collective-permute-start | bytes 1572872 | tf_op jit(solution)/shard_map/ppermute | solution.py:696
  63.6 25.1 %collective-permute-start.9 = (bf16[2,64,2048]{2,1,0:T(8,128)(2,1)}, bf16[2,64,2048]{2,1,0:T(8,128)(2,1)}, u32[]{:S(2)}, u32[]{:S(2)}) collective-permute-start(bf16[2,64,2048]{2,1,0:T(8,128)(2,1)} %slice_add_fusion.1), channel_id=1, source_target_pairs={{0,16},{4,20},{8,24},{12,28},{16,0},{20,4},{24,8},{28,12},{1,17},{... | collective-permute-start | bytes 1572872 | tf_op jit(solution)/shard_map/ppermute | solution.py:696
  67.6 7.3 %collective-permute-start.8 = (bf16[128,1024]{1,0:T(8,128)(2,1)S(1)}, bf16[128,1024]{1,0:T(8,128)(2,1)S(1)}, u32[]{:S(2)}, u32[]{:S(2)}) collective-permute-start(bf16[128,1024]{1,0:T(8,128)(2,1)S(1)} %get-tuple-element.137), channel_id=1, source_target_pairs={{0,4},{4,0},{8,12},{12,8},{16,20},{20,16},{24,28},{28,24},{1,5},{5... | collective-permute-start | bytes 786440 | tf_op jit(solution)/shard_map/ppermute | solution.py:696
  75.0 18.2 %copy-start.14 = (bf16[4,128,1024]{2,1,0:T(8,128)(2,1)S(1)}, bf16[4,128,1024]{2,1,0:T(8,128)(2,1)}, u32[]{:S(2)}) copy-start(bf16[4,128,1024]{2,1,0:T(8,128)(2,1)} %get-tuple-element.108) | copy-start | bytes 3145732
  88.4 6.2 %copy-start.16 = (bf16[4,64,2048]{2,1,0:T(8,128)(2,1)S(1)}, bf16[4,64,2048]{2,1,0:T(8,128)(2,1)}, u32[]{:S(2)}) copy-start(bf16[4,64,2048]{2,1,0:T(8,128)(2,1)} %get-tuple-element.67) | copy-start | bytes 3145732
  88.7 2.7 %collective-permute-start.11 = (bf16[1024,512]{1,0:T(8,128)(2,1)S(1)}, bf16[1024,512]{1,0:T(8,128)(2,1)S(1)}, u32[]{:S(2)}, u32[]{:S(2)}) collective-permute-start(bf16[1024,512]{1,0:T(8,128)(2,1)S(1)} %get-tuple-element.99), channel_id=1, source_target_pairs={{0,1},{1,0},{2,3},{3,2},{4,5},{5,4},{6,7},{7,6},{8,9},{9,8},{10,11... | collective-permute-start | bytes 3145736 | tf_op jit(solution)/shard_map/ppermute | solution.py:696
  91.6 25.3 %collective-permute-start.13 = (bf16[1024,512]{1,0:T(8,128)(2,1)S(1)}, bf16[1024,512]{1,0:T(8,128)(2,1)S(1)}, u32[]{:S(2)}, u32[]{:S(2)}) collective-permute-start(bf16[1024,512]{1,0:T(8,128)(2,1)S(1)} %add_convert_fusion.1), channel_id=1, source_target_pairs={{0,2},{1,3},{2,0},{3,1},{4,6},{5,7},{6,4},{7,5},{8,10},{9,11},{10,... | collective-permute-start | bytes 3145736 | tf_op jit(solution)/shard_map/ppermute | solution.py:696
  94.3 19.4 %collective-permute-start.15 = (bf16[2,128,1024]{2,1,0:T(8,128)(2,1)S(1)}, bf16[2,128,1024]{2,1,0:T(8,128)(2,1)S(1)}, u32[]{:S(2)}, u32[]{:S(2)}) collective-permute-start(bf16[2,128,1024]{2,1,0:T(8,128)(2,1)S(1)} %slice_add_fusion), channel_id=1, source_target_pairs={{0,8},{4,12},{8,0},{12,4},{16,24},{20,28},{24,16},{28,20},{1,9},{5... | collective-permute-start | bytes 1572872 | tf_op jit(solution)/shard_map/ppermute | solution.py:696
  96.0 17.5 %collective-permute-start.14 = (bf16[1,64,2048]{2,1,0:T(8,128)(2,1)S(1)}, bf16[1,64,2048]{2,1,0:T(8,128)(2,1)S(1)}, u32[]{:S(2)}, u32[]{:S(2)}) collective-permute-start(bf16[1,64,2048]{2,1,0:T(8,128)(2,1)S(1)} %get-tuple-element.107), channel_id=1, source_target_pairs={{0,4},{4,0},{8,12},{12,8},{16,20},{20,16},{24,28},{28,24},{1,5},{5... | collective-permute-start | bytes 786440 | tf_op jit(solution)/shard_map/ppermute | solution.py:696
  97.5 16.0 %collective-permute-start.12 = (bf16[1,64,2048]{2,1,0:T(8,128)(2,1)S(1)}, bf16[1,64,2048]{2,1,0:T(8,128)(2,1)S(1)}, u32[]{:S(2)}, u32[]{:S(2)}) collective-permute-start(bf16[1,64,2048]{2,1,0:T(8,128)(2,1)S(1)} %get-tuple-element.101), channel_id=1, source_target_pairs={{0,16},{4,20},{8,24},{12,28},{16,0},{20,4},{24,8},{28,12},{1,17},{... | collective-permute-start | bytes 786440 | tf_op jit(solution)/shard_map/ppermute | solution.py:696
  113.4 15.9 %copy-start = (bf16[1024,2048]{1,0:T(8,128)(2,1)S(1)}, bf16[1024,2048]{1,0:T(8,128)(2,1)}, u32[]{:S(2)}) copy-start(bf16[1024,2048]{1,0:T(8,128)(2,1)} %get-tuple-element.103.y_ref) | copy-start | bytes 12582916
  116.9 2.7 %collective-permute-start.16 = (bf16[1024,512]{1,0:T(8,128)(2,1)S(1)}, bf16[1024,512]{1,0:T(8,128)(2,1)S(1)}, u32[]{:S(2)}, u32[]{:S(2)}) collective-permute-start(bf16[1024,512]{1,0:T(8,128)(2,1)S(1)} %get-tuple-element.111), channel_id=1, source_target_pairs={{0,1},{1,0},{2,3},{3,2},{4,5},{5,4},{6,7},{7,6},{8,9},{9,8},{10,11... | collective-permute-start | bytes 3145736 | tf_op jit(solution)/shard_map/ppermute | solution.py:696
  119.9 27.1 %collective-permute-start.21 = (bf16[1024,512]{1,0:T(8,128)(2,1)S(1)}, bf16[1024,512]{1,0:T(8,128)(2,1)S(1)}, u32[]{:S(2)}, u32[]{:S(2)}) collective-permute-start(bf16[1024,512]{1,0:T(8,128)(2,1)S(1)} %add_convert_fusion), channel_id=1, source_target_pairs={{0,2},{1,3},{2,0},{3,1},{4,6},{5,7},{6,4},{7,5},{8,10},{9,11},{10,... | collective-permute-start | bytes 3145736 | tf_op jit(solution)/shard_map/ppermute | solution.py:696
  123.6 14.4 %collective-permute-start.17 = (bf16[1,128,1024]{2,1,0:T(8,128)(2,1)S(1)}, bf16[1,128,1024]{2,1,0:T(8,128)(2,1)S(1)}, u32[]{:S(2)}, u32[]{:S(2)}) collective-permute-start(bf16[1,128,1024]{2,1,0:T(8,128)(2,1)S(1)} %slice_add_fusion.3), channel_id=1, source_target_pairs={{0,16},{4,20},{8,24},{12,28},{16,0},{20,4},{24,8},{28,12},{1,17},{... | collective-permute-start | bytes 786440 | tf_op jit(solution)/shard_map/ppermute | solution.py:696
  124.9 17.5 %collective-permute-start.18 = (bf16[64,2048]{1,0:T(8,128)(2,1)S(1)}, bf16[64,2048]{1,0:T(8,128)(2,1)S(1)}, u32[]{:S(2)}, u32[]{:S(2)}) collective-permute-start(bf16[64,2048]{1,0:T(8,128)(2,1)S(1)} %add_bitcast_fusion.1.refs_2_), channel_id=1, source_target_pairs={{0,4},{4,8},{8,12},{12,16},{16,20},{20,24},{24,28},{1,5},{5,9},{9,... | collective-permute-start | bytes 786440 | tf_op jit(solution)/shard_map/ppermute | solution.py:692
  129.3 13.1 %copy-start.4 = (s32[16]{0:T(128)S(1)}, s32[16]{0:T(128)}, u32[]{:S(2)}) copy-start(s32[16]{0:T(128)} %start_ref.2) | copy-start | bytes 196
  139.0 6.3 %collective-permute-start.19 = (bf16[64,1024]{1,0:T(8,128)(2,1)S(1)}, bf16[64,1024]{1,0:T(8,128)(2,1)S(1)}, u32[]{:S(2)}, u32[]{:S(2)}) collective-permute-start(bf16[64,1024]{1,0:T(8,128)(2,1)S(1)} %get-tuple-element.140.refs_2_), channel_id=1, source_target_pairs={{0,4},{4,8},{8,12},{12,16},{16,20},{20,24},{24,28},{1,5},{5,9},{9,... | collective-permute-start | bytes 393224 | tf_op jit(solution)/shard_map/ppermute | solution.py:692
  145.2 1.5 collective-permute-start.20
  145.2 2.3 %collective-permute-start.26 = (bf16[1024,256]{1,0:T(8,128)(2,1)S(1)}, bf16[1024,256]{1,0:T(8,128)(2,1)S(1)}, u32[]{:S(2)}, u32[]{:S(2)}) collective-permute-start(bf16[1024,256]{1,0:T(8,128)(2,1)S(1)} %get-tuple-element.128), channel_id=1, source_target_pairs={{0,1},{1,0},{2,3},{3,2},{4,5},{5,4},{6,7},{7,6},{8,9},{9,8},{10,11... | collective-permute-start | bytes 1572872 | tf_op jit(solution)/shard_map/ppermute | solution.py:696
  145.8 2.5 %collective-permute-start.25 = (bf16[1024,256]{1,0:T(8,128)(2,1)S(1)}, bf16[1024,256]{1,0:T(8,128)(2,1)S(1)}, u32[]{:S(2)}, u32[]{:S(2)}) collective-permute-start(bf16[1024,256]{1,0:T(8,128)(2,1)S(1)} %get-tuple-element.126), channel_id=1, source_target_pairs={{0,1},{1,0},{2,3},{3,2},{4,5},{5,4},{6,7},{7,6},{8,9},{9,8},{10,11... | collective-permute-start | bytes 1572872 | tf_op jit(solution)/shard_map/ppermute | solution.py:696
  145.8 3.3 %collective-permute-start.24 = (bf16[1024,256]{1,0:T(8,128)(2,1)S(1)}, bf16[1024,256]{1,0:T(8,128)(2,1)S(1)}, u32[]{:S(2)}, u32[]{:S(2)}) collective-permute-start(bf16[1024,256]{1,0:T(8,128)(2,1)S(1)} %get-tuple-element.124), channel_id=1, source_target_pairs={{0,1},{1,0},{2,3},{3,2},{4,5},{5,4},{6,7},{7,6},{8,9},{9,8},{10,11... | collective-permute-start | bytes 1572872 | tf_op jit(solution)/shard_map/ppermute | solution.py:696
  146.8 3.0 %collective-permute-start.23 = (bf16[1024,256]{1,0:T(8,128)(2,1)S(1)}, bf16[1024,256]{1,0:T(8,128)(2,1)S(1)}, u32[]{:S(2)}, u32[]{:S(2)}) collective-permute-start(bf16[1024,256]{1,0:T(8,128)(2,1)S(1)} %get-tuple-element.122), channel_id=1, source_target_pairs={{0,1},{1,0},{2,3},{3,2},{4,5},{5,4},{6,7},{7,6},{8,9},{9,8},{10,11... | collective-permute-start | bytes 1572872 | tf_op jit(solution)/shard_map/ppermute | solution.py:696
  147.0 5.8 %collective-permute-start.22 = (bf16[512,128]{1,0:T(8,128)(2,1)S(1)}, bf16[512,128]{1,0:T(8,128)(2,1)S(1)}, u32[]{:S(2)}, u32[]{:S(2)}) collective-permute-start(bf16[512,128]{1,0:T(8,128)(2,1)S(1)} %get-tuple-element.120), channel_id=1, source_target_pairs={{0,2},{1,3},{2,0},{3,1},{4,6},{5,7},{6,4},{7,5},{8,10},{9,11},{10,... | collective-permute-start | bytes 393224 | tf_op jit(solution)/shard_map/ppermute | solution.py:696

commit v5 on v4

--- a/solution.py
+++ b/solution.py
@@ -16,7 +16,7 @@
 TURN_DEV = 2
 HALO = 16
 LANES = 128
-PIECES = 2
+PIECES = (5, 3)
 STATE_BLOCKS = 2
 FINAL_BLOCKS = 2
 Y_UNITS = 4
@@ -812,11 +812,11 @@
         b_conv_taps,
         spread,
     )
-    count = blocks // PIECES
+    cuts = [blocks * sum(PIECES[:piece]) // sum(PIECES) for piece in range(len(PIECES) + 1)]
 
     def mix_piece(piece, held, *earlier):
         return mix(
-            piece * count, count, after(parity_arg, *earlier), xc, bc, input_c_channels, halos, run, shifted,
+            cuts[piece], cuts[piece + 1] - cuts[piece], after(parity_arg, *earlier), xc, bc, input_c_channels, halos, run, shifted,
             before, start, input_gate_channels, head_skip_coeff[None], c_conv_taps, spread, held,
         )
 

time: 157 us -> 157 us (level)
  no operation moved by 1% of the time
where the time goes in v5:
time: 157 us; the launch traced here: 156 us
  Pallas kernels  78.4 us (50%)
  starting transfers between devices  36.1 us (23%)
  waiting for transfers between devices  29 us (18%)
  other arithmetic  11.9 us (8%)
    ppermute x23, waiting for transfers between devices, swap(): lax.ppermute(block, axis, [(i, i ^ bits) for i in range(lax.axis_size(axi...  28.7 us
    ppermute x23, starting transfers between devices, swap(): lax.ppermute(block, axis, [(i, i ^ bits) for i in range(lax.axis_size(axi...  25.9 us
    pallas_call x2, Pallas kernels, project_rest(): pl.pallas_call(functools.partial(rest_kernel, counts), grid_spec=pltpu.Pr...  20 us
    pallas_call x2, Pallas kernels, mix(): pl.pallas_call(functools.partial(mix_kernel, first, bool(aliased)), grid_...  16.8 us
    pallas_call x1, Pallas kernels, local_states(): pl.pallas_call(state_kernel, grid_spec=pltpu.PrefetchScalarGridSpec(num_s...  14.7 us
    pallas_call x1, Pallas kernels, norm_project(): pl.pallas_call(functools.partial(norm_kernel, tiles), grid_spec=pltpu.Pre...  13.5 us
    add x5, other arithmetic, merge(): sum((each[each.shape[0] - self.size:each.shape[0] - half] for each in sel...  7.17 us
    ppermute x2, starting transfers between devices, shift_up(): return lax.ppermute(block, axis, route)  6.67 us
  transfers between devices with their start and end apart: 27, of which 16 were waited for; matrix products, arithmetic and copies ran while one was open for 7% of the time, Pallas kernels for 47%

profile of v5, /device:TPU:0, one launch (start us, length us, event | category | flops | bytes accessed | tf_op | source)
XLA Modules:
  0.0 156.0 jit_solution(1671275992807092988)
XLA Ops:
  0.1 1.6 %sequence_edge.1 = bf16[16,2560]{1,0:T(8,128)(2,1)} custom-call(bf16[1024,2048]{1,0:T(8,128)(2,1)} %x_ref.3, bf16[1024,256]{1,0:T(8,128)(2,1)} %b_ref.3, bf16[1024,256]{1,0:T(8,128)(2,1)} %refs_3_.3), custom_call_target="tpu_custom_call" | custom-call | flops 100000 | bytes 1 | tf_op jit(solution)/shard_map/sequence_edge/pallas_call | solution.py:83
  1.7 3.0 %collective-permute-start.1 = (bf16[16,2560]{1,0:T(8,128)(2,1)}, bf16[16,2560]{1,0:T(8,128)(2,1)S(1)}, u32[]{:S(2)}, u32[]{:S(2)}) collective-permute-start(bf16[16,2560]{1,0:T(8,128)(2,1)} %sequence_edge.1), channel_id=1, source_target_pairs={{0,4},{4,0},{8,12},{12,8},{16,20},{20,16},{24,28},{28,24},{1,5},{5... | collective-permute-start | bytes 245768 | tf_op jit(solution)/shard_map/ppermute | solution.py:705
  4.6 0.7 collective-permute-start.2
  5.3 5.0 %pack_panels.1 = (bf16[4,64,2048]{2,1,0:T(8,128)(2,1)}, bf16[4,64,2048]{2,1,0:T(8,128)(2,1)S(1)}, bf16[4,64,2048]{2,1,0:T(8,128)(2,1)}, bf16[4,64,2048]{2,1,0:T(...) custom-call(s32[48]{0:T(128)S(1)} %copy-done.5, s32[16]{0:T(128)S(1)} %copy-done.6, ...), custom_call_target="tpu_custom_call" | custom-call | flops 500000 | bytes 1 | tf_op jit(solution)/shard_map/pack_panels/pallas_call | solution.py:151
  10.3 4.3 %collective-permute-start = (bf16[4,64,2048]{2,1,0:T(8,128)(2,1)}, bf16[4,64,2048]{2,1,0:T(8,128)(2,1)}, u32[]{:S(2)}, u32[]{:S(2)}) collective-permute-start(bf16[4,64,2048]{2,1,0:T(8,128)(2,1)} %get-tuple-element.68), channel_id=1, source_target_pairs={{0,4},{4,0},{8,12},{12,8},{16,20},{20,16},{24,28},{28,24},{1,5},{5... | collective-permute-start | bytes 3145736 | tf_op jit(solution)/shard_map/ppermute | solution.py:696
  14.7 1.6 %collective-permute-start.5 = (bf16[4,64,2048]{2,1,0:T(8,128)(2,1)}, bf16[4,64,2048]{2,1,0:T(8,128)(2,1)}, u32[]{:S(2)}, u32[]{:S(2)}) collective-permute-start(bf16[4,64,2048]{2,1,0:T(8,128)(2,1)} %get-tuple-element.69), channel_id=1, source_target_pairs={{0,8},{4,12},{8,0},{12,4},{16,24},{20,28},{24,16},{28,20},{1,9},{5... | collective-permute-start | bytes 3145736 | tf_op jit(solution)/shard_map/ppermute | solution.py:696
  16.4 14.7 %local_states.1 = (bf16[1024,2048]{1,0:T(8,128)(2,1)}, bf16[1024,256]{1,0:T(8,128)(2,1)S(1)}, f32[32,1024]{1,0:T(8,128)S(1)}, f32[32,1024]{1,0:T(8,128)S(1)}, bf...) custom-call(s32[1]{0:T(128)} %bitcast.3.parity_ref, ...), custom_call_target="tpu_custom_call" | custom-call | flops 15000000512 | bytes 1 | tf_op jit(solution)/shard_map/local_states/pallas_call | solution.py:269
  31.3 10.0 %mix.2 = (bf16[1024,2048]{1,0:T(8,128)(2,1)}, bf16[1024,2048]{1,0:T(8,128)(2,1)}, bf16[1024,256]{1,0:T(8,128)(2,1)S(1)}) custom-call(s32[1]{0:T(128)} %bitcast.3.parity_ref, bf16[1024,2048]{1,0:T(8,128)(2,1)} %get-tuple-element.73.refs_0_, bf16[1024,256]{1,0:T(8,128)(2,1)S(1)} %get-tuple-element.74.refs_1_, bf16[1024,256]{1,0:T(8,128)(2,1)S(1)} %copy-done.3, ...), custom_call_target="tpu_custom_call" | custom-call | flops 12499999744 | bytes 1 | tf_op jit(solution)/shard_map/mix/pallas_call | solution.py:390
  41.2 2.6 %collective-permute-done.3 = bf16[144,1024]{1,0:T(8,128)(2,1)S(1)} collective-permute-done((bf16[144,1024]{1,0:T(8,128)(2,1)S(1)}, bf16[144,1024]{1,0:T(8,128)(2,1)S(1)}, u32[]{:S(2)}, u32[]{:S(2)}) %collective-permute-start.3) | collective-permute-done | bytes 294944 | tf_op jit(solution)/shard_map/ppermute | solution.py:696
  44.1 1.6 %collective-permute-start.4 = (bf16[144,1024]{1,0:T(8,128)(2,1)S(1)}, bf16[144,1024]{1,0:T(8,128)(2,1)S(1)}, u32[]{:S(2)}, u32[]{:S(2)}) collective-permute-start(bf16[144,1024]{1,0:T(8,128)(2,1)S(1)} %maximum_maximum_fusion), channel_id=1, source_target_pairs={{0,8},{4,12},{8,0},{12,4},{16,24},{20,28},{24,16},{28,20},{1,9},{5... | collective-permute-start | bytes 884744 | tf_op jit(solution)/shard_map/ppermute | solution.py:696
  45.7 1.7 %collective-permute-start.10 = (bf16[4,128,1024]{2,1,0:T(8,128)(2,1)}, bf16[4,128,1024]{2,1,0:T(8,128)(2,1)}, u32[]{:S(2)}, u32[]{:S(2)}) collective-permute-start(bf16[4,128,1024]{2,1,0:T(8,128)(2,1)} %get-tuple-element.98), channel_id=1, source_target_pairs={{0,4},{4,0},{8,12},{12,8},{16,20},{20,16},{24,28},{28,24},{1,5},{5... | collective-permute-start | bytes 3145736 | tf_op jit(solution)/shard_map/ppermute | solution.py:696
  47.5 1.9 %slice_add_fusion.2 = bf16[2,64,2048]{2,1,0:T(8,128)(2,1)} fusion(bf16[4,64,2048]{2,1,0:T(8,128)(2,1)} %collective-permute-done, bf16[4,64,2048]{2,1,0:T(8,128)(2,1)S(1)} %copy-done.15), kind=kLoop, calls=%fused_computation.17 | loop fusion | flops 262144 | bytes 1572864 | tf_op jit(solution)/shard_map/add | solution.py:718
  49.4 1.9 %slice_add_fusion.1 = bf16[2,64,2048]{2,1,0:T(8,128)(2,1)} fusion(bf16[4,64,2048]{2,1,0:T(8,128)(2,1)} %collective-permute-done.5, bf16[4,64,2048]{2,1,0:T(8,128)(2,1)S(1)} %get-tuple-element.83), kind=kLoop, calls=%fused_computation.16 | loop fusion | flops 262144 | bytes 1572864 | tf_op jit(solution)/shard_map/add | solution.py:718
  52.1 2.7 %collective-permute-start.7 = (bf16[144,1024]{1,0:T(8,128)(2,1)S(1)}, bf16[144,1024]{1,0:T(8,128)(2,1)S(1)}, u32[]{:S(2)}, u32[]{:S(2)}) collective-permute-start(bf16[144,1024]{1,0:T(8,128)(2,1)S(1)} %maximum_maximum_fusion.1), channel_id=1, source_target_pairs={{0,16},{4,20},{8,24},{12,28},{16,0},{20,4},{24,8},{28,12},{1,17},{... | collective-permute-start | bytes 884744 | tf_op jit(solution)/shard_map/ppermute | solution.py:696
  54.8 6.9 %mix.3 = (bf16[1024,2048]{1,0:T(8,128)(2,1)}, bf16[1024,2048]{1,0:T(8,128)(2,1)}, bf16[1024,256]{1,0:T(8,128)(2,1)S(1)}) custom-call(s32[1]{0:T(128)} %bitcast.3.parity_ref, bf16[1024,2048]{1,0:T(8,128)(2,1)} %get-tuple-element.73.refs_0_, ...), custom_call_target="tpu_custom_call", output_to_operand_aliasing={{0}: (15, {}), {1}: (16, {}), {2}: (17, {})} | custom-call | flops 7500000256 | bytes 1 | tf_op jit(solution)/shard_map/mix/pallas_call | solution.py:390
  62.0 1.5 collective-permute-start.9
  63.5 3.9 %collective-permute-done.7 = bf16[144,1024]{1,0:T(8,128)(2,1)S(1)} collective-permute-done((bf16[144,1024]{1,0:T(8,128)(2,1)S(1)}, bf16[144,1024]{1,0:T(8,128)(2,1)S(1)}, u32[]{:S(2)}, u32[]{:S(2)}) %collective-permute-start.7) | collective-permute-done | bytes 294944 | tf_op jit(solution)/shard_map/ppermute | solution.py:696
  67.6 1.2 collective-permute-start.8
  68.9 6.1 %collective-permute-done.8.got_ref = bf16[128,1024]{1,0:T(8,128)(2,1)S(1)} collective-permute-done((bf16[128,1024]{1,0:T(8,128)(2,1)S(1)}, bf16[128,1024]{1,0:T(8,128)(2,1)S(1)}, u32[]{:S(2)}, u32[]{:S(2)}) %collective-permute-start.8) | collective-permute-done | bytes 262176 | tf_op jit(solution)/shard_map/ppermute | solution.py:696
  75.0 13.5 %norm_project.1 = (bf16[1024,2048]{1,0:T(8,128)(2,1)}, bf16[1024,512]{1,0:T(8,128)(2,1)S(1)}, bf16[1024,512]{1,0:T(8,128)(2,1)S(1)}) custom-call(s32[1]{0:T(128)} %bitcast.3.parity_ref, s32[1]{0:T(128)} %bitcast.1.place_ref.head_ref, bf16[1024,2048]{1,0:T(8,128)(2,1)} %get-tuple-element.91.part_ref, bf16[1024,2048]{1,0:T(8,128)(2,1)} %get-tuple-element.92.scale_ref, ...), custom_call_target="tpu_custom_call" | custom-call | flops 1100000 | bytes 1 | tf_op jit(solution)/shard_map/norm_project/pallas_call | solution.py:485
  88.7 2.7 %collective-permute-done.11 = bf16[1024,512]{1,0:T(8,128)(2,1)S(1)} collective-permute-done((bf16[1024,512]{1,0:T(8,128)(2,1)S(1)}, bf16[1024,512]{1,0:T(8,128)(2,1)S(1)}, u32[]{:S(2)}, u32[]{:S(2)}) %collective-permute-start.11) | collective-permute-done | bytes 1048608 | tf_op jit(solution)/shard_map/ppermute | solution.py:696
  91.6 1.6 %collective-permute-start.13 = (bf16[1024,512]{1,0:T(8,128)(2,1)S(1)}, bf16[1024,512]{1,0:T(8,128)(2,1)S(1)}, u32[]{:S(2)}, u32[]{:S(2)}) collective-permute-start(bf16[1024,512]{1,0:T(8,128)(2,1)S(1)} %add_convert_fusion.1), channel_id=1, source_target_pairs={{0,2},{1,3},{2,0},{3,1},{4,6},{5,7},{6,4},{7,5},{8,10},{9,11},{10,... | collective-permute-start | bytes 3145736 | tf_op jit(solution)/shard_map/ppermute | solution.py:696
  93.2 1.1 slice_add_fusion
  94.7 1.3 slice_add_fusion.4
  96.0 1.5 collective-permute-start.14
  97.5 2.6 %collective-permute-start.12 = (bf16[1,64,2048]{2,1,0:T(8,128)(2,1)S(1)}, bf16[1,64,2048]{2,1,0:T(8,128)(2,1)S(1)}, u32[]{:S(2)}, u32[]{:S(2)}) collective-permute-start(bf16[1,64,2048]{2,1,0:T(8,128)(2,1)S(1)} %get-tuple-element.101), channel_id=1, source_target_pairs={{0,16},{4,20},{8,24},{12,28},{16,0},{20,4},{24,8},{28,12},{1,17},{... | collective-permute-start | bytes 786440 | tf_op jit(solution)/shard_map/ppermute | solution.py:696
  100.1 13.3 %project_rest.2 = (bf16[1024,512]{1,0:T(8,128)(2,1)S(1)}, bf16[1024,512]{1,0:T(8,128)(2,1)S(1)}, bf16[1024,256]{1,0:T(8,128)(2,1)S(1)}, bf16[1024,256]{1,0:T(8,1...) custom-call(s32[1]{0:T(128)} %bitcast.1.place_ref.head_ref, ...), custom_call_target="tpu_custom_call" | custom-call | flops 100000 | bytes 1 | tf_op jit(solution)/shard_map/project_rest/pallas_call | solution.py:553
  113.7 3.2 %collective-permute-done.13.refs_8_.refs_9_ = bf16[1024,512]{1,0:T(8,128)(2,1)S(1)} collective-permute-done((bf16[1024,512]{1,0:T(8,128)(2,1)S(1)}, bf16[1024,512]{1,0:T(8,128)(2,1)S(1)}, u32[]{:S(2)}, u32[]{:S(2)}) %collective-permute-start.13) | collective-permute-done | bytes 1048608 | tf_op jit(solution)/shard_map/ppermute | solution.py:696
  116.9 2.7 %collective-permute-done.16 = bf16[1024,512]{1,0:T(8,128)(2,1)S(1)} collective-permute-done((bf16[1024,512]{1,0:T(8,128)(2,1)S(1)}, bf16[1024,512]{1,0:T(8,128)(2,1)S(1)}, u32[]{:S(2)}, u32[]{:S(2)}) %collective-permute-start.16) | collective-permute-done | bytes 1048608 | tf_op jit(solution)/shard_map/ppermute | solution.py:696
  119.9 1.6 %collective-permute-start.21 = (bf16[1024,512]{1,0:T(8,128)(2,1)S(1)}, bf16[1024,512]{1,0:T(8,128)(2,1)S(1)}, u32[]{:S(2)}, u32[]{:S(2)}) collective-permute-start(bf16[1024,512]{1,0:T(8,128)(2,1)S(1)} %add_convert_fusion), channel_id=1, source_target_pairs={{0,2},{1,3},{2,0},{3,1},{4,6},{5,7},{6,4},{7,5},{8,10},{9,11},{10,... | collective-permute-start | bytes 3145736 | tf_op jit(solution)/shard_map/ppermute | solution.py:696
  121.5 1.1 add_bitcast_fusion.1.refs_2_
  122.5 1.0 slice_add_fusion.3
  123.6 1.3 collective-permute-start.17
  124.9 3.3 %collective-permute-start.18 = (bf16[64,2048]{1,0:T(8,128)(2,1)S(1)}, bf16[64,2048]{1,0:T(8,128)(2,1)S(1)}, u32[]{:S(2)}, u32[]{:S(2)}) collective-permute-start(bf16[64,2048]{1,0:T(8,128)(2,1)S(1)} %add_bitcast_fusion.1.refs_2_), channel_id=1, source_target_pairs={{0,4},{4,8},{8,12},{12,16},{16,20},{20,24},{24,28},{1,5},{5,9},{9,... | collective-permute-start | bytes 786440 | tf_op jit(solution)/shard_map/ppermute | solution.py:692
  128.2 1.1 add_bitcast_fusion.refs_1_
  129.3 6.7 %project_rest.3.refs_0_.refs_1_.refs_2_.refs_3_ = bf16[1024,1024]{1,0:T(8,128)(2,1)S(1)} custom-call(s32[1]{0:T(128)} %bitcast.1.place_ref.head_ref, bf16[1024,2048]{1,0:T(8,128)(2,1)S(1)} %copy-done, bf16[2048,4096]{1,0:T(8,128)(2,1)} %w_ref.5), custom_call_target="tpu_custom_call" | custom-call | flops 100000 | bytes 1 | tf_op jit(solution)/shard_map/project_rest/pallas_call | solution.py:553
  136.0 2.0 %collective-permute-done.17 = bf16[1,128,1024]{2,1,0:T(8,128)(2,1)S(1)} collective-permute-done((bf16[1,128,1024]{2,1,0:T(8,128)(2,1)S(1)}, bf16[1,128,1024]{2,1,0:T(8,128)(2,1)S(1)}, u32[]{:S(2)}, u32[]{:S(2)}) %collective-permute-start.17) | collective-permute-done | bytes 262176 | tf_op jit(solution)/shard_map/ppermute | solution.py:696
  137.9 1.0 add_add_fusion
  139.0 3.4 %collective-permute-start.19 = (bf16[64,1024]{1,0:T(8,128)(2,1)S(1)}, bf16[64,1024]{1,0:T(8,128)(2,1)S(1)}, u32[]{:S(2)}, u32[]{:S(2)}) collective-permute-start(bf16[64,1024]{1,0:T(8,128)(2,1)S(1)} %get-tuple-element.140.refs_2_), channel_id=1, source_target_pairs={{0,4},{4,8},{8,12},{12,16},{16,20},{20,24},{24,28},{1,5},{5,9},{9,... | collective-permute-start | bytes 393224 | tf_op jit(solution)/shard_map/ppermute | solution.py:692
  142.4 2.7 %low_part.1 = f32[512,128]{1,0:T(8,128)S(1)} custom-call(s32[16]{0:T(128)S(1)} %copy-done.4, s32[1]{0:T(128)} %bitcast.me_ref, bf16[1024,2048]{1,0:T(8,128)(2,1)S(1)} %copy-done, bf16[64,2048]{1,0:T(8,128)(2,1)S(1)} %collective-permute-done.18.refs_0_, bf16[64,2048]{1,0:T(8,128)(2,1)S(1)} %add_bitcast_fusion.refs_1_, ...), custom_call_target="tpu_custom_call" | custom-call | flops 400000 | bytes 1 | tf_op jit(solution)/shard_map/low_part/pallas_call | solution.py:605
  146.3 0.5 collective-permute-done.20
  147.0 0.6 collective-permute-start.22
  147.6 0.7 collective-permute-done.25.refs_6_
  148.3 0.7 collective-permute-done.24.refs_5_
  149.0 0.7 collective-permute-done.23.refs_4_
  149.8 1.0 held_sum.1.held_ref
  150.8 2.0 %collective-permute-done.22 = bf16[512,128]{1,0:T(8,128)(2,1)S(1)} collective-permute-done((bf16[512,128]{1,0:T(8,128)(2,1)S(1)}, bf16[512,128]{1,0:T(8,128)(2,1)S(1)}, u32[]{:S(2)}, u32[]{:S(2)}) %collective-permute-start.22) | collective-permute-done | bytes 131104 | tf_op jit(solution)/shard_map/ppermute | solution.py:696
  152.8 3.2 %final_sum.1 = bf16[1024,1024]{1,0:T(8,128)(2,1)} custom-call(s32[16]{0:T(128)S(1)} %copy-done.4, s32[1]{0:T(128)} %bitcast.me_ref, f32[512,128]{1,0:T(8,128)S(1)} %convert_add_fusion.1.low_ref, f32[1024,1024]{1,0:T(8,128)S(1)} %held_sum.1.held_ref, bf16[64,1024]{1,0:T(8,128)(2,1)S(1)} %collective-permute-done.19.refs_0_, ...), custom_call_target="tpu_custom_call" | custom-call | flops 300000 | bytes 1 | tf_op jit(solution)/shard_map/final_sum/pallas_call | solution.py:672
  (78 shorter events, 4.9 us)
Async XLA Ops:
  0.0 16.3 %copy-start.13 = (bf16[64,2048]{1,0:T(8,128)(2,1)S(1)}, bf16[64,2048]{1,0:T(8,128)(2,1)}, u32[]{:S(2)}) copy-start(bf16[64,2048]{1,0:T(8,128)(2,1)} %constant.33.clone.spread_ref.refs_13_) | copy-start | bytes 786436
  0.0 16.3 %copy-start.2 = (bf16[1024,256]{1,0:T(8,128)(2,1)S(1)}, bf16[1024,256]{1,0:T(8,128)(2,1)}, u32[]{:S(2)}) copy-start(bf16[1024,256]{1,0:T(8,128)(2,1)} %b_ref.3) | copy-start | bytes 1572868
  0.0 5.3 %copy-start.1 = (bf16[6,64,1024]{2,1,0:T(8,128)(2,1)S(1)}, bf16[6,64,1024]{2,1,0:T(8,128)(2,1)}, u32[]{:S(2)}) copy-start(bf16[6,64,1024]{2,1,0:T(8,128)(2,1)} %refs_2_.3) | copy-start | bytes 2359300
  0.0 5.3 %copy-start.6 = (s32[16]{0:T(128)S(1)}, s32[16]{0:T(128)}, u32[]{:S(2)}) copy-start(s32[16]{0:T(128)} %tenant_ref.1) | copy-start | bytes 196
  0.0 5.3 %copy-start.5 = (s32[48]{0:T(128)S(1)}, s32[48]{0:T(128)}, u32[]{:S(2)}) copy-start(s32[48]{0:T(128)} %index_ref.1) | copy-start | bytes 580
  0.0 16.3 %copy-start.11 = (f32[32]{0:T(128)S(1)}, f32[32]{0:T(128)}, u32[]{:S(2)}) copy-start(f32[32]{0:T(128)} %param.23) | copy-start | bytes 388
  0.0 16.3 %copy-start.7 = (f32[32,1024]{1,0:T(8,128)S(1)}, f32[32,1024]{1,0:T(8,128)}, u32[]{:S(2)}) copy-start(f32[32,1024]{1,0:T(8,128)} %raw_ref.1) | copy-start | bytes 393220
  0.0 16.3 %copy-start.8 = (bf16[4,2048]{1,0:T(4,128)(2,1)S(1)}, bf16[4,2048]{1,0:T(4,128)(2,1)}, u32[]{:S(2)}) copy-start(bf16[4,2048]{1,0:T(4,128)(2,1)} %xt_ref.1) | copy-start | bytes 49156
  0.0 16.3 %copy-start.9 = (bf16[4,256]{1,0:T(4,128)(2,1)S(1)}, bf16[4,256]{1,0:T(4,128)(2,1)}, u32[]{:S(2)}) copy-start(bf16[4,256]{1,0:T(4,128)(2,1)} %bt_ref.1) | copy-start | bytes 6148
  1.7 14.7 %collective-permute-start.1 = (bf16[16,2560]{1,0:T(8,128)(2,1)}, bf16[16,2560]{1,0:T(8,128)(2,1)S(1)}, u32[]{:S(2)}, u32[]{:S(2)}) collective-permute-start(bf16[16,2560]{1,0:T(8,128)(2,1)} %sequence_edge.1), channel_id=1, source_target_pairs={{0,4},{4,0},{8,12},{12,8},{16,20},{20,16},{24,28},{28,24},{1,5},{5... | collective-permute-start | bytes 245768 | tf_op jit(solution)/shard_map/ppermute | solution.py:705
  4.6 11.7 %collective-permute-start.2 = (bf16[16,2560]{1,0:T(8,128)(2,1)}, bf16[16,2560]{1,0:T(8,128)(2,1)S(1)}, u32[]{:S(2)}, u32[]{:S(2)}) collective-permute-start(bf16[16,2560]{1,0:T(8,128)(2,1)} %sequence_edge.1), channel_id=1, source_target_pairs={{4,8},{8,4},{12,16},{16,12},{20,24},{24,20},{5,9},{9,5},{13,17},{1... | collective-permute-start | bytes 245768 | tf_op jit(solution)/shard_map/ppermute | solution.py:706
  10.3 37.1 %collective-permute-start = (bf16[4,64,2048]{2,1,0:T(8,128)(2,1)}, bf16[4,64,2048]{2,1,0:T(8,128)(2,1)}, u32[]{:S(2)}, u32[]{:S(2)}) collective-permute-start(bf16[4,64,2048]{2,1,0:T(8,128)(2,1)} %get-tuple-element.68), channel_id=1, source_target_pairs={{0,4},{4,0},{8,12},{12,8},{16,20},{20,16},{24,28},{28,24},{1,5},{5... | collective-permute-start | bytes 3145736 | tf_op jit(solution)/shard_map/ppermute | solution.py:696
  14.7 32.8 %collective-permute-start.5 = (bf16[4,64,2048]{2,1,0:T(8,128)(2,1)}, bf16[4,64,2048]{2,1,0:T(8,128)(2,1)}, u32[]{:S(2)}, u32[]{:S(2)}) collective-permute-start(bf16[4,64,2048]{2,1,0:T(8,128)(2,1)} %get-tuple-element.69), channel_id=1, source_target_pairs={{0,8},{4,12},{8,0},{12,4},{16,24},{20,28},{24,16},{28,20},{1,9},{5... | collective-permute-start | bytes 3145736 | tf_op jit(solution)/shard_map/ppermute | solution.py:696
  16.4 14.8 %copy-start.3 = (bf16[1024,256]{1,0:T(8,128)(2,1)S(1)}, bf16[1024,256]{1,0:T(8,128)(2,1)}, u32[]{:S(2)}) copy-start(bf16[1024,256]{1,0:T(8,128)(2,1)} %refs_3_.3) | copy-start | bytes 1572868
  16.4 14.8 %copy-start.10 = (bf16[4,256]{1,0:T(4,128)(2,1)S(1)}, bf16[4,256]{1,0:T(4,128)(2,1)}, u32[]{:S(2)}) copy-start(bf16[4,256]{1,0:T(4,128)(2,1)} %refs_12_.3) | copy-start | bytes 6148
  16.4 14.8 %copy-start.12 = (f32[32]{0:T(128)S(1)}, f32[32]{0:T(128)}, u32[]{:S(2)}) copy-start(f32[32]{0:T(128)} %param.24) | copy-start | bytes 388
  31.1 12.7 %collective-permute-start.3 = (bf16[144,1024]{1,0:T(8,128)(2,1)S(1)}, bf16[144,1024]{1,0:T(8,128)(2,1)S(1)}, u32[]{:S(2)}, u32[]{:S(2)}) collective-permute-start(bf16[144,1024]{1,0:T(8,128)(2,1)S(1)} %get-tuple-element.71), channel_id=1, source_target_pairs={{0,4},{4,0},{8,12},{12,8},{16,20},{20,16},{24,28},{28,24},{1,5},{5... | collective-permute-start | bytes 884744 | tf_op jit(solution)/shard_map/ppermute | solution.py:696
  31.2 16.2 %copy-start.15 = (bf16[4,64,2048]{2,1,0:T(8,128)(2,1)S(1)}, bf16[4,64,2048]{2,1,0:T(8,128)(2,1)}, u32[]{:S(2)}) copy-start(bf16[4,64,2048]{2,1,0:T(8,128)(2,1)} %get-tuple-element.67) | copy-start | bytes 3145732
  44.1 7.6 %collective-permute-start.4 = (bf16[144,1024]{1,0:T(8,128)(2,1)S(1)}, bf16[144,1024]{1,0:T(8,128)(2,1)S(1)}, u32[]{:S(2)}, u32[]{:S(2)}) collective-permute-start(bf16[144,1024]{1,0:T(8,128)(2,1)S(1)} %maximum_maximum_fusion), channel_id=1, source_target_pairs={{0,8},{4,12},{8,0},{12,4},{16,24},{20,28},{24,16},{28,20},{1,9},{5... | collective-permute-start | bytes 884744 | tf_op jit(solution)/shard_map/ppermute | solution.py:696
  45.7 42.7 %collective-permute-start.10 = (bf16[4,128,1024]{2,1,0:T(8,128)(2,1)}, bf16[4,128,1024]{2,1,0:T(8,128)(2,1)}, u32[]{:S(2)}, u32[]{:S(2)}) collective-permute-start(bf16[4,128,1024]{2,1,0:T(8,128)(2,1)} %get-tuple-element.98), channel_id=1, source_target_pairs={{0,4},{4,0},{8,12},{12,8},{16,20},{20,16},{24,28},{28,24},{1,5},{5... | collective-permute-start | bytes 3145736 | tf_op jit(solution)/shard_map/ppermute | solution.py:696
  52.1 15.3 %collective-permute-start.7 = (bf16[144,1024]{1,0:T(8,128)(2,1)S(1)}, bf16[144,1024]{1,0:T(8,128)(2,1)S(1)}, u32[]{:S(2)}, u32[]{:S(2)}) collective-permute-start(bf16[144,1024]{1,0:T(8,128)(2,1)S(1)} %maximum_maximum_fusion.1), channel_id=1, source_target_pairs={{0,16},{4,20},{8,24},{12,28},{16,0},{20,4},{24,8},{28,12},{1,17},{... | collective-permute-start | bytes 884744 | tf_op jit(solution)/shard_map/ppermute | solution.py:696
  54.7 14.1 %copy-start.17 = (bf16[2048]{0:T(1024)(128)(2,1)S(1)}, bf16[2048]{0:T(1024)(128)(2,1)}, u32[]{:S(2)}) copy-start(bf16[2048]{0:T(1024)(128)(2,1)} %param.28) | copy-start | bytes 12292
  61.6 26.8 %collective-permute-start.6 = (bf16[2,64,2048]{2,1,0:T(8,128)(2,1)}, bf16[2,64,2048]{2,1,0:T(8,128)(2,1)}, u32[]{:S(2)}, u32[]{:S(2)}) collective-permute-start(bf16[2,64,2048]{2,1,0:T(8,128)(2,1)} %slice_add_fusion.2), channel_id=1, source_target_pairs={{0,8},{4,12},{8,0},{12,4},{16,24},{20,28},{24,16},{28,20},{1,9},{5... | collective-permute-start | bytes 1572872 | tf_op jit(solution)/shard_map/ppermute | solution.py:696
  62.0 26.7 %collective-permute-start.9 = (bf16[2,64,2048]{2,1,0:T(8,128)(2,1)}, bf16[2,64,2048]{2,1,0:T(8,128)(2,1)}, u32[]{:S(2)}, u32[]{:S(2)}) collective-permute-start(bf16[2,64,2048]{2,1,0:T(8,128)(2,1)} %slice_add_fusion.1), channel_id=1, source_target_pairs={{0,16},{4,20},{8,24},{12,28},{16,0},{20,4},{24,8},{28,12},{1,17},{... | collective-permute-start | bytes 1572872 | tf_op jit(solution)/shard_map/ppermute | solution.py:696
  67.6 7.3 %collective-permute-start.8 = (bf16[128,1024]{1,0:T(8,128)(2,1)S(1)}, bf16[128,1024]{1,0:T(8,128)(2,1)S(1)}, u32[]{:S(2)}, u32[]{:S(2)}) collective-permute-start(bf16[128,1024]{1,0:T(8,128)(2,1)S(1)} %get-tuple-element.137), channel_id=1, source_target_pairs={{0,4},{4,0},{8,12},{12,8},{16,20},{20,16},{24,28},{28,24},{1,5},{5... | collective-permute-start | bytes 786440 | tf_op jit(solution)/shard_map/ppermute | solution.py:696
  75.0 18.2 %copy-start.14 = (bf16[4,128,1024]{2,1,0:T(8,128)(2,1)S(1)}, bf16[4,128,1024]{2,1,0:T(8,128)(2,1)}, u32[]{:S(2)}) copy-start(bf16[4,128,1024]{2,1,0:T(8,128)(2,1)} %get-tuple-element.108) | copy-start | bytes 3145732
  88.4 6.2 %copy-start.16 = (bf16[4,64,2048]{2,1,0:T(8,128)(2,1)S(1)}, bf16[4,64,2048]{2,1,0:T(8,128)(2,1)}, u32[]{:S(2)}) copy-start(bf16[4,64,2048]{2,1,0:T(8,128)(2,1)} %get-tuple-element.67) | copy-start | bytes 3145732
  88.7 2.7 %collective-permute-start.11 = (bf16[1024,512]{1,0:T(8,128)(2,1)S(1)}, bf16[1024,512]{1,0:T(8,128)(2,1)S(1)}, u32[]{:S(2)}, u32[]{:S(2)}) collective-permute-start(bf16[1024,512]{1,0:T(8,128)(2,1)S(1)} %get-tuple-element.99), channel_id=1, source_target_pairs={{0,1},{1,0},{2,3},{3,2},{4,5},{5,4},{6,7},{7,6},{8,9},{9,8},{10,11... | collective-permute-start | bytes 3145736 | tf_op jit(solution)/shard_map/ppermute | solution.py:696
  91.6 25.3 %collective-permute-start.13 = (bf16[1024,512]{1,0:T(8,128)(2,1)S(1)}, bf16[1024,512]{1,0:T(8,128)(2,1)S(1)}, u32[]{:S(2)}, u32[]{:S(2)}) collective-permute-start(bf16[1024,512]{1,0:T(8,128)(2,1)S(1)} %add_convert_fusion.1), channel_id=1, source_target_pairs={{0,2},{1,3},{2,0},{3,1},{4,6},{5,7},{6,4},{7,5},{8,10},{9,11},{10,... | collective-permute-start | bytes 3145736 | tf_op jit(solution)/shard_map/ppermute | solution.py:696
  94.3 19.4 %collective-permute-start.15 = (bf16[2,128,1024]{2,1,0:T(8,128)(2,1)S(1)}, bf16[2,128,1024]{2,1,0:T(8,128)(2,1)S(1)}, u32[]{:S(2)}, u32[]{:S(2)}) collective-permute-start(bf16[2,128,1024]{2,1,0:T(8,128)(2,1)S(1)} %slice_add_fusion), channel_id=1, source_target_pairs={{0,8},{4,12},{8,0},{12,4},{16,24},{20,28},{24,16},{28,20},{1,9},{5... | collective-permute-start | bytes 1572872 | tf_op jit(solution)/shard_map/ppermute | solution.py:696
  96.0 17.5 %collective-permute-start.14 = (bf16[1,64,2048]{2,1,0:T(8,128)(2,1)S(1)}, bf16[1,64,2048]{2,1,0:T(8,128)(2,1)S(1)}, u32[]{:S(2)}, u32[]{:S(2)}) collective-permute-start(bf16[1,64,2048]{2,1,0:T(8,128)(2,1)S(1)} %get-tuple-element.107), channel_id=1, source_target_pairs={{0,4},{4,0},{8,12},{12,8},{16,20},{20,16},{24,28},{28,24},{1,5},{5... | collective-permute-start | bytes 786440 | tf_op jit(solution)/shard_map/ppermute | solution.py:696
  97.5 16.0 %collective-permute-start.12 = (bf16[1,64,2048]{2,1,0:T(8,128)(2,1)S(1)}, bf16[1,64,2048]{2,1,0:T(8,128)(2,1)S(1)}, u32[]{:S(2)}, u32[]{:S(2)}) collective-permute-start(bf16[1,64,2048]{2,1,0:T(8,128)(2,1)S(1)} %get-tuple-element.101), channel_id=1, source_target_pairs={{0,16},{4,20},{8,24},{12,28},{16,0},{20,4},{24,8},{28,12},{1,17},{... | collective-permute-start | bytes 786440 | tf_op jit(solution)/shard_map/ppermute | solution.py:696
  113.4 15.9 %copy-start = (bf16[1024,2048]{1,0:T(8,128)(2,1)S(1)}, bf16[1024,2048]{1,0:T(8,128)(2,1)}, u32[]{:S(2)}) copy-start(bf16[1024,2048]{1,0:T(8,128)(2,1)} %get-tuple-element.103.y_ref) | copy-start | bytes 12582916
  116.9 2.7 %collective-permute-start.16 = (bf16[1024,512]{1,0:T(8,128)(2,1)S(1)}, bf16[1024,512]{1,0:T(8,128)(2,1)S(1)}, u32[]{:S(2)}, u32[]{:S(2)}) collective-permute-start(bf16[1024,512]{1,0:T(8,128)(2,1)S(1)} %get-tuple-element.111), channel_id=1, source_target_pairs={{0,1},{1,0},{2,3},{3,2},{4,5},{5,4},{6,7},{7,6},{8,9},{9,8},{10,11... | collective-permute-start | bytes 3145736 | tf_op jit(solution)/shard_map/ppermute | solution.py:696
  119.9 27.1 %collective-permute-start.21 = (bf16[1024,512]{1,0:T(8,128)(2,1)S(1)}, bf16[1024,512]{1,0:T(8,128)(2,1)S(1)}, u32[]{:S(2)}, u32[]{:S(2)}) collective-permute-start(bf16[1024,512]{1,0:T(8,128)(2,1)S(1)} %add_convert_fusion), channel_id=1, source_target_pairs={{0,2},{1,3},{2,0},{3,1},{4,6},{5,7},{6,4},{7,5},{8,10},{9,11},{10,... | collective-permute-start | bytes 3145736 | tf_op jit(solution)/shard_map/ppermute | solution.py:696
  123.6 14.4 %collective-permute-start.17 = (bf16[1,128,1024]{2,1,0:T(8,128)(2,1)S(1)}, bf16[1,128,1024]{2,1,0:T(8,128)(2,1)S(1)}, u32[]{:S(2)}, u32[]{:S(2)}) collective-permute-start(bf16[1,128,1024]{2,1,0:T(8,128)(2,1)S(1)} %slice_add_fusion.3), channel_id=1, source_target_pairs={{0,16},{4,20},{8,24},{12,28},{16,0},{20,4},{24,8},{28,12},{1,17},{... | collective-permute-start | bytes 786440 | tf_op jit(solution)/shard_map/ppermute | solution.py:696
  124.9 17.5 %collective-permute-start.18 = (bf16[64,2048]{1,0:T(8,128)(2,1)S(1)}, bf16[64,2048]{1,0:T(8,128)(2,1)S(1)}, u32[]{:S(2)}, u32[]{:S(2)}) collective-permute-start(bf16[64,2048]{1,0:T(8,128)(2,1)S(1)} %add_bitcast_fusion.1.refs_2_), channel_id=1, source_target_pairs={{0,4},{4,8},{8,12},{12,16},{16,20},{20,24},{24,28},{1,5},{5,9},{9,... | collective-permute-start | bytes 786440 | tf_op jit(solution)/shard_map/ppermute | solution.py:692
  129.3 13.1 %copy-start.4 = (s32[16]{0:T(128)S(1)}, s32[16]{0:T(128)}, u32[]{:S(2)}) copy-start(s32[16]{0:T(128)} %start_ref.2) | copy-start | bytes 196
  139.0 6.3 %collective-permute-start.19 = (bf16[64,1024]{1,0:T(8,128)(2,1)S(1)}, bf16[64,1024]{1,0:T(8,128)(2,1)S(1)}, u32[]{:S(2)}, u32[]{:S(2)}) collective-permute-start(bf16[64,1024]{1,0:T(8,128)(2,1)S(1)} %get-tuple-element.140.refs_2_), channel_id=1, source_target_pairs={{0,4},{4,8},{8,12},{12,16},{16,20},{20,24},{24,28},{1,5},{5,9},{9,... | collective-permute-start | bytes 393224 | tf_op jit(solution)/shard_map/ppermute | solution.py:692
  145.2 1.5 collective-permute-start.20
  145.2 2.3 %collective-permute-start.26 = (bf16[1024,256]{1,0:T(8,128)(2,1)S(1)}, bf16[1024,256]{1,0:T(8,128)(2,1)S(1)}, u32[]{:S(2)}, u32[]{:S(2)}) collective-permute-start(bf16[1024,256]{1,0:T(8,128)(2,1)S(1)} %get-tuple-element.128), channel_id=1, source_target_pairs={{0,1},{1,0},{2,3},{3,2},{4,5},{5,4},{6,7},{7,6},{8,9},{9,8},{10,11... | collective-permute-start | bytes 1572872 | tf_op jit(solution)/shard_map/ppermute | solution.py:696
  145.8 2.5 %collective-permute-start.25 = (bf16[1024,256]{1,0:T(8,128)(2,1)S(1)}, bf16[1024,256]{1,0:T(8,128)(2,1)S(1)}, u32[]{:S(2)}, u32[]{:S(2)}) collective-permute-start(bf16[1024,256]{1,0:T(8,128)(2,1)S(1)} %get-tuple-element.126), channel_id=1, source_target_pairs={{0,1},{1,0},{2,3},{3,2},{4,5},{5,4},{6,7},{7,6},{8,9},{9,8},{10,11... | collective-permute-start | bytes 1572872 | tf_op jit(solution)/shard_map/ppermute | solution.py:696
  145.8 3.3 %collective-permute-start.24 = (bf16[1024,256]{1,0:T(8,128)(2,1)S(1)}, bf16[1024,256]{1,0:T(8,128)(2,1)S(1)}, u32[]{:S(2)}, u32[]{:S(2)}) collective-permute-start(bf16[1024,256]{1,0:T(8,128)(2,1)S(1)} %get-tuple-element.124), channel_id=1, source_target_pairs={{0,1},{1,0},{2,3},{3,2},{4,5},{5,4},{6,7},{7,6},{8,9},{9,8},{10,11... | collective-permute-start | bytes 1572872 | tf_op jit(solution)/shard_map/ppermute | solution.py:696
  146.8 3.0 %collective-permute-start.23 = (bf16[1024,256]{1,0:T(8,128)(2,1)S(1)}, bf16[1024,256]{1,0:T(8,128)(2,1)S(1)}, u32[]{:S(2)}, u32[]{:S(2)}) collective-permute-start(bf16[1024,256]{1,0:T(8,128)(2,1)S(1)} %get-tuple-element.122), channel_id=1, source_target_pairs={{0,1},{1,0},{2,3},{3,2},{4,5},{5,4},{6,7},{7,6},{8,9},{9,8},{10,11... | collective-permute-start | bytes 1572872 | tf_op jit(solution)/shard_map/ppermute | solution.py:696
  147.0 5.8 %collective-permute-start.22 = (bf16[512,128]{1,0:T(8,128)(2,1)S(1)}, bf16[512,128]{1,0:T(8,128)(2,1)S(1)}, u32[]{:S(2)}, u32[]{:S(2)}) collective-permute-start(bf16[512,128]{1,0:T(8,128)(2,1)S(1)} %get-tuple-element.120), channel_id=1, source_target_pairs={{0,2},{1,3},{2,0},{3,1},{4,6},{5,7},{6,4},{7,5},{8,10},{9,11},{10,... | collective-permute-start | bytes 393224 | tf_op jit(solution)/shard_map/ppermute | solution.py:696
